TPU v7x, 32 devices: a whole 2x2x4 slice. The times are simulated.
32 devices in a mesh: sect: 2 (over x), wide: 4 (over y, core), narrow: 4 (over z).
Axes of the slice: x: 2, y: 2, z: 4, core: 2. Of those that a mesh axis runs over, the one named last changes fastest.
Arguments:
- leaf_rhs: bfloat16 [512, 8192], P('wide', ('sect', 'narrow')), may hold values from -6 to 6
- leaf_factor: bfloat16 [8192, 4096], P(('sect', 'wide'), 'narrow'), may hold values from -1 to 2
- leaf_coupling: bfloat16 [4096, 4096], P(('sect', 'wide'), 'narrow'), may hold values from -0.09375 to 0.09375
- root_factor: bfloat16 [16384, 16384], P('wide', ('sect', 'narrow')), may hold values from -1 to 2
- root_rhs: bfloat16 [512, 16384], P('wide', ('sect', 'narrow')), may hold values from -6 to 6
- border_map: int32 [2, 2048], replicated, may hold values from 0 to 16383, as said below
- border_rows: int32 [2], replicated, may hold values from 512 to 2048, as said below
Outputs:
- leaf_solution: bfloat16 [512, 8192], P('wide', ('sect', 'narrow'))
- root_solution: bfloat16 [512, 16384], P('wide', ('sect', 'narrow'))
Inputs may be any that keep to these rules, and one draw needn't show every extreme that they name: `border_map`: row s lists the root indices of the 2048 border rows of leaf s, all different within a row; different leaves may share root indices. The live border rows of leaf s are its first border_rows[s] rows.
All inputs are finite; a program needn't handle non-finite values.
Results may differ from a plain program's by a relative error of at most 0.024.
Values may be sent and summed in bfloat16 or wider, within the bound.
No kernel may reach another device: no remote copies, remote signals or barrier semaphores. Data moves between devices by JAX's collectives and lax.ppermute only.
A program may use at most 64 MiB of HBM per device.

v0:
```python
import jax
import jax.numpy as jnp
from jax import lax
from jax.sharding import PartitionSpec as P


def times_transposed(left, right):
    return lax.dot_general(
        left, right, (((1,), (1,)), ((), ())), preferred_element_type=jnp.float32
    )


def body(leaf_rhs, leaf_factor, leaf_coupling, root_factor, root_rhs, border_map, border_rows):
    wide_count = lax.axis_size("wide")
    narrow_count = lax.axis_size("narrow")
    sect_count = lax.axis_size("sect")
    sect_index = lax.axis_index("sect")
    wide_index = lax.axis_index("wide")
    narrow_index = lax.axis_index("narrow")
    pivot_block = leaf_factor.shape[0]
    border_block = leaf_coupling.shape[0]
    border_part = border_block // narrow_count
    border_total = border_block * wide_count
    root_block = root_rhs.shape[1]
    leaf_rows = border_rows[sect_index]
    own_map = lax.dynamic_index_in_dim(border_map, sect_index, 0, keepdims=False)
    piece = lax.all_gather(leaf_rhs, "wide", axis=0, tiled=True)
    terms = jnp.concatenate(
        [times_transposed(piece, leaf_factor), times_transposed(piece, leaf_coupling)], axis=1
    )
    pivot_terms = terms[:, :pivot_block]
    border_terms = terms[:, pivot_block:]
    pivot_sum, border_sum = (
        lax.psum_scatter(
            pivot_terms.astype(jnp.bfloat16), "narrow", scatter_dimension=1, tiled=True
        ).astype(jnp.float32),
        lax.psum_scatter(
            border_terms.astype(jnp.bfloat16), "narrow", scatter_dimension=1, tiled=True
        ).astype(jnp.float32),
    )
    leaf_mid = pivot_sum.astype(jnp.bfloat16)
    border_place = (
        wide_index * border_block
        + narrow_index * border_part
        + lax.broadcasted_iota(jnp.int32, (1, border_part), 1)
    )
    border_out = jnp.where(border_place < leaf_rows, border_sum, 0.0).astype(jnp.bfloat16)
    regrouped = lax.all_to_all(border_out, "wide", split_axis=0, concat_axis=1, tiled=True)
    root_start = (sect_index * narrow_count + narrow_index) * root_block
    order_map = (
        border_map.reshape(sect_count, wide_count, narrow_count, border_part)
        .transpose(0, 2, 1, 3)
        .reshape(-1)
    )
    targets = order_map - root_start
    targets = jnp.where((targets >= 0) & (targets < root_block), targets, root_block)
    landed = (
        jnp.zeros((regrouped.shape[0], root_block), jnp.float32)
        .at[:, targets]
        .add(
            lax.all_gather(regrouped, ("sect", "narrow"), axis=1, tiled=True).astype(jnp.float32),
            mode="drop",
        )
    )
    root_right = (root_rhs.astype(jnp.float32) - landed).astype(jnp.bfloat16)
    root_partial = times_transposed(
        lax.all_gather(root_right, "wide", axis=0, tiled=True), root_factor
    )
    root_mid = lax.psum_scatter(
        root_partial.astype(jnp.bfloat16), ("sect", "narrow"), scatter_dimension=0, tiled=True
    )
    back_terms = jnp.dot(
        lax.all_gather(root_mid, ("sect", "narrow"), axis=0, tiled=True),
        root_factor,
        preferred_element_type=jnp.float32,
    )
    root_solution = lax.psum_scatter(
        back_terms.astype(jnp.bfloat16), "wide", scatter_dimension=0, tiled=True
    )
    piece = lax.all_gather(root_solution, ("sect", "narrow"), axis=1, tiled=True)
    inside = (own_map >= 0) & (own_map < piece.shape[1])
    chosen = jnp.take(piece, jnp.clip(own_map, 0, piece.shape[1] - 1), axis=1)
    picked = jnp.where(inside[None, :], chosen, jnp.zeros((), jnp.bfloat16))
    border_live = lax.broadcasted_iota(jnp.int32, (1, border_total), 1) < leaf_rows
    picked = jnp.where(border_live, picked, jnp.zeros((), jnp.bfloat16))
    returned = lax.all_to_all(picked, "wide", split_axis=1, concat_axis=0, tiled=True)
    coupled = -jnp.dot(returned, leaf_coupling, preferred_element_type=jnp.float32)
    back_leaf = coupled + jnp.dot(
        lax.all_gather(leaf_mid, "narrow", axis=1, tiled=True),
        leaf_factor,
        preferred_element_type=jnp.float32,
    )
    leaf_solution = lax.psum_scatter(
        back_leaf.astype(jnp.bfloat16), "wide", scatter_dimension=0, tiled=True
    )
    return (leaf_solution, root_solution)


def solution(mesh):
    in_specs = (
        P("wide", ("sect", "narrow")),
        P(("sect", "wide"), "narrow"),
        P(("sect", "wide"), "narrow"),
        P("wide", ("sect", "narrow")),
        P("wide", ("sect", "narrow")),
        P(),
        P(),
    )
    out_specs = (P("wide", ("sect", "narrow")), P("wide", ("sect", "narrow")))
    return jax.shard_map(body, mesh=mesh, in_specs=in_specs, out_specs=out_specs, check_vma=False)
```

profile of v0, /device:TPU:0, one launch (start us, length us, event | category | flops | bytes accessed | tf_op | source)
XLA Modules:
  0.0 542.1 jit_solution(13916832024716986316)
XLA Ops:
  7.2 0.0 copy-start
  7.2 0.0 all-gather.7.cloned.1.call-start
  7.2 0.7 all-gather.7.cloned.1.call-update
  7.9 0.0 copy-start.4
  7.9 0.0 reduce-scatter.16.cloned.1.call-start
  8.0 21.1 %all-gather.7.cloned.1.call-done = bf16[512,1024]{1,0:T(8,128)(2,1)} async-done(((bf16[128,1024]{1,0:T(8,128)(2,1)}), bf16[512,1024]{1,0:T(8,128)(2,1)}) %all-gather.7.cloned.1.call-update) | async-done | bytes 1048592 | tf_op jit(solution)/shard_map/all_gather | solution.py:27
  29.0 2.3 convolution_convert_fusion.3
  31.3 0.0 copy-start.2
  31.3 0.0 copy-start.1
  31.3 1.0 copy.22
  32.3 0.0 reduce-scatter.16.cloned.1.call-update
  32.4 0.0 all-gather.9.cloned.1.call-start
  32.4 0.0 copy-done.4
  32.4 0.6 dynamic_slice.7
  33.1 0.6 add_compare_fusion.1
  33.7 20.5 %reduce-scatter.16.cloned.1.call-done = bf16[128,512]{1,0:T(8,128)(2,1)} async-done(((bf16[512,512]{1,0:T(8,128)(2,1)}), bf16[128,512]{1,0:T(8,128)(2,1)}) %reduce-scatter.16.cloned.1.call-update) | async-done | bytes 131088
  54.2 1.0 copy.23
  55.2 7.2 %all_to_all.35 = bf16[4,128,128]{2,1,0:T(8,128)(2,1)S(1)} all-to-all(bf16[4,128,128]{2,1,0:T(8,128)(2,1)S(1)} %bitcast.38), channel_id=1, replica_groups=mesh['sect'=2,'wide'=4,'narrow'=4] {'wide'}, dimensions={0} | all-to-all | bytes 262144 | tf_op jit(solution)/shard_map/all_to_all | solution.py:48
  62.4 0.8 copy.19
  63.2 0.0 all-gather.9.cloned.1.call-update
  63.2 0.0 all-gather.11.cloned.1.call-start
  63.3 0.0 copy-done.2
  63.3 1.0 copy.17
  64.4 36.6 %all-gather.9.cloned.1.call-done = bf16[128,4096]{0,1:T(8,128)(2,1)} async-done(((bf16[128,512]{0,1:T(8,128)(2,1)}), bf16[128,4096]{0,1:T(8,128)(2,1)}) %all-gather.9.cloned.1.call-update) | async-done | bytes 1048592 | tf_op jit(solution)/shard_map/all_gather | solution.py:61
  101.0 23.0 %scatter_custom_fusion = f32[128,2048]{0,1:T(8,128)S(1)} fusion(s32[4096]{0:T(1024)S(1)} %bitcast.43, bf16[128,4096]{0,1:T(8,128)(2,1)} %all-gather.9.cloned.1.call-done, f32[]{:T(128)} %constant.23.clone.1), kind=kCustom, calls=%fused_computation.4 | custom fusion | flops 1048576 | bytes 2097156 | tf_op jit(solution)/shard_map/scatter-add | solution.py:60
  124.0 1.9 subtract_convert_fusion
  125.9 0.0 all-gather.11.cloned.1.call-update
  126.0 0.0 reduce-scatter.8.cloned.1.call-start
  126.0 21.7 %all-gather.11.cloned.1.call-done = bf16[512,2048]{0,1:T(8,128)(2,1)} async-done(((bf16[128,2048]{0,1:T(8,128)(2,1)}), bf16[512,2048]{0,1:T(8,128)(2,1)}) %all-gather.11.cloned.1.call-update) | async-done | bytes 2097168 | tf_op jit(solution)/shard_map/all_gather | solution.py:67
  147.7 14.5 %convolution_convert_fusion = bf16[512,4096]{1,0:T(8,128)(2,1)} fusion(bf16[512,2048]{0,1:T(8,128)(2,1)} %all-gather.11.cloned.1.call-done, bf16[4096,2048]{1,0:T(8,128)(2,1)} %param.10), kind=kOutput, calls=%fused_computation.2 | convolution fusion | flops 8592031744 | bytes 23068672 | tf_op jit(solution)/shard_map/dot_general | solution.py:8
  162.2 0.0 reduce-scatter.8.cloned.1.call-update
  162.2 0.0 all-gather.13.cloned.1.call-start
  162.2 88.2 %reduce-scatter.8.cloned.1.call-done = bf16[64,4096]{1,0:T(8,128)(2,1)} async-done(((bf16[512,4096]{1,0:T(8,128)(2,1)}), bf16[64,4096]{1,0:T(8,128)(2,1)}) %reduce-scatter.8.cloned.1.call-update) | async-done | bytes 524304 | tf_op jit(solution)/shard_map/reduce_scatter | solution.py:69
  250.4 0.0 all-gather.13.cloned.1.call-update
  250.4 0.2 reduce-scatter.10.cloned.1.call-start
  250.7 75.1 %all-gather.13.cloned.1.call-done = bf16[512,4096]{1,0:T(8,128)(2,1)} async-done(((bf16[64,4096]{1,0:T(8,128)(2,1)}), bf16[512,4096]{1,0:T(8,128)(2,1)}) %all-gather.13.cloned.1.call-update) | async-done | bytes 4194320 | tf_op jit(solution)/shard_map/all_gather | solution.py:73
  325.8 14.6 %convolution_convert_fusion.1 = bf16[512,2048]{1,0:T(8,128)(2,1)} fusion(bf16[512,4096]{1,0:T(8,128)(2,1)} %all-gather.13.cloned.1.call-done, bf16[4096,2048]{1,0:T(8,128)(2,1)} %param.10), kind=kOutput, calls=%fused_computation.3 | convolution fusion | flops 8590983168 | bytes 23068672 | tf_op jit(solution)/shard_map/dot_general | solution.py:72
  340.4 0.0 reduce-scatter.10.cloned.1.call-update
  340.4 0.0 reduce-scatter.12.cloned.1.call-start
  340.4 0.0 copy-done
  340.4 1.1 copy-done.3
  341.6 2.3 convolution_convert_fusion.2
  343.9 0.0 reduce-scatter.12.cloned.1.call-update
  343.9 0.0 all-gather.15.cloned.1.call-start
  343.9 26.3 %reduce-scatter.10.cloned.1.call-done = bf16[128,2048]{1,0:T(8,128)(2,1)} async-done(((bf16[512,2048]{1,0:T(8,128)(2,1)}), bf16[128,2048]{1,0:T(8,128)(2,1)}) %reduce-scatter.10.cloned.1.call-update) | async-done | bytes 524304 | tf_op jit(solution)/shard_map/reduce_scatter | solution.py:77
  370.2 0.0 all-gather.15.cloned.1.call-update
  370.3 0.0 all-gather.17.cloned.1.call-start
  370.3 29.4 %reduce-scatter.12.cloned.1.call-done = bf16[512,256]{1,0:T(8,128)(2,1)} async-done(((bf16[512,1024]{1,0:T(8,128)(2,1)}), bf16[512,256]{1,0:T(8,128)(2,1)}) %reduce-scatter.12.cloned.1.call-update) | async-done | bytes 262160 | tf_op jit(solution)/shard_map/reduce_scatter | solution.py:34
  399.7 0.0 all-gather.17.cloned.1.call-update
  399.8 0.1 and_reduce_fusion
  399.9 0.6 add_compare_fusion
  400.6 74.2 %all-gather.15.cloned.1.call-done = bf16[128,16384]{1,0:T(8,128)(2,1)} async-done(((bf16[128,2048]{1,0:T(8,128)(2,1)}), bf16[128,16384]{1,0:T(8,128)(2,1)}) %all-gather.15.cloned.1.call-update) | async-done | bytes 4194320 | tf_op jit(solution)/shard_map/all_gather | solution.py:80
  474.7 6.4 %copy.20 = bf16[128,16384]{0,1:T(8,128)(2,1)} copy(bf16[128,16384]{1,0:T(8,128)(2,1)} %all-gather.15.cloned.1.call-done) | data formatting | bytes 8388608 | tf_op jit(solution)/shard_map/all_gather | solution.py:80
  481.2 8.4 %gather_fusion = bf16[2048,128]{1,0:T(8,128)(2,1)S(1)} fusion(bf16[128,16384]{0,1:T(8,128)(2,1)} %copy.20, s32[2048]{0:T(1024)S(1)} %broadcast_clamp_fusion), kind=kCustom, calls=%fused_computation | custom fusion | bytes 1056768 | tf_op jit(solution)/shard_map/jit(_take)/gather | solution.py:82
  489.6 0.2 copy.21
  489.8 0.9 select_select_fusion
  490.7 3.5 all-to-all-start.1
  494.2 0.0 reduce-scatter.14.cloned.1.call-start
  494.2 10.5 %all-gather.17.cloned.1.call-done = bf16[512,1024]{1,0:T(8,128)(2,1)} async-done(((bf16[512,256]{1,0:T(8,128)(2,1)}), bf16[512,1024]{1,0:T(8,128)(2,1)}) %all-gather.17.cloned.1.call-update) | async-done | bytes 1048592 | tf_op jit(solution)/shard_map/all_gather | solution.py:89
  504.7 3.8 fusion.4
  508.5 0.0 all-to-all-done.1
  508.5 3.6 add_convert_fusion
  512.1 0.0 reduce-scatter.14.cloned.1.call-update
  512.2 23.4 %reduce-scatter.14.cloned.1.call-done = bf16[128,1024]{1,0:T(8,128)(2,1)} async-done(((bf16[512,1024]{1,0:T(8,128)(2,1)}), bf16[128,1024]{1,0:T(8,128)(2,1)}) %reduce-scatter.14.cloned.1.call-update) | async-done | bytes 262160 | tf_op jit(solution)/shard_map/reduce_scatter | solution.py:93
  (12 shorter events, 0.2 us)
Async XLA Ops:
  7.2 333.3 %copy-start = (bf16[1024,1024]{1,0:T(8,128)(2,1)S(1)}, bf16[1024,1024]{1,0:T(8,128)(2,1)}, u32[]{:S(2)}) copy-start(bf16[1024,1024]{1,0:T(8,128)(2,1)} %param.8) | copy-start | bytes 6291460
  7.2 21.9 %all-gather.7.cloned.1.call-start = ((), (), s32[]{:S(2)}) async-start(), calls=%async_computation.7 | async-start | bytes 1310720 | tf_op jit(solution)/shard_map/all_gather | solution.py:27
  7.9 24.5 %copy-start.4 = (s32[2]{0:T(128)S(1)}, s32[2]{0:T(128)}, u32[]{:S(2)}) copy-start(s32[2]{0:T(128)} %param.13) | copy-start | bytes 28
  7.9 46.3 %reduce-scatter.16.cloned.1.call-start = ((), (), s32[]{:S(2)}) async-start(), calls=%async_computation.17 | async-start | bytes 655360
  31.3 31.9 %copy-start.2 = (s32[2,2048]{1,0:T(2,128)S(1)}, s32[2,2048]{1,0:T(2,128)}, u32[]{:S(2)}) copy-start(s32[2,2048]{1,0:T(2,128)} %param.12) | copy-start | bytes 49156
  31.3 32.0 %copy-start.1 = (bf16[128,2048]{1,0:T(8,128)(2,1)S(1)}, bf16[128,2048]{1,0:T(8,128)(2,1)}, u32[]{:S(2)}) copy-start(bf16[128,2048]{1,0:T(8,128)(2,1)} %param.11) | copy-start | bytes 1572868
  32.4 68.6 %all-gather.9.cloned.1.call-start = ((), (), s32[]{:S(2)}) async-start(), calls=%async_computation.8 | async-start | bytes 1179648 | tf_op jit(solution)/shard_map/all_gather | solution.py:61
  63.2 84.5 %all-gather.11.cloned.1.call-start = ((), (), s32[]{:S(2)}) async-start(), calls=%async_computation.9 | async-start | bytes 2621440 | tf_op jit(solution)/shard_map/all_gather | solution.py:67
  126.0 124.5 %reduce-scatter.8.cloned.1.call-start = ((), (), s32[]{:S(2)}) async-start(), calls=%async_computation.10 | async-start | bytes 4718592 | tf_op jit(solution)/shard_map/reduce_scatter | solution.py:69
  162.2 163.6 %all-gather.13.cloned.1.call-start = ((), (), s32[]{:S(2)}) async-start(), calls=%async_computation.11 | async-start | bytes 4718592 | tf_op jit(solution)/shard_map/all_gather | solution.py:73
  250.4 119.8 %reduce-scatter.10.cloned.1.call-start = ((), (), s32[]{:S(2)}) async-start(), calls=%async_computation.12 | async-start | bytes 2621440 | tf_op jit(solution)/shard_map/reduce_scatter | solution.py:77
  340.4 1.2 copy-start.3
  340.4 59.3 %reduce-scatter.12.cloned.1.call-start = ((), (), s32[]{:S(2)}) async-start(), calls=%async_computation.14 | async-start | bytes 1310720 | tf_op jit(solution)/shard_map/reduce_scatter | solution.py:34
  343.9 130.9 %all-gather.15.cloned.1.call-start = ((), (), s32[]{:S(2)}) async-start(), calls=%async_computation.13 | async-start | bytes 4718592 | tf_op jit(solution)/shard_map/all_gather | solution.py:80
  370.3 134.5 %all-gather.17.cloned.1.call-start = ((), (), s32[]{:S(2)}) async-start(), calls=%async_computation.15 | async-start | bytes 1310720 | tf_op jit(solution)/shard_map/all_gather | solution.py:89
  490.7 17.8 %all-to-all-start.1 = ((bf16[128,4,512]{2,0,1:T(8,128)(2,1)}), bf16[128,4,512]{2,0,1:T(8,128)(2,1)S(1)}, u32[]{:S(2)}, u32[]{:S(2)}) async-start(bf16[128,4,512]{2,0,1:T(8,128)(2,1)} %select_select_fusion), calls=%async_computation.3 | async-start | bytes 1048576 | tf_op jit(solution)/shard_map/all_to_all | solution.py:86
  494.2 41.3 %reduce-scatter.14.cloned.1.call-start = ((), (), s32[]{:S(2)}) async-start(), calls=%async_computation.16 | async-start | bytes 1310720 | tf_op jit(solution)/shard_map/reduce_scatter | solution.py:93
Sparse Core Ops, SparseCore 0:
  9.6 19.4 all-gather.6
  32.5 21.6 reduce-scatter.15
  63.3 37.6 all-gather.8
  126.1 21.5 all-gather.10
  162.3 88.0 reduce-scatter.7
  252.6 73.1 all-gather.12
  340.5 29.6 reduce-scatter.9
  372.5 27.1 reduce-scatter.11
  402.6 72.0 all-gather.14
  476.2 28.4 all-gather.16
  512.3 23.1 reduce-scatter.13
where the time goes:
time: 543 us; the launch traced here: 542 us
  waiting for transfers between devices  428 us (79%)
  matrix products  41 us (8%)
  other arithmetic  27.3 us (5%)
  local copies, waits for them, and re-layouts  20.7 us (4%)
  between operations  14.1 us (3%)
  blocking collectives  7.17 us (1%)
    reduce_scatter x1, waiting for transfers between devices, body(): lax.psum_scatter(root_partial.astype(jnp.bfloat16), ('sect', 'narrow'), s...  88.2 us
    all_gather x1, waiting for transfers between devices, body(): lax.all_gather(root_mid, ('sect', 'narrow'), axis=0, tiled=True)  75.1 us
    all_gather x1, waiting for transfers between devices, body(): lax.all_gather(root_solution, ('sect', 'narrow'), axis=1, tiled=True)  74.2 us
    all_gather x1, waiting for transfers between devices, body(): lax.all_gather(regrouped, ('sect', 'narrow'), axis=1, tiled=True)  36.6 us
    reduce_scatter x1, waiting for transfers between devices, body(): lax.psum_scatter(pivot_terms.astype(jnp.bfloat16), 'narrow', scatter_dime...  29.4 us
    reduce_scatter x1, waiting for transfers between devices, body(): lax.psum_scatter(back_terms.astype(jnp.bfloat16), 'wide', scatter_dimensi...  26.3 us
    reduce_scatter x1, waiting for transfers between devices, body(): lax.psum_scatter(back_leaf.astype(jnp.bfloat16), 'wide', scatter_dimensio...  23.4 us
    scatter-add x1, other arithmetic, body(): landed = jnp.zeros((regrouped.shape[0], root_block), jnp.float32).at[:, t...  23 us
  transfers between devices with their start and end apart: 12, of which 11 were waited for; matrix products, arithmetic and copies ran while one was open for 5% of the time, Pallas kernels for 0%

commit v1 on v0

v1 whole, which is shorter than its diff:
```python
import jax
import jax.numpy as jnp
from jax import lax
from jax.sharding import PartitionSpec as P

CHUNKS = 4


def times_transposed(left, right):
    return lax.dot_general(
        left, right, (((1,), (1,)), ((), ())), preferred_element_type=jnp.float32
    )


def times(left, right):
    return jnp.dot(left, right, preferred_element_type=jnp.float32)


def tie(values, others):
    return lax.optimization_barrier(tuple(values) + tuple(others))[: len(values)]


def swap(value, axis, distance):
    pairs = [(i, i ^ distance) for i in range(lax.axis_size(axis))]
    return lax.ppermute(value, axis, pairs)


def total(values):
    result = values[0].astype(jnp.float32)
    for value in values[1:]:
        result = result + value.astype(jnp.float32)
    return result.astype(jnp.bfloat16)


def relative_gather(value, axis):
    distance = lax.axis_size(axis) // 2
    while distance >= 1:
        value = jnp.concatenate([value, swap(value, axis, distance)], axis=0)
        distance //= 2
    return value


def relative_scatter(value, axis):
    distance = 1
    while distance < lax.axis_size(axis):
        half = value.shape[0] // 2
        value = total([value[:half], swap(value[half:].astype(jnp.bfloat16), axis, distance)])
        distance *= 2
    return value


def relative_places(axis):
    places = [0]
    distance = lax.axis_size(axis) // 2
    while distance >= 1:
        places = places + [place ^ distance for place in places]
        distance //= 2
    return places


def direct_scatter(value, axis, dim=0):
    count = lax.axis_size(axis)
    here = lax.axis_index(axis)
    block = value.shape[dim] // count
    shape = value.shape[:dim] + (count, block) + value.shape[dim + 1 :]
    blocks = value.reshape(shape)
    parts = [lax.dynamic_index_in_dim(blocks, here ^ k, dim, keepdims=False) for k in range(count)]
    return total([parts[0]] + [swap(parts[k], axis, k) for k in range(1, count)])


def direct_gather(value, axis, dim=0):
    count = lax.axis_size(axis)
    here = lax.axis_index(axis)
    shape = value.shape[:dim] + (count,) + value.shape[dim:]
    result = jnp.zeros(shape, value.dtype)
    for k in range(count):
        block = value if k == 0 else swap(value, axis, k)
        result = lax.dynamic_update_index_in_dim(result, block, here ^ k, dim)
    return result.reshape(value.shape[:dim] + (count * value.shape[dim],) + value.shape[dim + 1 :])


def root_solve(right, factor):
    rows = factor.shape[0] // CHUNKS
    blocks = [factor[c * rows : (c + 1) * rows] for c in range(CHUNKS)]
    value = {("product", c): times_transposed(right, blocks[c]).astype(jnp.bfloat16) for c in range(CHUNKS)}
    steps = {
        "sect_sum": (lambda v: direct_scatter(v, "sect"), "product"),
        "narrow_sum": (lambda v: direct_scatter(v, "narrow"), "sect_sum"),
        "narrow_all": (lambda v: direct_gather(v, "narrow"), "narrow_sum"),
        "sect_all": (lambda v: direct_gather(v, "sect"), "narrow_all"),
    }
    rounds = [
        [("sect_sum", 0)],
        [("narrow_sum", 0), ("sect_sum", 1)],
        [("narrow_all", 0), ("sect_sum", 2)],
        [("narrow_sum", 1), ("sect_all", 0)],
        [("narrow_all", 1), ("sect_sum", 3)],
        [("narrow_sum", 2), ("sect_all", 1)],
        [("narrow_all", 2)],
        [("narrow_sum", 3), ("sect_all", 2)],
        [("narrow_all", 3)],
        [("sect_all", 3)],
    ]
    before = []
    for turn in rounds:
        taken = [value[(steps[name][1], c)] for name, c in turn]
        if before:
            taken = tie(taken, before)
        before = [steps[name][0](v) for (name, c), v in zip(turn, taken)]
        for key, v in zip(turn, before):
            value[key] = v
    back = None
    for c in range(CHUNKS):
        term = times(value[("sect_all", c)], blocks[c])
        back = term if back is None else back + term
    return back, value[("narrow_all", CHUNKS - 1)]


def body(leaf_rhs, leaf_factor, leaf_coupling, root_factor, root_rhs, border_map, border_rows):
    wide_count = lax.axis_size("wide")
    narrow_count = lax.axis_size("narrow")
    sect_count = lax.axis_size("sect")
    sect_index = lax.axis_index("sect")
    wide_index = lax.axis_index("wide")
    narrow_index = lax.axis_index("narrow")
    border_block = leaf_coupling.shape[0]
    border_total = border_block * wide_count
    rows = leaf_rhs.shape[0]
    small = rows // narrow_count
    root_block = root_rhs.shape[1]
    root_start = (sect_index * narrow_count + narrow_index) * root_block

    columns = lax.broadcasted_iota(jnp.int32, (1, 1, root_block), 2) + root_start
    border_place = lax.broadcasted_iota(jnp.int32, border_map.shape, 1)
    live_map = jnp.where(border_place < border_rows[:, None], border_map, -1)
    landing = (live_map[:, :, None] == columns).astype(jnp.bfloat16)

    piece = relative_gather(leaf_rhs, "wide")
    places = relative_places("wide")
    border_terms = times_transposed(piece, leaf_coupling).astype(jnp.bfloat16)
    blocks = border_terms.reshape(wide_count, rows, border_block)
    order = [places.index(k) for k in range(wide_count)]

    def by_place(values, dim=0):
        near = [lax.index_in_dim(values, order[k], dim, keepdims=False) for k in range(wide_count)]
        near = jnp.stack(near, axis=dim)
        return jnp.stack(
            [lax.dynamic_index_in_dim(near, wide_index ^ k, dim, keepdims=False) for k in range(wide_count)],
            axis=dim,
        )

    def by_relation(values, dim=0):
        return jnp.stack(
            [lax.dynamic_index_in_dim(values, wide_index ^ p, dim, keepdims=False) for p in places],
            axis=dim,
        )

    sent = by_place(blocks).reshape(wide_count * narrow_count, small, border_block)
    got = lax.all_to_all(sent, ("wide", "narrow"), 0, 0, tiled=True)
    border_sum = jnp.sum(
        got.reshape(wide_count, narrow_count, small, border_block).astype(jnp.float32), axis=1
    )
    border_out = border_sum.transpose(1, 0, 2).reshape(small, border_total).astype(jnp.bfloat16)

    updates = direct_gather(border_out, "narrow")
    updates = direct_gather(updates[None], "sect")
    landed = jnp.zeros((rows, root_block), jnp.float32)
    for s in range(sect_count):
        landed = landed + times(updates[s], landing[s])
    root_right = (root_rhs.astype(jnp.float32) - landed).astype(jnp.bfloat16)
    right = relative_gather(root_right, "wide")

    (piece_late,) = tie([piece], [updates])
    pivot_terms = times_transposed(piece_late, leaf_factor).astype(jnp.bfloat16)
    pivot_terms = pivot_terms.reshape(wide_count, rows, -1)
    leaf_mid = lax.psum_scatter(pivot_terms, "narrow", scatter_dimension=1, tiled=True)

    back, late = root_solve(right, root_factor)
    root_solution = relative_scatter(back, "wide")

    (leaf_mid,) = tie([leaf_mid], [late])
    leaf_mid = lax.all_gather(leaf_mid, "narrow", axis=1, tiled=True).reshape(wide_count * rows, -1)

    picked = [
        times_transposed(root_solution, landing[s]).astype(jnp.bfloat16) for s in range(sect_count)
    ]
    picked = jnp.stack(picked).reshape(sect_count, narrow_count, small, wide_count, border_block)
    sent = picked.transpose(0, 3, 1, 2, 4).reshape(-1, small, border_block)
    got = lax.all_to_all(sent, ("sect", "wide", "narrow"), 0, 0, tiled=True)
    got = got.reshape(sect_count, wide_count, narrow_count, small, border_block)
    own = jnp.sum(got.astype(jnp.float32), axis=(0, 2)).astype(jnp.bfloat16)
    returned = direct_gather(by_relation(own), "narrow", 1).reshape(wide_count * rows, border_block)

    back_leaf = times(leaf_mid, leaf_factor) - times(returned, leaf_coupling)
    leaf_solution = relative_scatter(back_leaf, "wide")
    return (leaf_solution, root_solution)


def solution(mesh):
    in_specs = (
        P("wide", ("sect", "narrow")),
        P(("sect", "wide"), "narrow"),
        P(("sect", "wide"), "narrow"),
        P("wide", ("sect", "narrow")),
        P("wide", ("sect", "narrow")),
        P(),
        P(),
    )
    out_specs = (P("wide", ("sect", "narrow")), P("wide", ("sect", "narrow")))
    return jax.shard_map(body, mesh=mesh, in_specs=in_specs, out_specs=out_specs, check_vma=False)
```

time: 543 us -> 364 us (0.67)
  waiting for transfers between devices: 428 us -> 191 us
  starting transfers between devices: 4.1 us -> 81.9 us
  local copies, waits for them, and re-layouts: 20.7 us -> 7.17 us
  other arithmetic: 27.3 us -> 14.4 us
  matrix products: 41 us -> 51.1 us
  blocking collectives: 7.17 us -> 0 us
    all_gather x5 -> x0, waiting for transfers between devices: 229 us -> none  [the longest x1 75.1 us: body(): lax.all_gather(root_mid, ('sect', 'narrow'), axis=0, tiled=True)]
    reduce_scatter x4 -> x1, waiting for transfers between devices: 167 us -> 0.02 us  [body(): lax.psum_scatter(pivot_terms, 'narrow', scatter_dimension=1, tiled=True)]
    ppermute x0 -> x47, waiting for transfers between devices: none -> 136 us  [swap(): return lax.ppermute(value, axis, pairs)]
    ppermute x0 -> x47, starting transfers between devices: none -> 72.5 us  [swap(): return lax.ppermute(value, axis, pairs)]
    all_to_all x1 -> x2, waiting for transfers between devices: 0.01 us -> 54.1 us  [the longest x1 38.5 us: body(): got = lax.all_to_all(sent, ('sect', 'wide', 'narrow'), 0, 0, tiled=True)]
    scatter-add x1 -> x0, other arithmetic: 23 us -> none  [body(): landed = jnp.zeros((regrouped.shape[0], root_block), jnp.float32).at[:, t...]
    unnamed x12 -> x2, waiting for transfers between devices: 21.3 us -> 0.68 us
    all_gather x1, waiting for transfers between devices: 10.5 us -> 0.11 us  [body(): lax.all_gather(leaf_mid, 'narrow', axis=1, tiled=True)]
  transfers between devices with their start and end apart: 12 -> 51, of which waited for: 11 -> 33; matrix products, arithmetic and copies ran while one was open for 5% -> 13% of each run, Pallas kernels for 0% -> 0%
where the time goes in v1:
time: 364 us; the launch traced here: 361 us
  waiting for transfers between devices  191 us (52%)
  starting transfers between devices  81.9 us (23%)
  matrix products  51.1 us (14%)
  between operations  15.6 us (4%)
  other arithmetic  14.4 us (4%)
  local copies, waits for them, and re-layouts  7.17 us (2%)
    ppermute x47, waiting for transfers between devices, swap(): return lax.ppermute(value, axis, pairs)  136 us
    ppermute x47, starting transfers between devices, swap(): return lax.ppermute(value, axis, pairs)  72.5 us
    all_to_all x1, waiting for transfers between devices, body(): got = lax.all_to_all(sent, ('sect', 'wide', 'narrow'), 0, 0, tiled=True)  38.5 us
    dot_general x8, matrix products, times(): return jnp.dot(left, right, preferred_element_type=jnp.float32)  25.8 us
    dot_general x8, matrix products, times_transposed(): lax.dot_general(left, right, (((1,), (1,)), ((), ())), preferred_element_...  25.3 us
    all_to_all x1, waiting for transfers between devices, body(): got = lax.all_to_all(sent, ('wide', 'narrow'), 0, 0, tiled=True)  15.5 us
    eq x1, other arithmetic, body(): landing = (live_map[:, :, None] == columns).astype(jnp.bfloat16)  7.47 us
  transfers between devices with their start and end apart: 51, of which 33 were waited for; matrix products, arithmetic and copies ran while one was open for 13% of the time, Pallas kernels for 0%

profile of v1, /device:TPU:0, one launch (start us, length us, event | category | flops | bytes accessed | tf_op | source)
XLA Modules:
  0.0 361.0 jit_solution(11836097447246034239)
XLA Ops:
  7.2 3.0 collective-permute-start
  10.2 6.5 %collective-permute-done = bf16[128,1024]{1,0:T(8,128)(2,1)S(1)} collective-permute-done((bf16[128,1024]{1,0:T(8,128)(2,1)}, bf16[128,1024]{1,0:T(8,128)(2,1)S(1)}, u32[]{:S(2)}, u32[]{:S(2)}) %collective-permute-start) | collective-permute-done | bytes 262176 | tf_op jit(solution)/shard_map/ppermute | solution.py:25
  19.8 2.3 convolution_convert_fusion.1
  23.2 6.2 %all-to-all-start = ((bf16[16,32,512]{2,1,0:T(8,128)(2,1)}), bf16[16,32,512]{2,1,0:T(8,128)(2,1)S(1)}, u32[]{:S(2)}, u32[]{:S(2)}) async-start(bf16[16,32,512]{2,1,0:T(8,128)(2,1)} %bitcast.4), calls=%async_computation | async-start | bytes 1048576 | tf_op jit(solution)/shard_map/all_to_all | solution.py:159
  29.5 15.5 %all-to-all-done = bf16[16,32,512]{2,1,0:T(8,128)(2,1)S(1)} async-done(((bf16[16,32,512]{2,1,0:T(8,128)(2,1)}), bf16[16,32,512]{2,1,0:T(8,128)(2,1)S(1)}, u32[]{:S(2)}, u32[]{:S(2)}) %all-to-all-start) | async-done | bytes 524320 | tf_op jit(solution)/shard_map/all_to_all | solution.py:159
  46.6 2.9 collective-permute-start.4
  49.8 2.1 collective-permute-done.2
  52.0 6.2 %collective-permute-done.3 = bf16[32,2048]{1,0:T(8,128)(2,1)S(1)} collective-permute-done((bf16[32,2048]{1,0:T(8,128)(2,1)S(1)}, bf16[32,2048]{1,0:T(8,128)(2,1)S(1)}, u32[]{:S(2)}, u32[]{:S(2)}) %collective-permute-start.3) | collective-permute-done | bytes 131104 | tf_op jit(solution)/shard_map/ppermute | solution.py:25
  59.8 7.5 %broadcast_compare_fusion = pred[2,2048,2048]{2,1,0:T(32,128)(4,1)} fusion(s32[2048]{0:T(1024)S(1)} %iota_add_fusion, s32[2,2048]{1,0:T(2,128)S(1)} %compare_select_fusion), kind=kLoop, calls=%fused_computation | loop fusion | flops 8388608 | bytes 8413184 | tf_op jit(solution)/shard_map/eq | solution.py:136
  67.5 1.6 collective-permute-done.5
  69.1 4.9 %fusion.3 = f32[128,2048]{1,0:T(8,128)S(1)} fusion(pred[2,2048,2048]{2,1,0:T(32,128)(4,1)} %broadcast_compare_fusion, bf16[2,128,2048]{2,1,0:T(8,128)(2,1)S(1)} %constant_dynamic-update-slice_fusion), kind=kOutput, calls=%fused_computation.6 | convolution fusion | flops 1073741824 | bytes 5767168 | tf_op jit(solution)/shard_map/dot_general | solution.py:16
  74.1 3.2 fusion.26
  77.3 1.6 collective-permute-start.6
  78.9 8.4 %collective-permute-done.6 = bf16[128,2048]{1,0:T(8,128)(2,1)S(1)} collective-permute-done((bf16[128,2048]{1,0:T(8,128)(2,1)S(1)}, bf16[128,2048]{1,0:T(8,128)(2,1)S(1)}, u32[]{:S(2)}, u32[]{:S(2)}) %collective-permute-start.6) | collective-permute-done | bytes 524320 | tf_op jit(solution)/shard_map/ppermute | solution.py:25
  87.6 2.6 collective-permute-done.7
  90.2 2.4 fusion.28
  94.2 2.4 fusion.34
  96.6 2.4 fusion.31
  99.0 7.7 %collective-permute-done.8 = bf16[256,1024]{1,0:T(8,128)(2,1)S(1)} collective-permute-done((bf16[256,1024]{1,0:T(8,128)(2,1)S(1)}, bf16[256,1024]{1,0:T(8,128)(2,1)S(1)}, u32[]{:S(2)}, u32[]{:S(2)}) %collective-permute-start.8) | collective-permute-done | bytes 524320 | tf_op jit(solution)/shard_map/ppermute | solution.py:25
  107.0 5.8 %collective-permute-start.10 = (bf16[64,1024]{1,0:T(8,128)(2,1)S(1)}, bf16[64,1024]{1,0:T(8,128)(2,1)S(1)}, u32[]{:S(2)}, u32[]{:S(2)}) collective-permute-start(bf16[64,1024]{1,0:T(8,128)(2,1)S(1)} %get-tuple-element.45), channel_id=1, source_target_pairs={{0,1},{1,0},{2,3},{3,2},{4,5},{5,4},{6,7},{7,6},{8,9},{9,8},{10,11... | collective-permute-start | bytes 393224 | tf_op jit(solution)/shard_map/ppermute | solution.py:25
  115.3 1.8 collective-permute-start.9
  117.0 2.4 fusion.37
  119.4 5.7 %collective-permute-done.11 = bf16[64,1024]{1,0:T(8,128)(2,1)S(1)} collective-permute-done((bf16[64,1024]{1,0:T(8,128)(2,1)S(1)}, bf16[64,1024]{1,0:T(8,128)(2,1)S(1)}, u32[]{:S(2)}, u32[]{:S(2)}) %collective-permute-start.11) | collective-permute-done | bytes 131104 | tf_op jit(solution)/shard_map/ppermute | solution.py:25
  125.2 2.9 collective-permute-done.9
  129.2 2.1 collective-permute-start.14
  135.4 4.4 %collective-permute-done.14 = bf16[64,1024]{1,0:T(8,128)(2,1)S(1)} collective-permute-done((bf16[64,1024]{1,0:T(8,128)(2,1)S(1)}, bf16[64,1024]{1,0:T(8,128)(2,1)S(1)}, u32[]{:S(2)}, u32[]{:S(2)}) %collective-permute-start.14) | collective-permute-done | bytes 131104 | tf_op jit(solution)/shard_map/ppermute | solution.py:25
  139.8 4.9 %collective-permute-done.16 = bf16[256,1024]{1,0:T(8,128)(2,1)S(1)} collective-permute-done((bf16[256,1024]{1,0:T(8,128)(2,1)S(1)}, bf16[256,1024]{1,0:T(8,128)(2,1)S(1)}, u32[]{:S(2)}, u32[]{:S(2)}) %collective-permute-start.16) | collective-permute-done | bytes 524320 | tf_op jit(solution)/shard_map/ppermute | solution.py:25
  146.6 2.8 collective-permute-start.18
  151.1 1.8 collective-permute-done.17
  152.9 4.5 %collective-permute-done.19 = bf16[64,1024]{1,0:T(8,128)(2,1)S(1)} collective-permute-done((bf16[64,1024]{1,0:T(8,128)(2,1)S(1)}, bf16[64,1024]{1,0:T(8,128)(2,1)S(1)}, u32[]{:S(2)}, u32[]{:S(2)}) %collective-permute-start.19) | collective-permute-done | bytes 131104 | tf_op jit(solution)/shard_map/ppermute | solution.py:25
  157.6 3.3 collective-permute-start.22
  163.4 2.4 fusion.16
  166.5 3.2 collective-permute-done.23
  169.8 8.7 %collective-permute-done.21 = bf16[256,1024]{1,0:T(8,128)(2,1)S(1)} collective-permute-done((bf16[256,1024]{1,0:T(8,128)(2,1)S(1)}, bf16[256,1024]{1,0:T(8,128)(2,1)S(1)}, u32[]{:S(2)}, u32[]{:S(2)}) %collective-permute-start.21) | collective-permute-done | bytes 524320 | tf_op jit(solution)/shard_map/ppermute | solution.py:25
  178.7 1.8 collective-permute-start.28
  180.6 2.6 collective-permute-start.26
  183.1 1.8 collective-permute-start.27
  185.1 2.0 collective-permute-done.25
  187.1 3.5 collective-permute-done.26
  190.8 2.0 collective-permute-start.29
  195.2 2.4 fusion.12
  197.7 7.1 %collective-permute-done.30 = bf16[64,1024]{1,0:T(8,128)(2,1)S(1)} collective-permute-done((bf16[64,1024]{1,0:T(8,128)(2,1)S(1)}, bf16[64,1024]{1,0:T(8,128)(2,1)S(1)}, u32[]{:S(2)}, u32[]{:S(2)}) %collective-permute-start.30) | collective-permute-done | bytes 131104 | tf_op jit(solution)/shard_map/ppermute | solution.py:25
  204.9 1.6 collective-permute-start.35
  206.5 2.0 collective-permute-start.32
  209.4 1.6 collective-permute-start.34
  212.5 7.1 %collective-permute-done.33 = bf16[64,1024]{1,0:T(8,128)(2,1)S(1)} collective-permute-done((bf16[64,1024]{1,0:T(8,128)(2,1)S(1)}, bf16[64,1024]{1,0:T(8,128)(2,1)S(1)}, u32[]{:S(2)}, u32[]{:S(2)}) %collective-permute-start.33) | collective-permute-done | bytes 131104 | tf_op jit(solution)/shard_map/ppermute | solution.py:25
  219.7 3.1 collective-permute-start.36
  222.8 2.4 collective-permute-start.38
  225.8 5.6 %collective-permute-done.37 = bf16[64,1024]{1,0:T(8,128)(2,1)S(1)} collective-permute-done((bf16[64,1024]{1,0:T(8,128)(2,1)S(1)}, bf16[64,1024]{1,0:T(8,128)(2,1)S(1)}, u32[]{:S(2)}, u32[]{:S(2)}) %collective-permute-start.37) | collective-permute-done | bytes 131104 | tf_op jit(solution)/shard_map/ppermute | solution.py:25
  231.5 4.5 %fusion.8 = f32[512,2048]{1,0:T(8,128)S(1)} fusion(bf16[512,1024]{1,0:T(8,128)(2,1)S(1)} %bitcast.231, bf16[4096,2048]{1,0:T(8,128)(2,1)} %param.10), kind=kOutput, calls=%fused_computation.12 | convolution fusion | flops 2147483648 | bytes 9437184 | tf_op jit(solution)/shard_map/dot_general | solution.py:16
  236.2 4.4 %collective-permute-done.39 = bf16[256,1024]{1,0:T(8,128)(2,1)S(1)} collective-permute-done((bf16[256,1024]{1,0:T(8,128)(2,1)S(1)}, bf16[256,1024]{1,0:T(8,128)(2,1)S(1)}, u32[]{:S(2)}, u32[]{:S(2)}) %collective-permute-start.39) | collective-permute-done | bytes 524320 | tf_op jit(solution)/shard_map/ppermute | solution.py:25
  240.7 5.2 %add_add_fusion = f32[512,2048]{1,0:T(8,128)S(1)} fusion(f32[512,2048]{1,0:T(8,128)S(1)} %fusion.8, f32[512,2048]{1,0:T(8,128)S(1)} %fusion.16, f32[512,2048]{1,0:T(8,128)S(1)} %fusion.12, bf16[512,1024]{1,0:T(8,128)(2,1)S(1)} %bitcast.204, bf16[4096,2048]{1,0:T(8,128)(2,1)} %param.10), kind=kOutput, calls=%fused_computation.7 | convolution fusion | flops 2150629376 | bytes 22020096 | tf_op jit(solution)/shard_map/dot_general | solution.py:16
  246.1 2.6 collective-permute-done.40
  251.2 2.3 convolution_convert_fusion
  253.5 10.6 %collective-permute-done.41 = bf16[128,2048]{1,0:T(8,128)(2,1)} collective-permute-done((bf16[128,2048]{1,0:T(8,128)(2,1)}, bf16[128,2048]{1,0:T(8,128)(2,1)}, u32[]{:S(2)}, u32[]{:S(2)}) %collective-permute-start.41) | collective-permute-done | bytes 524320 | tf_op jit(solution)/shard_map/ppermute | solution.py:25
  266.1 5.1 %fusion.25 = bf16[128,2048]{1,0:T(8,128)(2,1)S(1)} fusion(bf16[128,2048]{1,0:T(8,128)(2,1)S(1)} %add_convert_fusion, pred[2,2048,2048]{2,1,0:T(32,128)(4,1)} %broadcast_compare_fusion), kind=kOutput, calls=%fused_computation.27 | convolution fusion | flops 1074003968 | bytes 5242880 | tf_op jit(solution)/shard_map/dot_general | solution.py:10
  271.7 6.1 %fusion.24 = bf16[128,2048]{1,0:T(8,128)(2,1)} fusion(bf16[128,2048]{1,0:T(8,128)(2,1)} %copy-done.2, pred[2,2048,2048]{2,1,0:T(32,128)(4,1)} %broadcast_compare_fusion), kind=kOutput, calls=%fused_computation.26 | convolution fusion | flops 1074003968 | bytes 5242880 | tf_op jit(solution)/shard_map/dot_general | solution.py:10
  280.4 3.2 all-to-all-start.1
  284.3 38.5 %all-to-all-done.1 = bf16[32,32,512]{2,1,0:T(8,128)(2,1)S(1)} async-done(((bf16[32,32,512]{2,1,0:T(8,128)(2,1)}), bf16[32,32,512]{2,1,0:T(8,128)(2,1)S(1)}, u32[]{:S(2)}, u32[]{:S(2)}) %all-to-all-start.1) | async-done | bytes 1048608 | tf_op jit(solution)/shard_map/all_to_all | solution.py:189
  323.1 3.9 %collective-permute-start.42 = (bf16[4,32,512]{2,1,0:T(8,128)(2,1)S(1)}, bf16[4,32,512]{2,1,0:T(8,128)(2,1)S(1)}, u32[]{:S(2)}, u32[]{:S(2)}) collective-permute-start(bf16[4,32,512]{2,1,0:T(8,128)(2,1)S(1)} %pad_maximum_fusion.6), channel_id=1, source_target_pairs={{0,1},{1,0},{2,3},{3,2},{4,5},{5,4},{6,7},{7,6},{8,9},{9,8},{10,11... | collective-permute-start | bytes 393224 | tf_op jit(solution)/shard_map/ppermute | solution.py:25
  327.1 2.6 fusion.57
  332.2 9.3 %collective-permute-done.43 = bf16[4,32,512]{2,1,0:T(8,128)(2,1)S(1)} collective-permute-done((bf16[4,32,512]{2,1,0:T(8,128)(2,1)S(1)}, bf16[4,32,512]{2,1,0:T(8,128)(2,1)S(1)}, u32[]{:S(2)}, u32[]{:S(2)}) %collective-permute-start.43) | collective-permute-done | bytes 131104 | tf_op jit(solution)/shard_map/ppermute | solution.py:25
  342.5 1.9 collective-permute-done.45
  346.0 6.9 %collective-permute-done.46 = bf16[128,1024]{1,0:T(8,128)(2,1)S(1)} collective-permute-done((bf16[128,1024]{1,0:T(8,128)(2,1)S(1)}, bf16[128,1024]{1,0:T(8,128)(2,1)S(1)}, u32[]{:S(2)}, u32[]{:S(2)}) %collective-permute-start.46) | collective-permute-done | bytes 262176 | tf_op jit(solution)/shard_map/ppermute | solution.py:25
  (179 shorter events, 45.5 us)
Async XLA Ops:
  7.2 244.1 %copy-start = (bf16[1024,1024]{1,0:T(8,128)(2,1)S(1)}, bf16[1024,1024]{1,0:T(8,128)(2,1)}, u32[]{:S(2)}) copy-start(bf16[1024,1024]{1,0:T(8,128)(2,1)} %param.8) | copy-start | bytes 6291460
  7.2 9.6 %collective-permute-start = (bf16[128,1024]{1,0:T(8,128)(2,1)}, bf16[128,1024]{1,0:T(8,128)(2,1)S(1)}, u32[]{:S(2)}, u32[]{:S(2)}) collective-permute-start(bf16[128,1024]{1,0:T(8,128)(2,1)} %param.7), channel_id=1, source_target_pairs={{0,8},{4,12},{8,0},{12,4},{1,9},{5,13},{9,1},{13,5},{2,10},{6,14},... | collective-permute-start | bytes 786440 | tf_op jit(solution)/shard_map/ppermute | solution.py:25
  17.7 2.0 collective-permute-start.1
  19.7 3.4 copy-start.3
  19.7 9.7 %copy-start.5 = (s32[2,2048]{1,0:T(2,128)S(1)}, s32[2,2048]{1,0:T(2,128)}, u32[]{:S(2)}) copy-start(s32[2,2048]{1,0:T(2,128)} %param.12) | copy-start | bytes 49156
  19.8 9.7 %copy-start.6 = (s32[2]{0:T(128)S(1)}, s32[2]{0:T(128)}, u32[]{:S(2)}) copy-start(s32[2]{0:T(128)} %param.13) | copy-start | bytes 28
  23.2 21.9 %all-to-all-start = ((bf16[16,32,512]{2,1,0:T(8,128)(2,1)}), bf16[16,32,512]{2,1,0:T(8,128)(2,1)S(1)}, u32[]{:S(2)}, u32[]{:S(2)}) async-start(bf16[16,32,512]{2,1,0:T(8,128)(2,1)} %bitcast.4), calls=%async_computation | async-start | bytes 1048576 | tf_op jit(solution)/shard_map/all_to_all | solution.py:159
  29.3 254.3 %reduce-scatter.2.cloned.1.call-start = ((), (), s32[]{:S(2)}) async-start(), calls=%async_computation.3 | async-start | bytes 1310720 | tf_op jit(solution)/shard_map/reduce_scatter | solution.py:176
  45.1 6.9 %collective-permute-start.2 = (bf16[32,2048]{1,0:T(8,128)(2,1)S(1)}, bf16[32,2048]{1,0:T(8,128)(2,1)S(1)}, u32[]{:S(2)}, u32[]{:S(2)}) collective-permute-start(bf16[32,2048]{1,0:T(8,128)(2,1)S(1)} %bitcast.242), channel_id=1, source_target_pairs={{0,1},{1,0},{2,3},{3,2},{4,5},{5,4},{6,7},{7,6},{8,9},{9,8},{10,11... | collective-permute-start | bytes 393224 | tf_op jit(solution)/shard_map/ppermute | solution.py:25
  45.2 13.0 %collective-permute-start.3 = (bf16[32,2048]{1,0:T(8,128)(2,1)S(1)}, bf16[32,2048]{1,0:T(8,128)(2,1)S(1)}, u32[]{:S(2)}, u32[]{:S(2)}) collective-permute-start(bf16[32,2048]{1,0:T(8,128)(2,1)S(1)} %bitcast.243), channel_id=1, source_target_pairs={{0,2},{1,3},{2,0},{3,1},{4,6},{5,7},{6,4},{7,5},{8,10},{9,11},{10,... | collective-permute-start | bytes 393224 | tf_op jit(solution)/shard_map/ppermute | solution.py:25
  46.6 11.6 %collective-permute-start.4 = (bf16[32,2048]{1,0:T(8,128)(2,1)S(1)}, bf16[32,2048]{1,0:T(8,128)(2,1)S(1)}, u32[]{:S(2)}, u32[]{:S(2)}) collective-permute-start(bf16[32,2048]{1,0:T(8,128)(2,1)S(1)} %bitcast.244), channel_id=1, source_target_pairs={{0,3},{1,2},{2,1},{3,0},{4,7},{5,6},{6,5},{7,4},{8,11},{9,10},{10,... | collective-permute-start | bytes 393224 | tf_op jit(solution)/shard_map/ppermute | solution.py:25
  58.2 10.8 %collective-permute-start.5 = (bf16[1,128,2048]{2,1,0:T(8,128)(2,1)S(1)}, bf16[1,128,2048]{2,1,0:T(8,128)(2,1)S(1)}, u32[]{:S(2)}, u32[]{:S(2)}) collective-permute-start(bf16[1,128,2048]{2,1,0:T(8,128)(2,1)S(1)} %bitcast.215), channel_id=1, source_target_pairs={{0,16},{16,0},{1,17},{17,1},{2,18},{18,2},{3,19},{19,3},{4,20},{20... | collective-permute-start | bytes 1572872 | tf_op jit(solution)/shard_map/ppermute | solution.py:25
  67.3 22.9 %slice-start.2 = ((s8[16777216]{0:T(1024)(128)(4,1)}), s8[4194304]{0:T(1024)(128)(4,1)S(1)}, s32[]{:S(2)}) async-start(s8[16777216]{0:T(1024)(128)(4,1)} %bitcast.240), calls=%async_computation.7 | async-start | bytes 8388608
  69.0 5.0 %slice-start = ((s8[8388608]{0:T(1024)(128)(4,1)}), s8[4194304]{0:T(1024)(128)(4,1)S(1)}, s32[]{:S(2)}) async-start(s8[8388608]{0:T(1024)(128)(4,1)} %bitcast.202), calls=%async_computation.5 | async-start | bytes 8388608
  69.1 5.0 %copy-start.7 = (bf16[128,2048]{1,0:T(8,128)(2,1)S(1)}, bf16[128,2048]{1,0:T(8,128)(2,1)}, u32[]{:S(2)}) copy-start(bf16[128,2048]{1,0:T(8,128)(2,1)} %param.11) | copy-start | bytes 1572868
  69.1 5.0 %slice-start.1 = ((s8[8388608]{0:T(1024)(128)(4,1)}), s8[4194304]{0:T(1024)(128)(4,1)S(1)}, s32[]{:S(2)}) async-start(s8[8388608]{0:T(1024)(128)(4,1)} %bitcast.202), calls=%async_computation.6 | async-start | bytes 8388608
  69.1 21.1 %slice-start.3 = ((s8[16777216]{0:T(1024)(128)(4,1)}), s8[4194304]{0:T(1024)(128)(4,1)S(1)}, s32[]{:S(2)}) async-start(s8[16777216]{0:T(1024)(128)(4,1)} %bitcast.240), calls=%async_computation.8 | async-start | bytes 8388608
  69.1 21.1 %slice-start.4 = ((s8[16777216]{0:T(1024)(128)(4,1)}), s8[4194304]{0:T(1024)(128)(4,1)S(1)}, s32[]{:S(2)}) async-start(s8[16777216]{0:T(1024)(128)(4,1)} %bitcast.240), calls=%async_computation.9 | async-start | bytes 8388608
  74.1 16.1 %slice-start.5 = ((s8[16777216]{0:T(1024)(128)(4,1)}), s8[4194304]{0:T(1024)(128)(4,1)S(1)}, s32[]{:S(2)}) async-start(s8[16777216]{0:T(1024)(128)(4,1)} %bitcast.240), calls=%async_computation.10 | async-start | bytes 8388608
  77.3 10.0 %collective-permute-start.6 = (bf16[128,2048]{1,0:T(8,128)(2,1)S(1)}, bf16[128,2048]{1,0:T(8,128)(2,1)S(1)}, u32[]{:S(2)}, u32[]{:S(2)}) collective-permute-start(bf16[128,2048]{1,0:T(8,128)(2,1)S(1)} %fusion.26), channel_id=1, source_target_pairs={{0,8},{4,12},{8,0},{12,4},{1,9},{5,13},{9,1},{13,5},{2,10},{6,14},... | collective-permute-start | bytes 1572872 | tf_op jit(solution)/shard_map/ppermute | solution.py:25
  87.5 2.7 collective-permute-start.7
  92.7 14.0 %collective-permute-start.8 = (bf16[256,1024]{1,0:T(8,128)(2,1)S(1)}, bf16[256,1024]{1,0:T(8,128)(2,1)S(1)}, u32[]{:S(2)}, u32[]{:S(2)}) collective-permute-start(bf16[256,1024]{1,0:T(8,128)(2,1)S(1)} %dynamic-slice_bitcast_fusion.3), channel_id=1, source_target_pairs={{0,16},{16,0},{1,17},{17,1},{2,18},{18,2},{3,19},{19,3},{4,20},{20... | collective-permute-start | bytes 1572872 | tf_op jit(solution)/shard_map/ppermute | solution.py:25
  107.0 12.5 %collective-permute-start.10 = (bf16[64,1024]{1,0:T(8,128)(2,1)S(1)}, bf16[64,1024]{1,0:T(8,128)(2,1)S(1)}, u32[]{:S(2)}, u32[]{:S(2)}) collective-permute-start(bf16[64,1024]{1,0:T(8,128)(2,1)S(1)} %get-tuple-element.45), channel_id=1, source_target_pairs={{0,1},{1,0},{2,3},{3,2},{4,5},{5,4},{6,7},{7,6},{8,9},{9,8},{10,11... | collective-permute-start | bytes 393224 | tf_op jit(solution)/shard_map/ppermute | solution.py:25
  112.8 12.3 %collective-permute-start.11 = (bf16[64,1024]{1,0:T(8,128)(2,1)S(1)}, bf16[64,1024]{1,0:T(8,128)(2,1)S(1)}, u32[]{:S(2)}, u32[]{:S(2)}) collective-permute-start(bf16[64,1024]{1,0:T(8,128)(2,1)S(1)} %get-tuple-element.47), channel_id=1, source_target_pairs={{0,2},{1,3},{2,0},{3,1},{4,6},{5,7},{6,4},{7,5},{8,10},{9,11},{10,... | collective-permute-start | bytes 393224 | tf_op jit(solution)/shard_map/ppermute | solution.py:25
  113.7 11.4 %collective-permute-start.12 = (bf16[64,1024]{1,0:T(8,128)(2,1)S(1)}, bf16[64,1024]{1,0:T(8,128)(2,1)S(1)}, u32[]{:S(2)}, u32[]{:S(2)}) collective-permute-start(bf16[64,1024]{1,0:T(8,128)(2,1)S(1)} %get-tuple-element.46), channel_id=1, source_target_pairs={{0,3},{1,2},{2,1},{3,0},{4,7},{5,6},{6,5},{7,4},{8,11},{9,10},{10,... | collective-permute-start | bytes 393224 | tf_op jit(solution)/shard_map/ppermute | solution.py:25
  115.3 12.8 %collective-permute-start.9 = (bf16[256,1024]{1,0:T(8,128)(2,1)S(1)}, bf16[256,1024]{1,0:T(8,128)(2,1)S(1)}, u32[]{:S(2)}, u32[]{:S(2)}) collective-permute-start(bf16[256,1024]{1,0:T(8,128)(2,1)S(1)} %dynamic-slice_bitcast_fusion.2), channel_id=1, source_target_pairs={{0,16},{16,0},{1,17},{17,1},{2,18},{18,2},{3,19},{19,3},{4,20},{20... | collective-permute-start | bytes 1572872 | tf_op jit(solution)/shard_map/ppermute | solution.py:25
  128.3 7.0 %collective-permute-start.13 = (bf16[64,1024]{1,0:T(8,128)(2,1)S(1)}, bf16[64,1024]{1,0:T(8,128)(2,1)S(1)}, u32[]{:S(2)}, u32[]{:S(2)}) collective-permute-start(bf16[64,1024]{1,0:T(8,128)(2,1)S(1)} %fusion.56), channel_id=1, source_target_pairs={{0,1},{1,0},{2,3},{3,2},{4,5},{5,4},{6,7},{7,6},{8,9},{9,8},{10,11... | collective-permute-start | bytes 393224 | tf_op jit(solution)/shard_map/ppermute | solution.py:25
  129.2 10.6 %collective-permute-start.14 = (bf16[64,1024]{1,0:T(8,128)(2,1)S(1)}, bf16[64,1024]{1,0:T(8,128)(2,1)S(1)}, u32[]{:S(2)}, u32[]{:S(2)}) collective-permute-start(bf16[64,1024]{1,0:T(8,128)(2,1)S(1)} %fusion.56), channel_id=1, source_target_pairs={{0,2},{1,3},{2,0},{3,1},{4,6},{5,7},{6,4},{7,5},{8,10},{9,11},{10,... | collective-permute-start | bytes 393224 | tf_op jit(solution)/shard_map/ppermute | solution.py:25
  131.2 8.6 %collective-permute-start.15 = (bf16[64,1024]{1,0:T(8,128)(2,1)S(1)}, bf16[64,1024]{1,0:T(8,128)(2,1)S(1)}, u32[]{:S(2)}, u32[]{:S(2)}) collective-permute-start(bf16[64,1024]{1,0:T(8,128)(2,1)S(1)} %fusion.56), channel_id=1, source_target_pairs={{0,3},{1,2},{2,1},{3,0},{4,7},{5,6},{6,5},{7,4},{8,11},{9,10},{10,... | collective-permute-start | bytes 393224 | tf_op jit(solution)/shard_map/ppermute | solution.py:25
  132.8 11.9 %collective-permute-start.16 = (bf16[256,1024]{1,0:T(8,128)(2,1)S(1)}, bf16[256,1024]{1,0:T(8,128)(2,1)S(1)}, u32[]{:S(2)}, u32[]{:S(2)}) collective-permute-start(bf16[256,1024]{1,0:T(8,128)(2,1)S(1)} %dynamic-slice_bitcast_fusion.1), channel_id=1, source_target_pairs={{0,16},{16,0},{1,17},{17,1},{2,18},{18,2},{3,19},{19,3},{4,20},{20... | collective-permute-start | bytes 1572872 | tf_op jit(solution)/shard_map/ppermute | solution.py:25
  144.9 12.7 %collective-permute-start.20 = (bf16[256,1024]{1,0:T(8,128)(2,1)S(1)}, bf16[256,1024]{1,0:T(8,128)(2,1)S(1)}, u32[]{:S(2)}, u32[]{:S(2)}) collective-permute-start(bf16[256,1024]{1,0:T(8,128)(2,1)S(1)} %bitcast.217), channel_id=1, source_target_pairs={{0,16},{16,0},{1,17},{17,1},{2,18},{18,2},{3,19},{19,3},{4,20},{20... | collective-permute-start | bytes 1572872 | tf_op jit(solution)/shard_map/ppermute | solution.py:25
  146.5 6.5 %collective-permute-start.17 = (bf16[64,1024]{1,0:T(8,128)(2,1)S(1)}, bf16[64,1024]{1,0:T(8,128)(2,1)S(1)}, u32[]{:S(2)}, u32[]{:S(2)}) collective-permute-start(bf16[64,1024]{1,0:T(8,128)(2,1)S(1)} %get-tuple-element.42), channel_id=1, source_target_pairs={{0,1},{1,0},{2,3},{3,2},{4,5},{5,4},{6,7},{7,6},{8,9},{9,8},{10,11... | collective-permute-start | bytes 393224 | tf_op jit(solution)/shard_map/ppermute | solution.py:25
  146.6 6.4 %collective-permute-start.18 = (bf16[64,1024]{1,0:T(8,128)(2,1)S(1)}, bf16[64,1024]{1,0:T(8,128)(2,1)S(1)}, u32[]{:S(2)}, u32[]{:S(2)}) collective-permute-start(bf16[64,1024]{1,0:T(8,128)(2,1)S(1)} %get-tuple-element.44), channel_id=1, source_target_pairs={{0,2},{1,3},{2,0},{3,1},{4,6},{5,7},{6,4},{7,5},{8,10},{9,11},{10,... | collective-permute-start | bytes 393224 | tf_op jit(solution)/shard_map/ppermute | solution.py:25
  149.4 8.1 %collective-permute-start.19 = (bf16[64,1024]{1,0:T(8,128)(2,1)S(1)}, bf16[64,1024]{1,0:T(8,128)(2,1)S(1)}, u32[]{:S(2)}, u32[]{:S(2)}) collective-permute-start(bf16[64,1024]{1,0:T(8,128)(2,1)S(1)} %get-tuple-element.43), channel_id=1, source_target_pairs={{0,3},{1,2},{2,1},{3,0},{4,7},{5,6},{6,5},{7,4},{8,11},{9,10},{10,... | collective-permute-start | bytes 393224 | tf_op jit(solution)/shard_map/ppermute | solution.py:25
  157.6 8.9 %collective-permute-start.22 = (bf16[64,1024]{1,0:T(8,128)(2,1)S(1)}, bf16[64,1024]{1,0:T(8,128)(2,1)S(1)}, u32[]{:S(2)}, u32[]{:S(2)}) collective-permute-start(bf16[64,1024]{1,0:T(8,128)(2,1)S(1)} %fusion.53), channel_id=1, source_target_pairs={{0,1},{1,0},{2,3},{3,2},{4,5},{5,4},{6,7},{7,6},{8,9},{9,8},{10,11... | collective-permute-start | bytes 393224 | tf_op jit(solution)/shard_map/ppermute | solution.py:25
  161.0 8.8 %collective-permute-start.23 = (bf16[64,1024]{1,0:T(8,128)(2,1)S(1)}, bf16[64,1024]{1,0:T(8,128)(2,1)S(1)}, u32[]{:S(2)}, u32[]{:S(2)}) collective-permute-start(bf16[64,1024]{1,0:T(8,128)(2,1)S(1)} %fusion.53), channel_id=1, source_target_pairs={{0,2},{1,3},{2,0},{3,1},{4,6},{5,7},{6,4},{7,5},{8,10},{9,11},{10,... | collective-permute-start | bytes 393224 | tf_op jit(solution)/shard_map/ppermute | solution.py:25
  162.0 7.7 %collective-permute-start.24 = (bf16[64,1024]{1,0:T(8,128)(2,1)S(1)}, bf16[64,1024]{1,0:T(8,128)(2,1)S(1)}, u32[]{:S(2)}, u32[]{:S(2)}) collective-permute-start(bf16[64,1024]{1,0:T(8,128)(2,1)S(1)} %fusion.53), channel_id=1, source_target_pairs={{0,3},{1,2},{2,1},{3,0},{4,7},{5,6},{6,5},{7,4},{8,11},{9,10},{10,... | collective-permute-start | bytes 393224 | tf_op jit(solution)/shard_map/ppermute | solution.py:25
  165.8 12.6 %collective-permute-start.21 = (bf16[256,1024]{1,0:T(8,128)(2,1)S(1)}, bf16[256,1024]{1,0:T(8,128)(2,1)S(1)}, u32[]{:S(2)}, u32[]{:S(2)}) collective-permute-start(bf16[256,1024]{1,0:T(8,128)(2,1)S(1)} %dynamic-slice_bitcast_fusion), channel_id=1, source_target_pairs={{0,16},{16,0},{1,17},{17,1},{2,18},{18,2},{3,19},{19,3},{4,20},{20... | collective-permute-start | bytes 1572872 | tf_op jit(solution)/shard_map/ppermute | solution.py:25
  178.7 12.1 %collective-permute-start.28 = (bf16[256,1024]{1,0:T(8,128)(2,1)S(1)}, bf16[256,1024]{1,0:T(8,128)(2,1)S(1)}, u32[]{:S(2)}, u32[]{:S(2)}) collective-permute-start(bf16[256,1024]{1,0:T(8,128)(2,1)S(1)} %bitcast.219), channel_id=1, source_target_pairs={{0,16},{16,0},{1,17},{17,1},{2,18},{18,2},{3,19},{19,3},{4,20},{20... | collective-permute-start | bytes 1572872 | tf_op jit(solution)/shard_map/ppermute | solution.py:25
  180.5 6.6 %collective-permute-start.25 = (bf16[64,1024]{1,0:T(8,128)(2,1)S(1)}, bf16[64,1024]{1,0:T(8,128)(2,1)S(1)}, u32[]{:S(2)}, u32[]{:S(2)}) collective-permute-start(bf16[64,1024]{1,0:T(8,128)(2,1)S(1)} %get-tuple-element.39), channel_id=1, source_target_pairs={{0,1},{1,0},{2,3},{3,2},{4,5},{5,4},{6,7},{7,6},{8,9},{9,8},{10,11... | collective-permute-start | bytes 393224 | tf_op jit(solution)/shard_map/ppermute | solution.py:25
  180.6 10.1 %collective-permute-start.26 = (bf16[64,1024]{1,0:T(8,128)(2,1)S(1)}, bf16[64,1024]{1,0:T(8,128)(2,1)S(1)}, u32[]{:S(2)}, u32[]{:S(2)}) collective-permute-start(bf16[64,1024]{1,0:T(8,128)(2,1)S(1)} %get-tuple-element.41), channel_id=1, source_target_pairs={{0,2},{1,3},{2,0},{3,1},{4,6},{5,7},{6,4},{7,5},{8,10},{9,11},{10,... | collective-permute-start | bytes 393224 | tf_op jit(solution)/shard_map/ppermute | solution.py:25
  183.1 7.5 %collective-permute-start.27 = (bf16[64,1024]{1,0:T(8,128)(2,1)S(1)}, bf16[64,1024]{1,0:T(8,128)(2,1)S(1)}, u32[]{:S(2)}, u32[]{:S(2)}) collective-permute-start(bf16[64,1024]{1,0:T(8,128)(2,1)S(1)} %get-tuple-element.40), channel_id=1, source_target_pairs={{0,3},{1,2},{2,1},{3,0},{4,7},{5,6},{6,5},{7,4},{8,11},{9,10},{10,... | collective-permute-start | bytes 393224 | tf_op jit(solution)/shard_map/ppermute | solution.py:25
  190.8 6.9 %collective-permute-start.29 = (bf16[64,1024]{1,0:T(8,128)(2,1)S(1)}, bf16[64,1024]{1,0:T(8,128)(2,1)S(1)}, u32[]{:S(2)}, u32[]{:S(2)}) collective-permute-start(bf16[64,1024]{1,0:T(8,128)(2,1)S(1)} %fusion.50), channel_id=1, source_target_pairs={{0,1},{1,0},{2,3},{3,2},{4,5},{5,4},{6,7},{7,6},{8,9},{9,8},{10,11... | collective-permute-start | bytes 393224 | tf_op jit(solution)/shard_map/ppermute | solution.py:25
  192.8 12.0 %collective-permute-start.30 = (bf16[64,1024]{1,0:T(8,128)(2,1)S(1)}, bf16[64,1024]{1,0:T(8,128)(2,1)S(1)}, u32[]{:S(2)}, u32[]{:S(2)}) collective-permute-start(bf16[64,1024]{1,0:T(8,128)(2,1)S(1)} %fusion.50), channel_id=1, source_target_pairs={{0,2},{1,3},{2,0},{3,1},{4,6},{5,7},{6,4},{7,5},{8,10},{9,11},{10,... | collective-permute-start | bytes 393224 | tf_op jit(solution)/shard_map/ppermute | solution.py:25
  193.7 11.2 %collective-permute-start.31 = (bf16[64,1024]{1,0:T(8,128)(2,1)S(1)}, bf16[64,1024]{1,0:T(8,128)(2,1)S(1)}, u32[]{:S(2)}, u32[]{:S(2)}) collective-permute-start(bf16[64,1024]{1,0:T(8,128)(2,1)S(1)} %fusion.50), channel_id=1, source_target_pairs={{0,3},{1,2},{2,1},{3,0},{4,7},{5,6},{6,5},{7,4},{8,11},{9,10},{10,... | collective-permute-start | bytes 393224 | tf_op jit(solution)/shard_map/ppermute | solution.py:25
  204.9 14.7 %collective-permute-start.35 = (bf16[256,1024]{1,0:T(8,128)(2,1)S(1)}, bf16[256,1024]{1,0:T(8,128)(2,1)S(1)}, u32[]{:S(2)}, u32[]{:S(2)}) collective-permute-start(bf16[256,1024]{1,0:T(8,128)(2,1)S(1)} %bitcast.221), channel_id=1, source_target_pairs={{0,16},{16,0},{1,17},{17,1},{2,18},{18,2},{3,19},{19,3},{4,20},{20... | collective-permute-start | bytes 1572872 | tf_op jit(solution)/shard_map/ppermute | solution.py:25
  206.5 6.0 %collective-permute-start.32 = (bf16[64,1024]{1,0:T(8,128)(2,1)S(1)}, bf16[64,1024]{1,0:T(8,128)(2,1)S(1)}, u32[]{:S(2)}, u32[]{:S(2)}) collective-permute-start(bf16[64,1024]{1,0:T(8,128)(2,1)S(1)} %get-tuple-element.36), channel_id=1, source_target_pairs={{0,1},{1,0},{2,3},{3,2},{4,5},{5,4},{6,7},{7,6},{8,9},{9,8},{10,11... | collective-permute-start | bytes 393224 | tf_op jit(solution)/shard_map/ppermute | solution.py:25
  208.5 11.0 %collective-permute-start.33 = (bf16[64,1024]{1,0:T(8,128)(2,1)S(1)}, bf16[64,1024]{1,0:T(8,128)(2,1)S(1)}, u32[]{:S(2)}, u32[]{:S(2)}) collective-permute-start(bf16[64,1024]{1,0:T(8,128)(2,1)S(1)} %get-tuple-element.38), channel_id=1, source_target_pairs={{0,2},{1,3},{2,0},{3,1},{4,6},{5,7},{6,4},{7,5},{8,10},{9,11},{10,... | collective-permute-start | bytes 393224 | tf_op jit(solution)/shard_map/ppermute | solution.py:25
  209.4 10.2 %collective-permute-start.34 = (bf16[64,1024]{1,0:T(8,128)(2,1)S(1)}, bf16[64,1024]{1,0:T(8,128)(2,1)S(1)}, u32[]{:S(2)}, u32[]{:S(2)}) collective-permute-start(bf16[64,1024]{1,0:T(8,128)(2,1)S(1)} %get-tuple-element.37), channel_id=1, source_target_pairs={{0,3},{1,2},{2,1},{3,0},{4,7},{5,6},{6,5},{7,4},{8,11},{9,10},{10,... | collective-permute-start | bytes 393224 | tf_op jit(solution)/shard_map/ppermute | solution.py:25
  219.7 6.1 %collective-permute-start.36 = (bf16[64,1024]{1,0:T(8,128)(2,1)S(1)}, bf16[64,1024]{1,0:T(8,128)(2,1)S(1)}, u32[]{:S(2)}, u32[]{:S(2)}) collective-permute-start(bf16[64,1024]{1,0:T(8,128)(2,1)S(1)} %fusion.47), channel_id=1, source_target_pairs={{0,1},{1,0},{2,3},{3,2},{4,5},{5,4},{6,7},{7,6},{8,9},{9,8},{10,11... | collective-permute-start | bytes 393224 | tf_op jit(solution)/shard_map/ppermute | solution.py:25
  222.8 8.5 %collective-permute-start.37 = (bf16[64,1024]{1,0:T(8,128)(2,1)S(1)}, bf16[64,1024]{1,0:T(8,128)(2,1)S(1)}, u32[]{:S(2)}, u32[]{:S(2)}) collective-permute-start(bf16[64,1024]{1,0:T(8,128)(2,1)S(1)} %fusion.47), channel_id=1, source_target_pairs={{0,2},{1,3},{2,0},{3,1},{4,6},{5,7},{6,4},{7,5},{8,10},{9,11},{10,... | collective-permute-start | bytes 393224 | tf_op jit(solution)/shard_map/ppermute | solution.py:25
  222.8 8.6 %collective-permute-start.38 = (bf16[64,1024]{1,0:T(8,128)(2,1)S(1)}, bf16[64,1024]{1,0:T(8,128)(2,1)S(1)}, u32[]{:S(2)}, u32[]{:S(2)}) collective-permute-start(bf16[64,1024]{1,0:T(8,128)(2,1)S(1)} %fusion.47), channel_id=1, source_target_pairs={{0,3},{1,2},{2,1},{3,0},{4,7},{5,6},{6,5},{7,4},{8,11},{9,10},{10,... | collective-permute-start | bytes 393224 | tf_op jit(solution)/shard_map/ppermute | solution.py:25
  231.4 9.2 %collective-permute-start.39 = (bf16[256,1024]{1,0:T(8,128)(2,1)S(1)}, bf16[256,1024]{1,0:T(8,128)(2,1)S(1)}, u32[]{:S(2)}, u32[]{:S(2)}) collective-permute-start(bf16[256,1024]{1,0:T(8,128)(2,1)S(1)} %bitcast.223), channel_id=1, source_target_pairs={{0,16},{16,0},{1,17},{17,1},{2,18},{18,2},{3,19},{19,3},{4,20},{20... | collective-permute-start | bytes 1572872 | tf_op jit(solution)/shard_map/ppermute | solution.py:25
  245.9 5.4 %copy-start.4 = (bf16[512,1024]{1,0:T(8,128)(2,1)S(1)}, bf16[512,1024]{1,0:T(8,128)(2,1)}, u32[]{:S(2)}) copy-start(bf16[512,1024]{1,0:T(8,128)(2,1)} %copy-done.3) | copy-start | bytes 3145732
  246.0 2.7 collective-permute-start.40
  249.9 14.3 %collective-permute-start.41 = (bf16[128,2048]{1,0:T(8,128)(2,1)}, bf16[128,2048]{1,0:T(8,128)(2,1)}, u32[]{:S(2)}, u32[]{:S(2)}) collective-permute-start(bf16[128,2048]{1,0:T(8,128)(2,1)} %slice.111), channel_id=1, source_target_pairs={{0,8},{4,12},{8,0},{12,4},{1,9},{5,13},{9,1},{13,5},{2,10},{6,14},... | collective-permute-start | bytes 1572872 | tf_op jit(solution)/shard_map/ppermute | solution.py:25
  280.4 42.5 %all-to-all-start.1 = ((bf16[32,32,512]{2,1,0:T(8,128)(2,1)}), bf16[32,32,512]{2,1,0:T(8,128)(2,1)S(1)}, u32[]{:S(2)}, u32[]{:S(2)}) async-start(bf16[32,32,512]{2,1,0:T(8,128)(2,1)} %bitcast.206), calls=%async_computation.2 | async-start | bytes 2097152 | tf_op jit(solution)/shard_map/all_to_all | solution.py:189
  283.6 43.5 %all-gather.2.cloned.1.call-start = ((), (), s32[]{:S(2)}) async-start(), calls=%async_computation.4 | async-start | bytes 1310720 | tf_op jit(solution)/shard_map/all_gather | solution.py:182
  323.1 9.1 %collective-permute-start.42 = (bf16[4,32,512]{2,1,0:T(8,128)(2,1)S(1)}, bf16[4,32,512]{2,1,0:T(8,128)(2,1)S(1)}, u32[]{:S(2)}, u32[]{:S(2)}) collective-permute-start(bf16[4,32,512]{2,1,0:T(8,128)(2,1)S(1)} %pad_maximum_fusion.6), channel_id=1, source_target_pairs={{0,1},{1,0},{2,3},{3,2},{4,5},{5,4},{6,7},{7,6},{8,9},{9,8},{10,11... | collective-permute-start | bytes 393224 | tf_op jit(solution)/shard_map/ppermute | solution.py:25
  327.1 14.5 %copy-start.1 = (bf16[512,1024]{1,0:T(8,128)(2,1)S(1)}, bf16[512,1024]{1,0:T(8,128)(2,1)}, u32[]{:S(2)}) copy-start(bf16[512,1024]{1,0:T(8,128)(2,1)} %param.9) | copy-start | bytes 3145732
  329.6 11.9 %collective-permute-start.43 = (bf16[4,32,512]{2,1,0:T(8,128)(2,1)S(1)}, bf16[4,32,512]{2,1,0:T(8,128)(2,1)S(1)}, u32[]{:S(2)}, u32[]{:S(2)}) collective-permute-start(bf16[4,32,512]{2,1,0:T(8,128)(2,1)S(1)} %pad_maximum_fusion.6), channel_id=1, source_target_pairs={{0,2},{1,3},{2,0},{3,1},{4,6},{5,7},{6,4},{7,5},{8,10},{9,11},{10,... | collective-permute-start | bytes 393224 | tf_op jit(solution)/shard_map/ppermute | solution.py:25
  331.0 10.5 %collective-permute-start.44 = (bf16[4,32,512]{2,1,0:T(8,128)(2,1)S(1)}, bf16[4,32,512]{2,1,0:T(8,128)(2,1)S(1)}, u32[]{:S(2)}, u32[]{:S(2)}) collective-permute-start(bf16[4,32,512]{2,1,0:T(8,128)(2,1)S(1)} %pad_maximum_fusion.6), channel_id=1, source_target_pairs={{0,3},{1,2},{2,1},{3,0},{4,7},{5,6},{6,5},{7,4},{8,11},{9,10},{10,... | collective-permute-start | bytes 393224 | tf_op jit(solution)/shard_map/ppermute | solution.py:25
  342.4 2.0 collective-permute-start.45
  344.5 8.4 %collective-permute-start.46 = (bf16[128,1024]{1,0:T(8,128)(2,1)S(1)}, bf16[128,1024]{1,0:T(8,128)(2,1)S(1)}, u32[]{:S(2)}, u32[]{:S(2)}) collective-permute-start(bf16[128,1024]{1,0:T(8,128)(2,1)S(1)} %slice.115), channel_id=1, source_target_pairs={{0,8},{4,12},{8,0},{12,4},{1,9},{5,13},{9,1},{13,5},{2,10},{6,14},... | collective-permute-start | bytes 786440 | tf_op jit(solution)/shard_map/ppermute | solution.py:25
  (1 other events, 0.8 us)
Sparse Core Ops, SparseCore 0:
  253.6 25.2 reduce-scatter.1
  286.1 40.9 all-gather.1

commit v2 on v1

--- a/solution.py
+++ b/solution.py
@@ -16,8 +16,10 @@
     return jnp.dot(left, right, preferred_element_type=jnp.float32)
 
 
-def tie(values, others):
-    return lax.optimization_barrier(tuple(values) + tuple(others))[: len(values)]
+def hold(value, other):
+    corner = lax.slice(other, (0,) * other.ndim, (1,) * other.ndim).reshape(())
+    zero = lax.clamp(jnp.int32(0), corner.astype(jnp.int32), jnp.int32(0))
+    return value + zero.astype(value.dtype)
 
 
 def swap(value, axis, distance):
@@ -32,16 +34,15 @@
     return result.astype(jnp.bfloat16)
 
 
-def relative_gather(value, axis):
+def relative_gather(value, axis, last=1):
     distance = lax.axis_size(axis) // 2
-    while distance >= 1:
+    while distance >= last:
         value = jnp.concatenate([value, swap(value, axis, distance)], axis=0)
         distance //= 2
     return value
 
 
-def relative_scatter(value, axis):
-    distance = 1
+def relative_scatter(value, axis, distance=1):
     while distance < lax.axis_size(axis):
         half = value.shape[0] // 2
         value = total([value[:half], swap(value[half:].astype(jnp.bfloat16), axis, distance)])
@@ -79,41 +80,57 @@
     return result.reshape(value.shape[:dim] + (count * value.shape[dim],) + value.shape[dim + 1 :])
 
 
-def root_solve(right, factor):
+def halve(value, axis, distance, other=None):
+    bit = (lax.axis_index(axis) // distance) % 2
+    halves = value.reshape((2, value.shape[0] // 2) + value.shape[1:])
+    kept, given = (lax.dynamic_index_in_dim(halves, k, 0, keepdims=False) for k in (bit, 1 - bit))
+    if other is not None:
+        given = hold(given, other)
+    return total([kept, swap(given, axis, distance)])
+
+
+def double(value, axis, distance):
+    bit = (lax.axis_index(axis) // distance) % 2
+    result = jnp.zeros((2,) + value.shape, value.dtype)
+    result = lax.dynamic_update_index_in_dim(result, value, bit, 0)
+    result = lax.dynamic_update_index_in_dim(result, swap(value, axis, distance), 1 - bit, 0)
+    return result.reshape((2 * value.shape[0],) + value.shape[1:])
+
+
+def distances(axis):
+    return [(axis, 1 << k) for k in range(lax.axis_size(axis).bit_length() - 1)]
+
+
+def sum_all(value, order, other):
+    first = value = halve(value, *order[0], other)
+    for axis, distance in order[1:]:
+        value = halve(value, axis, distance)
+    for axis, distance in reversed(order):
+        value = double(value, axis, distance)
+    return value, first
+
+
+def root_solve(right, factor, beside):
     rows = factor.shape[0] // CHUNKS
+    half = right.shape[0] // 2
+    sect, narrow = distances("sect"), distances("narrow")
+    orders = [sect + narrow, narrow[:1] + sect + narrow[1:]]
     blocks = [factor[c * rows : (c + 1) * rows] for c in range(CHUNKS)]
-    value = {("product", c): times_transposed(right, blocks[c]).astype(jnp.bfloat16) for c in range(CHUNKS)}
-    steps = {
-        "sect_sum": (lambda v: direct_scatter(v, "sect"), "product"),
-        "narrow_sum": (lambda v: direct_scatter(v, "narrow"), "sect_sum"),
-        "narrow_all": (lambda v: direct_gather(v, "narrow"), "narrow_sum"),
-        "sect_all": (lambda v: direct_gather(v, "sect"), "narrow_all"),
-    }
-    rounds = [
-        [("sect_sum", 0)],
-        [("narrow_sum", 0), ("sect_sum", 1)],
-        [("narrow_all", 0), ("sect_sum", 2)],
-        [("narrow_sum", 1), ("sect_all", 0)],
-        [("narrow_all", 1), ("sect_sum", 3)],
-        [("narrow_sum", 2), ("sect_all", 1)],
-        [("narrow_all", 2)],
-        [("narrow_sum", 3), ("sect_all", 2)],
-        [("narrow_all", 3)],
-        [("sect_all", 3)],
-    ]
-    before = []
-    for turn in rounds:
-        taken = [value[(steps[name][1], c)] for name, c in turn]
-        if before:
-            taken = tie(taken, before)
-        before = [steps[name][0](v) for (name, c), v in zip(turn, taken)]
-        for key, v in zip(turn, before):
-            value[key] = v
-    back = None
+    middles, firsts = [], []
     for c in range(CHUNKS):
-        term = times(value[("sect_all", c)], blocks[c])
-        back = term if back is None else back + term
-    return back, value[("narrow_all", CHUNKS - 1)]
+        product = times_transposed(right, blocks[c]).astype(jnp.bfloat16)
+        other = firsts[c - len(orders)] if c >= len(orders) else beside
+        middle, first = sum_all(product, orders[c % len(orders)], other)
+        middles.append(middle)
+        firsts.append(first)
+    backs = []
+    for part in (slice(half, None), slice(0, half)):
+        back = None
+        for c in range(CHUNKS):
+            term = times(middles[c][part], blocks[c])
+            back = term if back is None else back + term
+        backs.append(back)
+    return backs, middles
 
 
 def body(leaf_rhs, leaf_factor, leaf_coupling, root_factor, root_rhs, border_map, border_rows):
@@ -163,29 +180,31 @@
     border_out = border_sum.transpose(1, 0, 2).reshape(small, border_total).astype(jnp.bfloat16)
 
     updates = direct_gather(border_out, "narrow")
+    pivot_terms = times_transposed(piece, leaf_factor).astype(jnp.bfloat16)
+    pivot_terms = hold(pivot_terms.reshape(wide_count, rows, -1), updates)
+    leaf_mid = lax.psum_scatter(pivot_terms, "narrow", scatter_dimension=1, tiled=True)
     updates = direct_gather(updates[None], "sect")
     landed = jnp.zeros((rows, root_block), jnp.float32)
     for s in range(sect_count):
         landed = landed + times(updates[s], landing[s])
     root_right = (root_rhs.astype(jnp.float32) - landed).astype(jnp.bfloat16)
-    right = relative_gather(root_right, "wide")
-
-    (piece_late,) = tie([piece], [updates])
-    pivot_terms = times_transposed(piece_late, leaf_factor).astype(jnp.bfloat16)
-    pivot_terms = pivot_terms.reshape(wide_count, rows, -1)
-    leaf_mid = lax.psum_scatter(pivot_terms, "narrow", scatter_dimension=1, tiled=True)
-
-    back, late = root_solve(right, root_factor)
-    root_solution = relative_scatter(back, "wide")
-
-    (leaf_mid,) = tie([leaf_mid], [late])
+    right = relative_gather(root_right, "wide", 2)
+    right = jnp.concatenate([right, swap(right, "wide", 1)], axis=0)
+
+    (given, kept), late = root_solve(right, root_factor, leaf_mid)
+    kept = total([kept, swap(given.astype(jnp.bfloat16), "wide", 1)])
+    root_solution = relative_scatter(kept, "wide", 2)
+
+    leaf_mid = hold(leaf_mid, late[-1])
     leaf_mid = lax.all_gather(leaf_mid, "narrow", axis=1, tiled=True).reshape(wide_count * rows, -1)
 
-    picked = [
-        times_transposed(root_solution, landing[s]).astype(jnp.bfloat16) for s in range(sect_count)
-    ]
-    picked = jnp.stack(picked).reshape(sect_count, narrow_count, small, wide_count, border_block)
-    sent = picked.transpose(0, 3, 1, 2, 4).reshape(-1, small, border_block)
+    wanted = landing.reshape(sect_count * wide_count, border_block, root_block)
+    source = jnp.broadcast_to(root_solution[None], (sect_count * wide_count, rows, root_block))
+    picked = lax.dot_general(
+        source, wanted, (((2,), (2,)), ((0,), (0,))), preferred_element_type=jnp.float32
+    )
+    picked = lax.optimization_barrier(picked.astype(jnp.bfloat16))
+    sent = hold(picked, leaf_mid).reshape(-1, small, border_block)
     got = lax.all_to_all(sent, ("sect", "wide", "narrow"), 0, 0, tiled=True)
     got = got.reshape(sect_count, wide_count, narrow_count, small, border_block)
     own = jnp.sum(got.astype(jnp.float32), axis=(0, 2)).astype(jnp.bfloat16)

time: 364 us -> 312 us (0.86)
  waiting for transfers between devices: 191 us -> 125 us
  blocking collectives: 0 us -> 29 us
  starting transfers between devices: 81.9 us -> 61.4 us
    all_to_all x1 -> x0, waiting for transfers between devices: 38.5 us -> none  [body(): got = lax.all_to_all(sent, ('sect', 'wide', 'narrow'), 0, 0, tiled=True)]
    all_to_all x0 -> x1, blocking collectives: none -> 29 us  [body(): got = lax.all_to_all(sent, ('sect', 'wide', 'narrow'), 0, 0, tiled=True)]
    ppermute x47 -> x39, waiting for transfers between devices: 136 us -> 109 us  [swap(): return lax.ppermute(value, axis, pairs)]
    ppermute x47 -> x39, starting transfers between devices: 72.5 us -> 55 us  [swap(): return lax.ppermute(value, axis, pairs)]
    all_to_all x1, waiting for transfers between devices: 15.5 us -> 8.33 us  [body(): got = lax.all_to_all(sent, ('wide', 'narrow'), 0, 0, tiled=True)]
    dot_general x0 -> x1, matrix products: none -> 6.59 us  [body(): lax.dot_general(source, wanted, (((2,), (2,)), ((0,), (0,))), preferred_e...]
    all_gather x1, waiting for transfers between devices: 0.11 us -> 5.55 us  [body(): lax.all_gather(leaf_mid, 'narrow', axis=1, tiled=True)]
    slice x0 -> x6, local copies, waits for them, and re-layouts: none -> 4.37 us  [hold(): corner = lax.slice(other, (0,) * other.ndim, (1,) * other.ndim).reshape(())]
  transfers between devices with their start and end apart: 51 -> 42, of which waited for: 33 -> 24; matrix products, arithmetic and copies ran while one was open for 13% -> 19% of each run, Pallas kernels for 0% -> 0%
where the time goes in v2:
time: 312 us; the launch traced here: 311 us
  waiting for transfers between devices  125 us (40%)
  starting transfers between devices  61.4 us (20%)
  matrix products  52.7 us (17%)
  blocking collectives  29 us (9%)
  between operations  18.8 us (6%)
  other arithmetic  14.6 us (5%)
  local copies, waits for them, and re-layouts  10.1 us (3%)
    ppermute x39, waiting for transfers between devices, swap(): return lax.ppermute(value, axis, pairs)  109 us
    ppermute x39, starting transfers between devices, swap(): return lax.ppermute(value, axis, pairs)  55 us
    all_to_all x1, blocking collectives, body(): got = lax.all_to_all(sent, ('sect', 'wide', 'narrow'), 0, 0, tiled=True)  29 us
    dot_general x6, matrix products, times_transposed(): lax.dot_general(left, right, (((1,), (1,)), ((), ())), preferred_element_...  24.1 us
    dot_general x12, matrix products, times(): return jnp.dot(left, right, preferred_element_type=jnp.float32)  22 us
    all_to_all x1, waiting for transfers between devices, body(): got = lax.all_to_all(sent, ('wide', 'narrow'), 0, 0, tiled=True)  8.33 us
    eq x1, other arithmetic, body(): landing = (live_map[:, :, None] == columns).astype(jnp.bfloat16)  7.31 us
    dot_general x1, matrix products, body(): lax.dot_general(source, wanted, (((2,), (2,)), ((0,), (0,))), preferred_e...  6.59 us
  transfers between devices with their start and end apart: 42, of which 24 were waited for; matrix products, arithmetic and copies ran while one was open for 19% of the time, Pallas kernels for 0%

profile of v2, /device:TPU:0, one launch (start us, length us, event | category | flops | bytes accessed | tf_op | source)
XLA Modules:
  0.0 311.4 jit_solution(3378574985916271438)
XLA Ops:
  7.2 3.0 collective-permute-start
  11.2 5.5 %collective-permute-done = bf16[128,1024]{1,0:T(8,128)(2,1)S(1)} collective-permute-done((bf16[128,1024]{1,0:T(8,128)(2,1)}, bf16[128,1024]{1,0:T(8,128)(2,1)S(1)}, u32[]{:S(2)}, u32[]{:S(2)}) %collective-permute-start) | collective-permute-done | bytes 262176 | tf_op jit(solution)/shard_map/ppermute | solution.py:27
  19.7 2.3 convolution_convert_fusion.1
  23.1 6.2 %all-to-all-start = ((bf16[16,32,512]{2,1,0:T(8,128)(2,1)}), bf16[16,32,512]{2,1,0:T(8,128)(2,1)S(1)}, u32[]{:S(2)}, u32[]{:S(2)}) async-start(bf16[16,32,512]{2,1,0:T(8,128)(2,1)} %bitcast.4), calls=%async_computation | async-start | bytes 1048576 | tf_op jit(solution)/shard_map/all_to_all | solution.py:176
  29.3 7.3 %broadcast_compare_fusion = pred[2,2048,2048]{2,1,0:T(32,128)(4,1)} fusion(s32[2048]{0:T(1024)S(1)} %iota_add_fusion, s32[2,2048]{1,0:T(2,128)S(1)} %compare_select_fusion), kind=kLoop, calls=%fused_computation.4 | loop fusion | flops 8388608 | bytes 8413184 | tf_op jit(solution)/shard_map/eq | solution.py:153
  36.7 8.3 %all-to-all-done = bf16[16,32,512]{2,1,0:T(8,128)(2,1)S(1)} async-done(((bf16[16,32,512]{2,1,0:T(8,128)(2,1)}), bf16[16,32,512]{2,1,0:T(8,128)(2,1)S(1)}, u32[]{:S(2)}, u32[]{:S(2)}) %all-to-all-start) | async-done | bytes 524320 | tf_op jit(solution)/shard_map/all_to_all | solution.py:176
  45.2 1.4 collective-permute-start.3
  46.6 2.9 collective-permute-start.4
  49.8 2.1 collective-permute-done.2
  52.0 6.2 %collective-permute-done.3 = bf16[32,2048]{1,0:T(8,128)(2,1)S(1)} collective-permute-done((bf16[32,2048]{1,0:T(8,128)(2,1)S(1)}, bf16[32,2048]{1,0:T(8,128)(2,1)S(1)}, u32[]{:S(2)}, u32[]{:S(2)}) %collective-permute-start.3) | collective-permute-done | bytes 131104 | tf_op jit(solution)/shard_map/ppermute | solution.py:27
  58.2 1.6 collective-permute-start.5
  60.9 3.5 %fusion.78 = bf16[512,1024]{1,0:T(8,128)(2,1)} fusion(bf16[512,1024]{1,0:T(8,128)(2,1)} %copy-done.8, bf16[1024,1024]{1,0:T(8,128)(2,1)S(1)} %copy-done, bf16[]{:T(256)} %bitcast.11), kind=kOutput, calls=%fused_computation.55 | convolution fusion | flops 1074790400 | bytes 4194306 | tf_op jit(solution)/shard_map/dot_general | solution.py:10
  64.8 4.2 %collective-permute-done.5 = bf16[1,128,2048]{2,1,0:T(8,128)(2,1)S(1)} collective-permute-done((bf16[1,128,2048]{2,1,0:T(8,128)(2,1)S(1)}, bf16[1,128,2048]{2,1,0:T(8,128)(2,1)S(1)}, u32[]{:S(2)}, u32[]{:S(2)}) %collective-permute-start.5) | collective-permute-done | bytes 524320 | tf_op jit(solution)/shard_map/ppermute | solution.py:27
  69.1 4.9 %fusion.5 = f32[128,2048]{1,0:T(8,128)S(1)} fusion(pred[2,2048,2048]{2,1,0:T(32,128)(4,1)} %broadcast_compare_fusion, bf16[2,128,2048]{2,1,0:T(8,128)(2,1)S(1)} %constant_dynamic-update-slice_fusion), kind=kOutput, calls=%fused_computation.8 | convolution fusion | flops 1073741824 | bytes 5767168 | tf_op jit(solution)/shard_map/dot_general | solution.py:16
  74.0 3.2 %fusion.59 = bf16[128,2048]{1,0:T(8,128)(2,1)S(1)} fusion(f32[128,2048]{1,0:T(8,128)S(1)} %fusion.5, pred[2,2048,2048]{2,1,0:T(32,128)(4,1)S(1)} %bitcast.241, bf16[128,2048]{1,0:T(8,128)(2,1)S(1)} %copy-done.9, bf16[2,128,2048]{2,1,0:T(8,128)(2,1)S(1)} %constant_dynamic-update-slice_fusion), kind=kOutput, calls=%fused_computation.44 | convolution fusion | flops 1074790400 | bytes 6815744 | tf_op jit(solution)/shard_map/dot_general | solution.py:16
  77.2 1.6 collective-permute-start.6
  78.9 8.4 %collective-permute-done.6 = bf16[128,2048]{1,0:T(8,128)(2,1)S(1)} collective-permute-done((bf16[128,2048]{1,0:T(8,128)(2,1)S(1)}, bf16[128,2048]{1,0:T(8,128)(2,1)S(1)}, u32[]{:S(2)}, u32[]{:S(2)}) %collective-permute-start.6) | collective-permute-done | bytes 524320 | tf_op jit(solution)/shard_map/ppermute | solution.py:27
  88.1 2.3 reduce-scatter.2.cloned.1.call-done
  90.4 1.1 slice.187
  92.2 5.3 %fusion.72 = bf16[512,1024]{1,0:T(8,128)(2,1)S(1)} fusion(bf16[4096,2048]{1,0:T(8,128)(2,1)} %param.10, bf16[256,2048]{1,0:T(8,128)(2,1)} %collective-permute-done.7, bf16[128,2048]{1,0:T(8,128)(2,1)} %copy-done.5, bf16[128,2048]{1,0:T(8,128)(2,1)} %copy-done.3), kind=kOutput, calls=%fused_computation.52 | convolution fusion | flops 2154299392 | bytes 7340032 | tf_op jit(solution)/shard_map/dot_general | solution.py:10
  97.6 1.5 collective-permute-start.15
  99.1 5.5 %fusion.69 = bf16[512,1024]{1,0:T(8,128)(2,1)S(1)} fusion(bf16[4096,2048]{1,0:T(8,128)(2,1)} %param.10, bf16[256,2048]{1,0:T(8,128)(2,1)} %collective-permute-done.7, bf16[128,2048]{1,0:T(8,128)(2,1)S(1)} %copy-done.6, bf16[128,2048]{1,0:T(8,128)(2,1)S(1)} %copy-done.4), kind=kOutput, calls=%fused_computation.51 | convolution fusion | flops 2154299392 | bytes 7340032 | tf_op jit(solution)/shard_map/dot_general | solution.py:10
  104.7 4.7 %collective-permute-start.8 = (bf16[256,1024]{1,0:T(8,128)(2,1)S(1)}, bf16[256,1024]{1,0:T(8,128)(2,1)S(1)}, u32[]{:S(2)}, u32[]{:S(2)}) collective-permute-start(bf16[256,1024]{1,0:T(8,128)(2,1)S(1)} %add_bitcast_fusion.3), channel_id=1, source_target_pairs={{0,1},{1,0},{2,3},{3,2},{4,5},{5,4},{6,7},{7,6},{8,9},{9,8},{10,11... | collective-permute-start | bytes 1572872 | tf_op jit(solution)/shard_map/ppermute | solution.py:27
  109.4 3.6 %fusion.75 = bf16[512,1024]{1,0:T(8,128)(2,1)S(1)} fusion(bf16[4096,2048]{1,0:T(8,128)(2,1)S(1)} %bitcast.244, bf16[256,2048]{1,0:T(8,128)(2,1)} %collective-permute-done.7, bf16[128,2048]{1,0:T(8,128)(2,1)S(1)} %copy-done.6, bf16[128,2048]{1,0:T(8,128)(2,1)S(1)} %copy-done.4), kind=kOutput, calls=%fused_computation.53 | convolution fusion | flops 2154299392 | bytes 7340032 | tf_op jit(solution)/shard_map/dot_general | solution.py:10
  113.0 3.8 %fusion.66 = bf16[512,1024]{1,0:T(8,128)(2,1)S(1)} fusion(bf16[4096,2048]{1,0:T(8,128)(2,1)S(1)} %bitcast.244, bf16[256,2048]{1,0:T(8,128)(2,1)} %collective-permute-done.7, bf16[128,2048]{1,0:T(8,128)(2,1)S(1)} %copy-done.6, bf16[128,2048]{1,0:T(8,128)(2,1)S(1)} %copy-done.4), kind=kOutput, calls=%fused_computation.50 | convolution fusion | flops 2154299392 | bytes 7340032 | tf_op jit(solution)/shard_map/dot_general | solution.py:10
  117.2 4.9 %collective-permute-done.8 = bf16[256,1024]{1,0:T(8,128)(2,1)S(1)} collective-permute-done((bf16[256,1024]{1,0:T(8,128)(2,1)S(1)}, bf16[256,1024]{1,0:T(8,128)(2,1)S(1)}, u32[]{:S(2)}, u32[]{:S(2)}) %collective-permute-start.8) | collective-permute-done | bytes 524320 | tf_op jit(solution)/shard_map/ppermute | solution.py:27
  124.2 2.0 collective-permute-start.26
  126.8 2.1 collective-permute-start.9
  129.9 2.7 collective-permute-done.21
  132.7 2.9 collective-permute-start.22
  135.7 7.8 %collective-permute-done.17 = bf16[64,1024]{1,0:T(8,128)(2,1)S(1)} collective-permute-done((bf16[64,1024]{1,0:T(8,128)(2,1)S(1)}, bf16[64,1024]{1,0:T(8,128)(2,1)S(1)}, u32[]{:S(2)}, u32[]{:S(2)}) %collective-permute-start.17) | collective-permute-done | bytes 131104 | tf_op jit(solution)/shard_map/ppermute | solution.py:27
  143.5 3.5 %collective-permute-start.18 = (bf16[64,1024]{1,0:T(8,128)(2,1)S(1)}, bf16[64,1024]{1,0:T(8,128)(2,1)S(1)}, u32[]{:S(2)}, u32[]{:S(2)}) collective-permute-start(bf16[64,1024]{1,0:T(8,128)(2,1)S(1)} %get-tuple-element.3), channel_id=1, source_target_pairs={{0,2},{1,3},{2,0},{3,1},{4,6},{5,7},{6,4},{7,5},{8,10},{9,11},{10,... | collective-permute-start | bytes 393224 | tf_op jit(solution)/shard_map/ppermute | solution.py:27
  147.1 2.7 collective-permute-start.23
  151.4 3.0 collective-permute-start.19
  155.0 5.7 %collective-permute-done.27 = bf16[128,1024]{1,0:T(8,128)(2,1)S(1)} collective-permute-done((bf16[128,1024]{1,0:T(8,128)(2,1)S(1)}, bf16[128,1024]{1,0:T(8,128)(2,1)S(1)}, u32[]{:S(2)}, u32[]{:S(2)}) %collective-permute-start.27) | collective-permute-done | bytes 262176 | tf_op jit(solution)/shard_map/ppermute | solution.py:27
  160.8 2.0 collective-permute-start.28
  164.0 7.6 %collective-permute-done.19 = bf16[128,1024]{1,0:T(8,128)(2,1)S(1)} collective-permute-done((bf16[128,1024]{1,0:T(8,128)(2,1)S(1)}, bf16[128,1024]{1,0:T(8,128)(2,1)S(1)}, u32[]{:S(2)}, u32[]{:S(2)}) %collective-permute-start.19) | collective-permute-done | bytes 262176 | tf_op jit(solution)/shard_map/ppermute | solution.py:27
  172.3 2.6 collective-permute-start.29
  175.4 8.2 %collective-permute-done.29 = bf16[64,1024]{1,0:T(8,128)(2,1)S(1)} collective-permute-done((bf16[64,1024]{1,0:T(8,128)(2,1)S(1)}, bf16[64,1024]{1,0:T(8,128)(2,1)S(1)}, u32[]{:S(2)}, u32[]{:S(2)}) %collective-permute-start.29) | collective-permute-done | bytes 131104 | tf_op jit(solution)/shard_map/ppermute | solution.py:27
  183.6 3.4 %collective-permute-start.30 = (bf16[128,1024]{1,0:T(8,128)(2,1)S(1)}, bf16[128,1024]{1,0:T(8,128)(2,1)S(1)}, u32[]{:S(2)}, u32[]{:S(2)}) collective-permute-start(bf16[128,1024]{1,0:T(8,128)(2,1)S(1)} %bitcast.282), channel_id=1, source_target_pairs={{0,1},{1,0},{2,3},{3,2},{4,5},{5,4},{6,7},{7,6},{8,9},{9,8},{10,11... | collective-permute-start | bytes 786440 | tf_op jit(solution)/shard_map/ppermute | solution.py:27
  188.0 6.1 %collective-permute-done.30 = bf16[128,1024]{1,0:T(8,128)(2,1)S(1)} collective-permute-done((bf16[128,1024]{1,0:T(8,128)(2,1)S(1)}, bf16[128,1024]{1,0:T(8,128)(2,1)S(1)}, u32[]{:S(2)}, u32[]{:S(2)}) %collective-permute-start.30) | collective-permute-done | bytes 262176 | tf_op jit(solution)/shard_map/ppermute | solution.py:27
  194.7 1.4 collective-permute-done.13
  197.7 1.3 fusion.18
  198.9 4.5 %collective-permute-done.31 = bf16[256,1024]{1,0:T(8,128)(2,1)S(1)} collective-permute-done((bf16[256,1024]{1,0:T(8,128)(2,1)S(1)}, bf16[256,1024]{1,0:T(8,128)(2,1)S(1)}, u32[]{:S(2)}, u32[]{:S(2)}) %collective-permute-start.31) | collective-permute-done | bytes 524320 | tf_op jit(solution)/shard_map/ppermute | solution.py:27
  203.5 1.3 fusion.6
  204.8 1.3 fusion.42
  206.2 1.3 fusion.54
  207.5 1.3 fusion.20
  210.0 1.3 fusion.8
  211.2 1.6 fusion.45
  212.9 1.4 fusion.51
  215.1 1.4 collective-permute-start.33
  217.3 12.5 %collective-permute-done.33 = bf16[128,2048]{1,0:T(8,128)(2,1)} collective-permute-done((bf16[128,2048]{1,0:T(8,128)(2,1)}, bf16[128,2048]{1,0:T(8,128)(2,1)}, u32[]{:S(2)}, u32[]{:S(2)}) %collective-permute-start.33) | collective-permute-done | bytes 524320 | tf_op jit(solution)/shard_map/ppermute | solution.py:27
  229.7 1.2 add_convert_fusion
  231.7 6.6 %fusion.61 = bf16[8,128,512]{2,1,0:T(8,128)(2,1)S(1)} fusion(s32[2048]{0:T(1024)S(1)} %iota_add_fusion, s32[8,512]{1,0:T(8,128)S(1)} %eq.50, bf16[128,2048]{1,0:T(8,128)(2,1)S(1)} %add_convert_fusion), kind=kOutput, calls=%fused_computation.48 | convolution fusion | flops 2156396544 | bytes 1597440 | tf_op jit(solution)/shard_map/dot_general | solution.py:203
  238.3 5.6 %all-gather.2.cloned.1.call-done = bf16[4,128,1024]{2,1,0:T(8,128)(2,1)} async-done(((bf16[4,32,1024]{2,1,0:T(8,128)(2,1)}), bf16[4,128,1024]{2,1,0:T(8,128)(2,1)}) %all-gather.2.cloned.1.call-update) | async-done | bytes 1048592 | tf_op jit(solution)/shard_map/all_gather | solution.py:199
  243.9 1.2 slice.201
  245.7 29.0 %all_to_all.10 = bf16[32,32,512]{2,1,0:T(8,128)(2,1)S(1)} all-to-all(bf16[32,32,512]{2,1,0:T(8,128)(2,1)S(1)} %bitcast.242), channel_id=1, replica_groups=mesh['sect'=2,'wide'=4,'narrow'=4] {'sect','wide','narrow'}, dimensions={0} | all-to-all | bytes 2097152 | tf_op jit(solution)/shard_map/all_to_all | solution.py:208
  274.9 3.2 %collective-permute-start.34 = (bf16[4,32,512]{2,1,0:T(8,128)(2,1)S(1)}, bf16[4,32,512]{2,1,0:T(8,128)(2,1)S(1)}, u32[]{:S(2)}, u32[]{:S(2)}) collective-permute-start(bf16[4,32,512]{2,1,0:T(8,128)(2,1)S(1)} %pad_maximum_fusion.5), channel_id=1, source_target_pairs={{0,1},{1,0},{2,3},{3,2},{4,5},{5,4},{6,7},{7,6},{8,9},{9,8},{10,11... | collective-permute-start | bytes 393224 | tf_op jit(solution)/shard_map/ppermute | solution.py:27
  278.1 2.5 fusion.96
  281.3 1.8 collective-permute-start.36
  283.2 9.2 %collective-permute-done.35 = bf16[4,32,512]{2,1,0:T(8,128)(2,1)S(1)} collective-permute-done((bf16[4,32,512]{2,1,0:T(8,128)(2,1)S(1)}, bf16[4,32,512]{2,1,0:T(8,128)(2,1)S(1)}, u32[]{:S(2)}, u32[]{:S(2)}) %collective-permute-start.35) | collective-permute-done | bytes 131104 | tf_op jit(solution)/shard_map/ppermute | solution.py:27
  293.3 1.9 collective-permute-done.37
  296.2 7.6 %collective-permute-done.38 = bf16[128,1024]{1,0:T(8,128)(2,1)S(1)} collective-permute-done((bf16[128,1024]{1,0:T(8,128)(2,1)S(1)}, bf16[128,1024]{1,0:T(8,128)(2,1)S(1)}, u32[]{:S(2)}, u32[]{:S(2)}) %collective-permute-start.38) | collective-permute-done | bytes 262176 | tf_op jit(solution)/shard_map/ppermute | solution.py:27
  (179 shorter events, 24.6 us)
Async XLA Ops:
  7.2 53.7 %copy-start = (bf16[1024,1024]{1,0:T(8,128)(2,1)S(1)}, bf16[1024,1024]{1,0:T(8,128)(2,1)}, u32[]{:S(2)}) copy-start(bf16[1024,1024]{1,0:T(8,128)(2,1)} %param.8) | copy-start | bytes 6291460
  7.2 9.6 %collective-permute-start = (bf16[128,1024]{1,0:T(8,128)(2,1)}, bf16[128,1024]{1,0:T(8,128)(2,1)S(1)}, u32[]{:S(2)}, u32[]{:S(2)}) collective-permute-start(bf16[128,1024]{1,0:T(8,128)(2,1)} %param.7), channel_id=1, source_target_pairs={{0,8},{4,12},{8,0},{12,4},{1,9},{5,13},{9,1},{13,5},{2,10},{6,14},... | collective-permute-start | bytes 786440 | tf_op jit(solution)/shard_map/ppermute | solution.py:27
  17.7 2.0 collective-permute-start.1
  19.7 3.4 %copy-start.8 = (bf16[512,1024]{1,0:T(8,128)(2,1)}, bf16[512,1024]{1,0:T(8,128)(2,1)S(1)}, u32[]{:S(2)}) copy-start(bf16[512,1024]{1,0:T(8,128)(2,1)S(1)} %constant_dynamic-update-slice_fusion.3) | copy-start | bytes 3145732
  23.1 21.9 %all-to-all-start = ((bf16[16,32,512]{2,1,0:T(8,128)(2,1)}), bf16[16,32,512]{2,1,0:T(8,128)(2,1)S(1)}, u32[]{:S(2)}, u32[]{:S(2)}) async-start(bf16[16,32,512]{2,1,0:T(8,128)(2,1)} %bitcast.4), calls=%async_computation | async-start | bytes 1048576 | tf_op jit(solution)/shard_map/all_to_all | solution.py:176
  29.3 61.1 %reduce-scatter.2.cloned.1.call-start = ((), (), s32[]{:S(2)}) async-start(), calls=%async_computation.3 | async-start | bytes 1310720 | tf_op jit(solution)/shard_map/reduce_scatter | solution.py:185
  45.1 6.9 %collective-permute-start.2 = (bf16[32,2048]{1,0:T(8,128)(2,1)S(1)}, bf16[32,2048]{1,0:T(8,128)(2,1)S(1)}, u32[]{:S(2)}, u32[]{:S(2)}) collective-permute-start(bf16[32,2048]{1,0:T(8,128)(2,1)S(1)} %bitcast.294), channel_id=1, source_target_pairs={{0,1},{1,0},{2,3},{3,2},{4,5},{5,4},{6,7},{7,6},{8,9},{9,8},{10,11... | collective-permute-start | bytes 393224 | tf_op jit(solution)/shard_map/ppermute | solution.py:27
  45.2 13.0 %collective-permute-start.3 = (bf16[32,2048]{1,0:T(8,128)(2,1)S(1)}, bf16[32,2048]{1,0:T(8,128)(2,1)S(1)}, u32[]{:S(2)}, u32[]{:S(2)}) collective-permute-start(bf16[32,2048]{1,0:T(8,128)(2,1)S(1)} %bitcast.295), channel_id=1, source_target_pairs={{0,2},{1,3},{2,0},{3,1},{4,6},{5,7},{6,4},{7,5},{8,10},{9,11},{10,... | collective-permute-start | bytes 393224 | tf_op jit(solution)/shard_map/ppermute | solution.py:27
  46.6 11.6 %collective-permute-start.4 = (bf16[32,2048]{1,0:T(8,128)(2,1)S(1)}, bf16[32,2048]{1,0:T(8,128)(2,1)S(1)}, u32[]{:S(2)}, u32[]{:S(2)}) collective-permute-start(bf16[32,2048]{1,0:T(8,128)(2,1)S(1)} %bitcast.296), channel_id=1, source_target_pairs={{0,3},{1,2},{2,1},{3,0},{4,7},{5,6},{6,5},{7,4},{8,11},{9,10},{10,... | collective-permute-start | bytes 393224 | tf_op jit(solution)/shard_map/ppermute | solution.py:27
  58.2 10.8 %collective-permute-start.5 = (bf16[1,128,2048]{2,1,0:T(8,128)(2,1)S(1)}, bf16[1,128,2048]{2,1,0:T(8,128)(2,1)S(1)}, u32[]{:S(2)}, u32[]{:S(2)}) collective-permute-start(bf16[1,128,2048]{2,1,0:T(8,128)(2,1)S(1)} %bitcast.254), channel_id=1, source_target_pairs={{0,16},{16,0},{1,17},{17,1},{2,18},{18,2},{3,19},{19,3},{4,20},{20... | collective-permute-start | bytes 1572872 | tf_op jit(solution)/shard_map/ppermute | solution.py:27
  64.4 179.5 %all-gather.2.cloned.1.call-start = ((), (), s32[]{:S(2)}) async-start(), calls=%async_computation.4 | async-start | bytes 1310720 | tf_op jit(solution)/shard_map/all_gather | solution.py:199
  69.0 5.0 %slice-start = ((s8[8388608]{0:T(1024)(128)(4,1)}), s8[4194304]{0:T(1024)(128)(4,1)S(1)}, s32[]{:S(2)}) async-start(s8[8388608]{0:T(1024)(128)(4,1)} %bitcast.240), calls=%async_computation.5 | async-start | bytes 8388608
  69.1 4.9 %slice-start.1 = ((s8[8388608]{0:T(1024)(128)(4,1)}), s8[4194304]{0:T(1024)(128)(4,1)S(1)}, s32[]{:S(2)}) async-start(s8[8388608]{0:T(1024)(128)(4,1)} %bitcast.240), calls=%async_computation.6 | async-start | bytes 8388608
  69.1 4.9 %copy-start.9 = (bf16[128,2048]{1,0:T(8,128)(2,1)S(1)}, bf16[128,2048]{1,0:T(8,128)(2,1)}, u32[]{:S(2)}) copy-start(bf16[128,2048]{1,0:T(8,128)(2,1)} %param.11) | copy-start | bytes 1572868
  77.2 10.0 %copy-start.3 = (bf16[128,2048]{1,0:T(8,128)(2,1)}, bf16[128,2048]{1,0:T(8,128)(2,1)S(1)}, u32[]{:S(2)}) copy-start(bf16[128,2048]{1,0:T(8,128)(2,1)S(1)} %fusion.59) | copy-start | bytes 1572868
  77.2 10.0 %collective-permute-start.6 = (bf16[128,2048]{1,0:T(8,128)(2,1)S(1)}, bf16[128,2048]{1,0:T(8,128)(2,1)S(1)}, u32[]{:S(2)}, u32[]{:S(2)}) collective-permute-start(bf16[128,2048]{1,0:T(8,128)(2,1)S(1)} %fusion.59), channel_id=1, source_target_pairs={{0,8},{4,12},{8,0},{12,4},{1,9},{5,13},{9,1},{13,5},{2,10},{6,14},... | collective-permute-start | bytes 1572872 | tf_op jit(solution)/shard_map/ppermute | solution.py:27
  87.3 0.8 copy-start.5
  88.1 4.1 %collective-permute-start.7 = (bf16[256,2048]{1,0:T(8,128)(2,1)S(1)}, bf16[256,2048]{1,0:T(8,128)(2,1)}, u32[]{:S(2)}, u32[]{:S(2)}) collective-permute-start(bf16[256,2048]{1,0:T(8,128)(2,1)S(1)} %pad_maximum_fusion.1), channel_id=1, source_target_pairs={{0,4},{4,0},{8,12},{12,8},{1,5},{5,1},{9,13},{13,9},{2,6},{6,2},{1... | collective-permute-start | bytes 3145736 | tf_op jit(solution)/shard_map/ppermute | solution.py:27
  92.2 7.0 %copy-start.4 = (bf16[128,2048]{1,0:T(8,128)(2,1)S(1)}, bf16[128,2048]{1,0:T(8,128)(2,1)}, u32[]{:S(2)}) copy-start(bf16[128,2048]{1,0:T(8,128)(2,1)} %copy-done.3) | copy-start | bytes 1572868
  92.2 7.0 %copy-start.6 = (bf16[128,2048]{1,0:T(8,128)(2,1)S(1)}, bf16[128,2048]{1,0:T(8,128)(2,1)}, u32[]{:S(2)}) copy-start(bf16[128,2048]{1,0:T(8,128)(2,1)} %copy-done.5) | copy-start | bytes 1572868
  92.2 17.2 %slice-start.2 = ((s8[16777216]{0:T(1024)(128)(4,1)}), s8[4194304]{0:T(1024)(128)(4,1)S(1)}, s32[]{:S(2)}) async-start(s8[16777216]{0:T(1024)(128)(4,1)} %bitcast.243), calls=%async_computation.7 | async-start | bytes 8388608
  92.2 17.2 %slice-start.3 = ((s8[16777216]{0:T(1024)(128)(4,1)}), s8[4194304]{0:T(1024)(128)(4,1)S(1)}, s32[]{:S(2)}) async-start(s8[16777216]{0:T(1024)(128)(4,1)} %bitcast.243), calls=%async_computation.8 | async-start | bytes 8388608
  97.5 11.9 %slice-start.4 = ((s8[16777216]{0:T(1024)(128)(4,1)}), s8[4194304]{0:T(1024)(128)(4,1)S(1)}, s32[]{:S(2)}) async-start(s8[16777216]{0:T(1024)(128)(4,1)} %bitcast.243), calls=%async_computation.9 | async-start | bytes 8388608
  97.6 11.8 %slice-start.5 = ((s8[16777216]{0:T(1024)(128)(4,1)}), s8[4194304]{0:T(1024)(128)(4,1)S(1)}, s32[]{:S(2)}) async-start(s8[16777216]{0:T(1024)(128)(4,1)} %bitcast.243), calls=%async_computation.10 | async-start | bytes 8388608
  97.6 19.3 %collective-permute-start.15 = (bf16[256,1024]{1,0:T(8,128)(2,1)S(1)}, bf16[256,1024]{1,0:T(8,128)(2,1)S(1)}, u32[]{:S(2)}, u32[]{:S(2)}) collective-permute-start(bf16[256,1024]{1,0:T(8,128)(2,1)S(1)} %add_bitcast_fusion.1), channel_id=1, source_target_pairs={{0,16},{16,0},{1,17},{17,1},{2,18},{18,2},{3,19},{19,3},{4,20},{20... | collective-permute-start | bytes 1572872 | tf_op jit(solution)/shard_map/ppermute | solution.py:27
  104.7 17.4 %collective-permute-start.8 = (bf16[256,1024]{1,0:T(8,128)(2,1)S(1)}, bf16[256,1024]{1,0:T(8,128)(2,1)S(1)}, u32[]{:S(2)}, u32[]{:S(2)}) collective-permute-start(bf16[256,1024]{1,0:T(8,128)(2,1)S(1)} %add_bitcast_fusion.3), channel_id=1, source_target_pairs={{0,1},{1,0},{2,3},{3,2},{4,5},{5,4},{6,7},{7,6},{8,9},{9,8},{10,11... | collective-permute-start | bytes 1572872 | tf_op jit(solution)/shard_map/ppermute | solution.py:27
  117.1 11.8 %collective-permute-start.16 = (bf16[128,1024]{1,0:T(8,128)(2,1)S(1)}, bf16[128,1024]{1,0:T(8,128)(2,1)S(1)}, u32[]{:S(2)}, u32[]{:S(2)}) collective-permute-start(bf16[128,1024]{1,0:T(8,128)(2,1)S(1)} %dynamic-slice_bitcast_fusion.2), channel_id=1, source_target_pairs={{0,1},{1,0},{2,3},{3,2},{4,5},{5,4},{6,7},{7,6},{8,9},{9,8},{10,11... | collective-permute-start | bytes 786440 | tf_op jit(solution)/shard_map/ppermute | solution.py:27
  123.4 9.2 %collective-permute-start.21 = (bf16[128,1024]{1,0:T(8,128)(2,1)S(1)}, bf16[128,1024]{1,0:T(8,128)(2,1)S(1)}, u32[]{:S(2)}, u32[]{:S(2)}) collective-permute-start(bf16[128,1024]{1,0:T(8,128)(2,1)S(1)} %dynamic-slice_bitcast_fusion.1), channel_id=1, source_target_pairs={{0,16},{16,0},{1,17},{17,1},{2,18},{18,2},{3,19},{19,3},{4,20},{20... | collective-permute-start | bytes 786440 | tf_op jit(solution)/shard_map/ppermute | solution.py:27
  124.2 25.6 %collective-permute-start.26 = (bf16[256,1024]{1,0:T(8,128)(2,1)S(1)}, bf16[256,1024]{1,0:T(8,128)(2,1)S(1)}, u32[]{:S(2)}, u32[]{:S(2)}) collective-permute-start(bf16[256,1024]{1,0:T(8,128)(2,1)S(1)} %add_bitcast_fusion), channel_id=1, source_target_pairs={{0,16},{16,0},{1,17},{17,1},{2,18},{18,2},{3,19},{19,3},{4,20},{20... | collective-permute-start | bytes 1572872 | tf_op jit(solution)/shard_map/ppermute | solution.py:27
  126.8 23.5 %collective-permute-start.9 = (bf16[256,1024]{1,0:T(8,128)(2,1)S(1)}, bf16[256,1024]{1,0:T(8,128)(2,1)S(1)}, u32[]{:S(2)}, u32[]{:S(2)}) collective-permute-start(bf16[256,1024]{1,0:T(8,128)(2,1)S(1)} %add_bitcast_fusion.2), channel_id=1, source_target_pairs={{0,1},{1,0},{2,3},{3,2},{4,5},{5,4},{6,7},{7,6},{8,9},{9,8},{10,11... | collective-permute-start | bytes 1572872 | tf_op jit(solution)/shard_map/ppermute | solution.py:27
  129.0 14.4 %collective-permute-start.17 = (bf16[64,1024]{1,0:T(8,128)(2,1)S(1)}, bf16[64,1024]{1,0:T(8,128)(2,1)S(1)}, u32[]{:S(2)}, u32[]{:S(2)}) collective-permute-start(bf16[64,1024]{1,0:T(8,128)(2,1)S(1)} %dynamic-slice_bitcast_fusion.6), channel_id=1, source_target_pairs={{0,2},{1,3},{2,0},{3,1},{4,6},{5,7},{6,4},{7,5},{8,10},{9,11},{10,... | collective-permute-start | bytes 393224 | tf_op jit(solution)/shard_map/ppermute | solution.py:27
  132.7 14.3 %collective-permute-start.22 = (bf16[64,1024]{1,0:T(8,128)(2,1)S(1)}, bf16[64,1024]{1,0:T(8,128)(2,1)S(1)}, u32[]{:S(2)}, u32[]{:S(2)}) collective-permute-start(bf16[64,1024]{1,0:T(8,128)(2,1)S(1)} %dynamic-slice_bitcast_fusion.5), channel_id=1, source_target_pairs={{0,2},{1,3},{2,0},{3,1},{4,6},{5,7},{6,4},{7,5},{8,10},{9,11},{10,... | collective-permute-start | bytes 393224 | tf_op jit(solution)/shard_map/ppermute | solution.py:27
  143.5 7.9 %collective-permute-start.18 = (bf16[64,1024]{1,0:T(8,128)(2,1)S(1)}, bf16[64,1024]{1,0:T(8,128)(2,1)S(1)}, u32[]{:S(2)}, u32[]{:S(2)}) collective-permute-start(bf16[64,1024]{1,0:T(8,128)(2,1)S(1)} %get-tuple-element.3), channel_id=1, source_target_pairs={{0,2},{1,3},{2,0},{3,1},{4,6},{5,7},{6,4},{7,5},{8,10},{9,11},{10,... | collective-permute-start | bytes 393224 | tf_op jit(solution)/shard_map/ppermute | solution.py:27
  147.1 7.3 %collective-permute-start.23 = (bf16[64,1024]{1,0:T(8,128)(2,1)S(1)}, bf16[64,1024]{1,0:T(8,128)(2,1)S(1)}, u32[]{:S(2)}, u32[]{:S(2)}) collective-permute-start(bf16[64,1024]{1,0:T(8,128)(2,1)S(1)} %get-tuple-element.5), channel_id=1, source_target_pairs={{0,2},{1,3},{2,0},{3,1},{4,6},{5,7},{6,4},{7,5},{8,10},{9,11},{10,... | collective-permute-start | bytes 393224 | tf_op jit(solution)/shard_map/ppermute | solution.py:27
  150.0 10.7 %collective-permute-start.27 = (bf16[128,1024]{1,0:T(8,128)(2,1)S(1)}, bf16[128,1024]{1,0:T(8,128)(2,1)S(1)}, u32[]{:S(2)}, u32[]{:S(2)}) collective-permute-start(bf16[128,1024]{1,0:T(8,128)(2,1)S(1)} %dynamic-slice_bitcast_fusion), channel_id=1, source_target_pairs={{0,1},{1,0},{2,3},{3,2},{4,5},{5,4},{6,7},{7,6},{8,9},{9,8},{10,11... | collective-permute-start | bytes 786440 | tf_op jit(solution)/shard_map/ppermute | solution.py:27
  150.6 12.3 %collective-permute-start.10 = (bf16[128,1024]{1,0:T(8,128)(2,1)S(1)}, bf16[128,1024]{1,0:T(8,128)(2,1)S(1)}, u32[]{:S(2)}, u32[]{:S(2)}) collective-permute-start(bf16[128,1024]{1,0:T(8,128)(2,1)S(1)} %dynamic-slice_bitcast_fusion.3), channel_id=1, source_target_pairs={{0,16},{16,0},{1,17},{17,1},{2,18},{18,2},{3,19},{19,3},{4,20},{20... | collective-permute-start | bytes 786440 | tf_op jit(solution)/shard_map/ppermute | solution.py:27
  151.4 20.2 %collective-permute-start.19 = (bf16[128,1024]{1,0:T(8,128)(2,1)S(1)}, bf16[128,1024]{1,0:T(8,128)(2,1)S(1)}, u32[]{:S(2)}, u32[]{:S(2)}) collective-permute-start(bf16[128,1024]{1,0:T(8,128)(2,1)S(1)} %bitcast.278), channel_id=1, source_target_pairs={{0,1},{1,0},{2,3},{3,2},{4,5},{5,4},{6,7},{7,6},{8,9},{9,8},{10,11... | collective-permute-start | bytes 786440 | tf_op jit(solution)/shard_map/ppermute | solution.py:27
  154.5 17.2 %collective-permute-start.24 = (bf16[128,1024]{1,0:T(8,128)(2,1)S(1)}, bf16[128,1024]{1,0:T(8,128)(2,1)S(1)}, u32[]{:S(2)}, u32[]{:S(2)}) collective-permute-start(bf16[128,1024]{1,0:T(8,128)(2,1)S(1)} %bitcast.280), channel_id=1, source_target_pairs={{0,16},{16,0},{1,17},{17,1},{2,18},{18,2},{3,19},{19,3},{4,20},{20... | collective-permute-start | bytes 786440 | tf_op jit(solution)/shard_map/ppermute | solution.py:27
  160.8 11.4 %collective-permute-start.28 = (bf16[64,1024]{1,0:T(8,128)(2,1)S(1)}, bf16[64,1024]{1,0:T(8,128)(2,1)S(1)}, u32[]{:S(2)}, u32[]{:S(2)}) collective-permute-start(bf16[64,1024]{1,0:T(8,128)(2,1)S(1)} %dynamic-slice_bitcast_fusion.4), channel_id=1, source_target_pairs={{0,2},{1,3},{2,0},{3,1},{4,6},{5,7},{6,4},{7,5},{8,10},{9,11},{10,... | collective-permute-start | bytes 393224 | tf_op jit(solution)/shard_map/ppermute | solution.py:27
  163.0 11.9 %collective-permute-start.11 = (bf16[64,1024]{1,0:T(8,128)(2,1)S(1)}, bf16[64,1024]{1,0:T(8,128)(2,1)S(1)}, u32[]{:S(2)}, u32[]{:S(2)}) collective-permute-start(bf16[64,1024]{1,0:T(8,128)(2,1)S(1)} %dynamic-slice_bitcast_fusion.7), channel_id=1, source_target_pairs={{0,2},{1,3},{2,0},{3,1},{4,6},{5,7},{6,4},{7,5},{8,10},{9,11},{10,... | collective-permute-start | bytes 393224 | tf_op jit(solution)/shard_map/ppermute | solution.py:27
  171.6 25.7 %collective-permute-start.20 = (bf16[256,1024]{1,0:T(8,128)(2,1)S(1)}, bf16[256,1024]{1,0:T(8,128)(2,1)S(1)}, u32[]{:S(2)}, u32[]{:S(2)}) collective-permute-start(bf16[256,1024]{1,0:T(8,128)(2,1)S(1)} %bitcast.257), channel_id=1, source_target_pairs={{0,16},{16,0},{1,17},{17,1},{2,18},{18,2},{3,19},{19,3},{4,20},{20... | collective-permute-start | bytes 1572872 | tf_op jit(solution)/shard_map/ppermute | solution.py:27
  171.7 25.7 %collective-permute-start.25 = (bf16[256,1024]{1,0:T(8,128)(2,1)S(1)}, bf16[256,1024]{1,0:T(8,128)(2,1)S(1)}, u32[]{:S(2)}, u32[]{:S(2)}) collective-permute-start(bf16[256,1024]{1,0:T(8,128)(2,1)S(1)} %bitcast.259), channel_id=1, source_target_pairs={{0,1},{1,0},{2,3},{3,2},{4,5},{5,4},{6,7},{7,6},{8,9},{9,8},{10,11... | collective-permute-start | bytes 1572872 | tf_op jit(solution)/shard_map/ppermute | solution.py:27
  172.3 11.4 %collective-permute-start.29 = (bf16[64,1024]{1,0:T(8,128)(2,1)S(1)}, bf16[64,1024]{1,0:T(8,128)(2,1)S(1)}, u32[]{:S(2)}, u32[]{:S(2)}) collective-permute-start(bf16[64,1024]{1,0:T(8,128)(2,1)S(1)} %get-tuple-element.7), channel_id=1, source_target_pairs={{0,2},{1,3},{2,0},{3,1},{4,6},{5,7},{6,4},{7,5},{8,10},{9,11},{10,... | collective-permute-start | bytes 393224 | tf_op jit(solution)/shard_map/ppermute | solution.py:27
  174.9 12.2 %collective-permute-start.12 = (bf16[64,1024]{1,0:T(8,128)(2,1)S(1)}, bf16[64,1024]{1,0:T(8,128)(2,1)S(1)}, u32[]{:S(2)}, u32[]{:S(2)}) collective-permute-start(bf16[64,1024]{1,0:T(8,128)(2,1)S(1)} %get-tuple-element.9), channel_id=1, source_target_pairs={{0,2},{1,3},{2,0},{3,1},{4,6},{5,7},{6,4},{7,5},{8,10},{9,11},{10,... | collective-permute-start | bytes 393224 | tf_op jit(solution)/shard_map/ppermute | solution.py:27
  183.6 10.5 %collective-permute-start.30 = (bf16[128,1024]{1,0:T(8,128)(2,1)S(1)}, bf16[128,1024]{1,0:T(8,128)(2,1)S(1)}, u32[]{:S(2)}, u32[]{:S(2)}) collective-permute-start(bf16[128,1024]{1,0:T(8,128)(2,1)S(1)} %bitcast.282), channel_id=1, source_target_pairs={{0,1},{1,0},{2,3},{3,2},{4,5},{5,4},{6,7},{7,6},{8,9},{9,8},{10,11... | collective-permute-start | bytes 786440 | tf_op jit(solution)/shard_map/ppermute | solution.py:27
  187.1 9.1 %collective-permute-start.13 = (bf16[128,1024]{1,0:T(8,128)(2,1)S(1)}, bf16[128,1024]{1,0:T(8,128)(2,1)S(1)}, u32[]{:S(2)}, u32[]{:S(2)}) collective-permute-start(bf16[128,1024]{1,0:T(8,128)(2,1)S(1)} %bitcast.276), channel_id=1, source_target_pairs={{0,16},{16,0},{1,17},{17,1},{2,18},{18,2},{3,19},{19,3},{4,20},{20... | collective-permute-start | bytes 786440 | tf_op jit(solution)/shard_map/ppermute | solution.py:27
  194.2 9.2 %collective-permute-start.31 = (bf16[256,1024]{1,0:T(8,128)(2,1)S(1)}, bf16[256,1024]{1,0:T(8,128)(2,1)S(1)}, u32[]{:S(2)}, u32[]{:S(2)}) collective-permute-start(bf16[256,1024]{1,0:T(8,128)(2,1)S(1)} %bitcast.261), channel_id=1, source_target_pairs={{0,16},{16,0},{1,17},{17,1},{2,18},{18,2},{3,19},{19,3},{4,20},{20... | collective-permute-start | bytes 1572872 | tf_op jit(solution)/shard_map/ppermute | solution.py:27
  196.2 9.9 %collective-permute-start.14 = (bf16[256,1024]{1,0:T(8,128)(2,1)S(1)}, bf16[256,1024]{1,0:T(8,128)(2,1)S(1)}, u32[]{:S(2)}, u32[]{:S(2)}) collective-permute-start(bf16[256,1024]{1,0:T(8,128)(2,1)S(1)} %bitcast.263), channel_id=1, source_target_pairs={{0,1},{1,0},{2,3},{3,2},{4,5},{5,4},{6,7},{7,6},{8,9},{9,8},{10,11... | collective-permute-start | bytes 1572872 | tf_op jit(solution)/shard_map/ppermute | solution.py:27
  207.5 5.4 %collective-permute-start.32 = (bf16[256,2048]{1,0:T(8,128)(2,1)S(1)}, bf16[256,2048]{1,0:T(8,128)(2,1)S(1)}, u32[]{:S(2)}, u32[]{:S(2)}) collective-permute-start(bf16[256,2048]{1,0:T(8,128)(2,1)S(1)} %fusion.54), channel_id=1, source_target_pairs={{0,4},{4,0},{8,12},{12,8},{1,5},{5,1},{9,13},{13,9},{2,6},{6,2},{1... | collective-permute-start | bytes 3145736 | tf_op jit(solution)/shard_map/ppermute | solution.py:27
  212.8 3.6 %copy-start.7 = (bf16[4,32,1024]{2,1,0:T(8,128)(2,1)S(1)}, bf16[4,32,1024]{2,1,0:T(8,128)(2,1)}, u32[]{:S(2)}) copy-start(bf16[4,32,1024]{2,1,0:T(8,128)(2,1)} %reduce-scatter.2.cloned.1.call-done) | copy-start | bytes 786436
  215.1 14.6 %collective-permute-start.33 = (bf16[128,2048]{1,0:T(8,128)(2,1)}, bf16[128,2048]{1,0:T(8,128)(2,1)}, u32[]{:S(2)}, u32[]{:S(2)}) collective-permute-start(bf16[128,2048]{1,0:T(8,128)(2,1)} %slice.200), channel_id=1, source_target_pairs={{0,8},{4,12},{8,0},{12,4},{1,9},{5,13},{9,1},{13,5},{2,10},{6,14},... | collective-permute-start | bytes 1572872 | tf_op jit(solution)/shard_map/ppermute | solution.py:27
  230.9 0.8 copy-start.2
  274.9 17.5 %copy-start.1 = (bf16[512,1024]{1,0:T(8,128)(2,1)S(1)}, bf16[512,1024]{1,0:T(8,128)(2,1)}, u32[]{:S(2)}) copy-start(bf16[512,1024]{1,0:T(8,128)(2,1)} %param.9) | copy-start | bytes 3145732
  274.9 8.2 %collective-permute-start.34 = (bf16[4,32,512]{2,1,0:T(8,128)(2,1)S(1)}, bf16[4,32,512]{2,1,0:T(8,128)(2,1)S(1)}, u32[]{:S(2)}, u32[]{:S(2)}) collective-permute-start(bf16[4,32,512]{2,1,0:T(8,128)(2,1)S(1)} %pad_maximum_fusion.5), channel_id=1, source_target_pairs={{0,1},{1,0},{2,3},{3,2},{4,5},{5,4},{6,7},{7,6},{8,9},{9,8},{10,11... | collective-permute-start | bytes 393224 | tf_op jit(solution)/shard_map/ppermute | solution.py:27
  280.5 11.8 %collective-permute-start.35 = (bf16[4,32,512]{2,1,0:T(8,128)(2,1)S(1)}, bf16[4,32,512]{2,1,0:T(8,128)(2,1)S(1)}, u32[]{:S(2)}, u32[]{:S(2)}) collective-permute-start(bf16[4,32,512]{2,1,0:T(8,128)(2,1)S(1)} %pad_maximum_fusion.5), channel_id=1, source_target_pairs={{0,2},{1,3},{2,0},{3,1},{4,6},{5,7},{6,4},{7,5},{8,10},{9,11},{10,... | collective-permute-start | bytes 393224 | tf_op jit(solution)/shard_map/ppermute | solution.py:27
  281.3 11.1 %collective-permute-start.36 = (bf16[4,32,512]{2,1,0:T(8,128)(2,1)S(1)}, bf16[4,32,512]{2,1,0:T(8,128)(2,1)S(1)}, u32[]{:S(2)}, u32[]{:S(2)}) collective-permute-start(bf16[4,32,512]{2,1,0:T(8,128)(2,1)S(1)} %pad_maximum_fusion.5), channel_id=1, source_target_pairs={{0,3},{1,2},{2,1},{3,0},{4,7},{5,6},{6,5},{7,4},{8,11},{9,10},{10,... | collective-permute-start | bytes 393224 | tf_op jit(solution)/shard_map/ppermute | solution.py:27
  293.2 2.0 collective-permute-start.37
  295.4 8.4 %collective-permute-start.38 = (bf16[128,1024]{1,0:T(8,128)(2,1)S(1)}, bf16[128,1024]{1,0:T(8,128)(2,1)S(1)}, u32[]{:S(2)}, u32[]{:S(2)}) collective-permute-start(bf16[128,1024]{1,0:T(8,128)(2,1)S(1)} %slice.205), channel_id=1, source_target_pairs={{0,8},{4,12},{8,0},{12,4},{1,9},{5,13},{9,1},{13,5},{2,10},{6,14},... | collective-permute-start | bytes 786440 | tf_op jit(solution)/shard_map/ppermute | solution.py:27
Sparse Core Ops, SparseCore 0:
  64.5 25.8 reduce-scatter.1
  217.3 26.4 all-gather.1

commit v3 on v2

--- a/solution.py
+++ b/solution.py
@@ -16,9 +16,9 @@
     return jnp.dot(left, right, preferred_element_type=jnp.float32)
 
 
-def hold(value, other):
-    corner = lax.slice(other, (0,) * other.ndim, (1,) * other.ndim).reshape(())
-    zero = lax.clamp(jnp.int32(0), corner.astype(jnp.int32), jnp.int32(0))
+def hold(value, *others):
+    corners = [lax.slice(o, (0,) * o.ndim, (1,) * o.ndim).reshape(()) for o in others]
+    zero = lax.clamp(jnp.int32(0), sum(c.astype(jnp.int32) for c in corners), jnp.int32(0))
     return value + zero.astype(value.dtype)
 
 
@@ -80,12 +80,12 @@
     return result.reshape(value.shape[:dim] + (count * value.shape[dim],) + value.shape[dim + 1 :])
 
 
-def halve(value, axis, distance, other=None):
+def halve(value, axis, distance, others=()):
     bit = (lax.axis_index(axis) // distance) % 2
     halves = value.reshape((2, value.shape[0] // 2) + value.shape[1:])
     kept, given = (lax.dynamic_index_in_dim(halves, k, 0, keepdims=False) for k in (bit, 1 - bit))
-    if other is not None:
-        given = hold(given, other)
+    if others:
+        given = hold(given, *others)
     return total([kept, swap(given, axis, distance)])
 
 
@@ -101,8 +101,8 @@
     return [(axis, 1 << k) for k in range(lax.axis_size(axis).bit_length() - 1)]
 
 
-def sum_all(value, order, other):
-    first = value = halve(value, *order[0], other)
+def sum_all(value, order, others):
+    first = value = halve(value, *order[0], others)
     for axis, distance in order[1:]:
         value = halve(value, axis, distance)
     for axis, distance in reversed(order):
@@ -119,8 +119,8 @@
     middles, firsts = [], []
     for c in range(CHUNKS):
         product = times_transposed(right, blocks[c]).astype(jnp.bfloat16)
-        other = firsts[c - len(orders)] if c >= len(orders) else beside
-        middle, first = sum_all(product, orders[c % len(orders)], other)
+        others = [firsts[c - len(orders)]] if c >= len(orders) else ([beside] if c == 1 else [])
+        middle, first = sum_all(product, orders[c % len(orders)], others)
         middles.append(middle)
         firsts.append(first)
     backs = []
@@ -150,7 +150,10 @@
     columns = lax.broadcasted_iota(jnp.int32, (1, 1, root_block), 2) + root_start
     border_place = lax.broadcasted_iota(jnp.int32, border_map.shape, 1)
     live_map = jnp.where(border_place < border_rows[:, None], border_map, -1)
-    landing = (live_map[:, :, None] == columns).astype(jnp.bfloat16)
+    near_map = jnp.stack(
+        [lax.dynamic_index_in_dim(live_map, sect_index ^ r, 0, keepdims=False) for r in range(sect_count)]
+    )
+    landing = (near_map[:, :, None] == columns).astype(jnp.bfloat16)
 
     piece = relative_gather(leaf_rhs, "wide")
     places = relative_places("wide")
@@ -179,35 +182,38 @@
     )
     border_out = border_sum.transpose(1, 0, 2).reshape(small, border_total).astype(jnp.bfloat16)
 
-    updates = direct_gather(border_out, "narrow")
+    updates = direct_gather(hold(border_out, landing), "narrow")
     pivot_terms = times_transposed(piece, leaf_factor).astype(jnp.bfloat16)
-    pivot_terms = hold(pivot_terms.reshape(wide_count, rows, -1), updates)
+    pivot_terms = pivot_terms.reshape(wide_count, rows, -1)
+    passed = hold(updates, pivot_terms)
     leaf_mid = lax.psum_scatter(pivot_terms, "narrow", scatter_dimension=1, tiled=True)
-    updates = direct_gather(updates[None], "sect")
-    landed = jnp.zeros((rows, root_block), jnp.float32)
-    for s in range(sect_count):
-        landed = landed + times(updates[s], landing[s])
+    others = [swap(passed, "sect", r) for r in range(1, sect_count)]
+    landed = times(jnp.concatenate([updates] + others, axis=1), landing.reshape(-1, root_block))
     root_right = (root_rhs.astype(jnp.float32) - landed).astype(jnp.bfloat16)
     right = relative_gather(root_right, "wide", 2)
     right = jnp.concatenate([right, swap(right, "wide", 1)], axis=0)
 
     (given, kept), late = root_solve(right, root_factor, leaf_mid)
-    kept = total([kept, swap(given.astype(jnp.bfloat16), "wide", 1)])
+    given = swap(given.astype(jnp.bfloat16), "wide", 1)
+    leaf_mid = hold(leaf_mid, given)
+    kept = total([kept, given])
     root_solution = relative_scatter(kept, "wide", 2)
 
-    leaf_mid = hold(leaf_mid, late[-1])
     leaf_mid = lax.all_gather(leaf_mid, "narrow", axis=1, tiled=True).reshape(wide_count * rows, -1)
 
-    wanted = landing.reshape(sect_count * wide_count, border_block, root_block)
-    source = jnp.broadcast_to(root_solution[None], (sect_count * wide_count, rows, root_block))
-    picked = lax.dot_general(
-        source, wanted, (((2,), (2,)), ((0,), (0,))), preferred_element_type=jnp.float32
-    )
-    picked = lax.optimization_barrier(picked.astype(jnp.bfloat16))
-    sent = hold(picked, leaf_mid).reshape(-1, small, border_block)
-    got = lax.all_to_all(sent, ("sect", "wide", "narrow"), 0, 0, tiled=True)
-    got = got.reshape(sect_count, wide_count, narrow_count, small, border_block)
-    own = jnp.sum(got.astype(jnp.float32), axis=(0, 2)).astype(jnp.bfloat16)
+    source = jnp.broadcast_to(root_solution[None], (wide_count, rows, root_block))
+    picked = []
+    for r in reversed(range(sect_count)):
+        wanted = landing[r].reshape(wide_count, border_block, root_block)
+        part = lax.dot_general(
+            source, wanted, (((2,), (2,)), ((0,), (0,))), preferred_element_type=jnp.float32
+        ).astype(jnp.bfloat16)
+        part = lax.optimization_barrier(part)
+        picked.append(swap(part, "sect", r) if r else part)
+    sent = hold(total(picked), leaf_mid).reshape(-1, small, border_block)
+    got = lax.all_to_all(sent, ("wide", "narrow"), 0, 0, tiled=True)
+    got = got.reshape(wide_count, narrow_count, small, border_block)
+    own = jnp.sum(got.astype(jnp.float32), axis=1).astype(jnp.bfloat16)
     returned = direct_gather(by_relation(own), "narrow", 1).reshape(wide_count * rows, border_block)
 
     back_leaf = times(leaf_mid, leaf_factor) - times(returned, leaf_coupling)

time: 312 us -> 307 us (0.984); the launches traced: 311 us -> 303 us
  blocking collectives: 29 us -> 19.9 us
  local copies, waits for them, and re-layouts: 10.1 us -> 16.8 us
  waiting for transfers between devices: 125 us -> 120 us
    all_to_all x1, blocking collectives: 29 us -> 19.9 us  [body(): got = lax.all_to_all(sent, ('wide', 'narrow'), 0, 0, tiled=True)]
    slice x6 -> x8, local copies, waits for them, and re-layouts: 4.37 us -> 12 us  [the longest x7 6.22 us: hold(): lax.slice(o, (0,) * o.ndim, (1,) * o.ndim).reshape(())]
    all_to_all x1, waiting for transfers between devices: 8.33 us -> 1.27 us  [body(): got = lax.all_to_all(sent, ('wide', 'narrow'), 0, 0, tiled=True)]
    ppermute x39 -> x40, waiting for transfers between devices: 109 us -> 112 us  [swap(): return lax.ppermute(value, axis, pairs)]
    ppermute x39 -> x40, starting transfers between devices: 55 us -> 53 us  [swap(): return lax.ppermute(value, axis, pairs)]
    dot_general x12 -> x11, matrix products: 22 us -> 21.3 us  [times(): return jnp.dot(left, right, preferred_element_type=jnp.float32)]
    dot_general x1 -> x2, matrix products: 6.59 us -> 6.65 us  [body(): lax.dot_general(source, wanted, (((2,), (2,)), ((0,), (0,))), preferred_e...]
  transfers between devices with their start and end apart: 42 -> 43, of which waited for: 24 -> 24; matrix products, arithmetic and copies ran while one was open for 19% -> 22% of each run, Pallas kernels for 0% -> 0%
where the time goes in v3:
time: 307 us; the launch traced here: 303 us
  waiting for transfers between devices  120 us (39%)
  starting transfers between devices  59.5 us (19%)
  matrix products  52.1 us (17%)
  blocking collectives  19.9 us (6%)
  between operations  19.8 us (6%)
  local copies, waits for them, and re-layouts  16.8 us (5%)
  other arithmetic  14.7 us (5%)
    ppermute x40, waiting for transfers between devices, swap(): return lax.ppermute(value, axis, pairs)  112 us
    ppermute x40, starting transfers between devices, swap(): return lax.ppermute(value, axis, pairs)  53 us
    dot_general x6, matrix products, times_transposed(): lax.dot_general(left, right, (((1,), (1,)), ((), ())), preferred_element_...  24.2 us
    dot_general x11, matrix products, times(): return jnp.dot(left, right, preferred_element_type=jnp.float32)  21.3 us
    all_to_all x1, blocking collectives, body(): got = lax.all_to_all(sent, ('wide', 'narrow'), 0, 0, tiled=True)  19.9 us
    eq x1, other arithmetic, body(): landing = (near_map[:, :, None] == columns).astype(jnp.bfloat16)  7.31 us
    all_gather x1, waiting for transfers between devices, body(): lax.all_gather(leaf_mid, 'narrow', axis=1, tiled=True)  6.95 us
    dot_general x2, matrix products, body(): lax.dot_general(source, wanted, (((2,), (2,)), ((0,), (0,))), preferred_e...  6.65 us
  transfers between devices with their start and end apart: 43, of which 24 were waited for; matrix products, arithmetic and copies ran while one was open for 22% of the time, Pallas kernels for 0%

profile of v3, /device:TPU:0, one launch (start us, length us, event | category | flops | bytes accessed | tf_op | source)
XLA Modules:
  0.0 303.0 jit_solution(14767427212353657392)
XLA Ops:
  7.2 3.0 %collective-permute-start = (bf16[128,1024]{1,0:T(8,128)(2,1)}, bf16[128,1024]{1,0:T(8,128)(2,1)S(1)}, u32[]{:S(2)}, u32[]{:S(2)}) collective-permute-start(bf16[128,1024]{1,0:T(8,128)(2,1)} %param.7), channel_id=1, source_target_pairs={{0,8},{4,12},{8,0},{12,4},{1,9},{5,13},{9,1},{13,5},{2,10},{6,14},... | collective-permute-start | bytes 786440 | tf_op jit(solution)/shard_map/ppermute | solution.py:27
  12.0 4.7 %collective-permute-done = bf16[128,1024]{1,0:T(8,128)(2,1)S(1)} collective-permute-done((bf16[128,1024]{1,0:T(8,128)(2,1)}, bf16[128,1024]{1,0:T(8,128)(2,1)S(1)}, u32[]{:S(2)}, u32[]{:S(2)}) %collective-permute-start) | collective-permute-done | bytes 262176 | tf_op jit(solution)/shard_map/ppermute | solution.py:27
  17.9 1.8 collective-permute-done.1
  19.7 2.3 convolution_convert_fusion.3
  23.1 6.2 %all-to-all-start = ((bf16[16,32,512]{2,1,0:T(8,128)(2,1)}), bf16[16,32,512]{2,1,0:T(8,128)(2,1)S(1)}, u32[]{:S(2)}, u32[]{:S(2)}) async-start(bf16[16,32,512]{2,1,0:T(8,128)(2,1)} %bitcast.5), calls=%async_computation.1 | async-start | bytes 1048576 | tf_op jit(solution)/shard_map/all_to_all | solution.py:179
  29.3 7.3 %broadcast_compare_fusion = pred[2,2048,2048]{2,1,0:T(8,128)(4,1)} fusion(s32[2048]{0:T(1024)S(1)} %iota_add_fusion, s32[2,2048]{1,0:T(2,128)S(1)} %get-tuple-element.26), kind=kLoop, calls=%fused_computation.3 | loop fusion | flops 8388608 | bytes 8413184 | tf_op jit(solution)/shard_map/eq | solution.py:156
  38.4 3.5 %convolution_convert_fusion = bf16[512,1024]{1,0:T(8,128)(2,1)} fusion(bf16[512,1024]{1,0:T(8,128)(2,1)} %copy-done.8, bf16[1024,1024]{1,0:T(8,128)(2,1)S(1)} %copy-done), kind=kOutput, calls=%fused_computation.42 | convolution fusion | flops 1074266112 | bytes 4194304 | tf_op jit(solution)/shard_map/dot_general | solution.py:10
  43.7 1.3 all-to-all-done
  45.8 2.4 collective-permute-start.3
  48.2 1.4 collective-permute-start.4
  49.8 2.5 collective-permute-done.2
  52.4 6.4 %collective-permute-done.3 = bf16[32,2048]{1,0:T(8,128)(2,1)S(1)} collective-permute-done((bf16[32,2048]{1,0:T(8,128)(2,1)S(1)}, bf16[32,2048]{1,0:T(8,128)(2,1)S(1)}, u32[]{:S(2)}, u32[]{:S(2)}) %collective-permute-start.3) | collective-permute-done | bytes 131104 | tf_op jit(solution)/shard_map/ppermute | solution.py:27
  58.9 1.6 collective-permute-start.5
  60.7 10.1 %collective-permute-done.5 = bf16[128,2048]{1,0:T(8,128)(2,1)} collective-permute-done((bf16[128,2048]{1,0:T(8,128)(2,1)S(1)}, bf16[128,2048]{1,0:T(8,128)(2,1)}, u32[]{:S(2)}, u32[]{:S(2)}) %collective-permute-start.5) | collective-permute-done | bytes 524320 | tf_op jit(solution)/shard_map/ppermute | solution.py:27
  70.8 7.3 %fusion.58 = bf16[128,2048]{1,0:T(8,128)(2,1)S(1)} fusion(s32[2048]{0:T(1024)S(1)} %iota_add_fusion, s32[4096]{0:T(1024)S(1)} %bitcast.282, bf16[128,2048]{1,0:T(8,128)(2,1)} %collective-permute-done.5, bf16[128,2048]{1,0:T(8,128)(2,1)S(1)} %bitcast.243, bf16[128,2048]{1,0:T(8,128)(2,1)} %param.11), kind=kOutput, calls=%fused_computation.39 | convolution fusion | flops 2158755840 | bytes 2121728 | tf_op jit(solution)/shard_map/dot_general | solution.py:16
  78.1 1.5 collective-permute-start.6
  79.6 9.4 %collective-permute-done.6 = bf16[128,2048]{1,0:T(8,128)(2,1)S(1)} collective-permute-done((bf16[128,2048]{1,0:T(8,128)(2,1)S(1)}, bf16[128,2048]{1,0:T(8,128)(2,1)S(1)}, u32[]{:S(2)}, u32[]{:S(2)}) %collective-permute-start.6) | collective-permute-done | bytes 524320 | tf_op jit(solution)/shard_map/ppermute | solution.py:27
  92.6 5.3 %fusion.61 = bf16[512,1024]{1,0:T(8,128)(2,1)S(1)} fusion(bf16[4096,2048]{1,0:T(8,128)(2,1)} %param.10, bf16[256,2048]{1,0:T(8,128)(2,1)} %collective-permute-done.7, bf16[128,2048]{1,0:T(8,128)(2,1)} %copy-done.5, bf16[128,2048]{1,0:T(8,128)(2,1)} %copy-done.3), kind=kOutput, calls=%fused_computation.43 | convolution fusion | flops 2154299392 | bytes 7340032 | tf_op jit(solution)/shard_map/dot_general | solution.py:10
  98.0 1.6 collective-permute-start.8
  99.6 5.6 %fusion.64 = bf16[512,1024]{1,0:T(8,128)(2,1)S(1)} fusion(bf16[4096,2048]{1,0:T(8,128)(2,1)} %param.10, bf16[256,2048]{1,0:T(8,128)(2,1)} %collective-permute-done.7, bf16[128,2048]{1,0:T(8,128)(2,1)S(1)} %copy-done.6, bf16[128,2048]{1,0:T(8,128)(2,1)S(1)} %copy-done.4), kind=kOutput, calls=%fused_computation.44 | convolution fusion | flops 2154299392 | bytes 7340032 | tf_op jit(solution)/shard_map/dot_general | solution.py:10
  105.2 4.5 %collective-permute-start.14 = (bf16[256,1024]{1,0:T(8,128)(2,1)S(1)}, bf16[256,1024]{1,0:T(8,128)(2,1)S(1)}, u32[]{:S(2)}, u32[]{:S(2)}) collective-permute-start(bf16[256,1024]{1,0:T(8,128)(2,1)S(1)} %add_bitcast_fusion.2), channel_id=1, source_target_pairs={{0,1},{1,0},{2,3},{3,2},{4,5},{5,4},{6,7},{7,6},{8,9},{9,8},{10,11... | collective-permute-start | bytes 1572872 | tf_op jit(solution)/shard_map/ppermute | solution.py:27
  109.8 3.6 %fusion.67 = bf16[512,1024]{1,0:T(8,128)(2,1)S(1)} fusion(bf16[4096,2048]{1,0:T(8,128)(2,1)S(1)} %bitcast.231, bf16[256,2048]{1,0:T(8,128)(2,1)} %collective-permute-done.7, bf16[128,2048]{1,0:T(8,128)(2,1)S(1)} %copy-done.6, bf16[128,2048]{1,0:T(8,128)(2,1)S(1)} %copy-done.4), kind=kOutput, calls=%fused_computation.45 | convolution fusion | flops 2154299392 | bytes 7340032 | tf_op jit(solution)/shard_map/dot_general | solution.py:10
  113.4 3.8 %fusion.70 = bf16[512,1024]{1,0:T(8,128)(2,1)S(1)} fusion(bf16[4096,2048]{1,0:T(8,128)(2,1)S(1)} %bitcast.231, bf16[256,2048]{1,0:T(8,128)(2,1)} %collective-permute-done.7, bf16[128,2048]{1,0:T(8,128)(2,1)S(1)} %copy-done.6, bf16[128,2048]{1,0:T(8,128)(2,1)S(1)} %copy-done.4), kind=kOutput, calls=%fused_computation.46 | convolution fusion | flops 2154299392 | bytes 7340032 | tf_op jit(solution)/shard_map/dot_general | solution.py:10
  117.6 4.9 %collective-permute-done.14 = bf16[256,1024]{1,0:T(8,128)(2,1)S(1)} collective-permute-done((bf16[256,1024]{1,0:T(8,128)(2,1)S(1)}, bf16[256,1024]{1,0:T(8,128)(2,1)S(1)}, u32[]{:S(2)}, u32[]{:S(2)}) %collective-permute-start.14) | collective-permute-done | bytes 524320 | tf_op jit(solution)/shard_map/ppermute | solution.py:27
  124.6 2.0 collective-permute-start.20
  127.2 2.1 collective-permute-start.26
  130.4 2.7 collective-permute-done.15
  133.2 3.0 collective-permute-start.16
  136.2 7.7 %collective-permute-done.10 = bf16[64,1024]{1,0:T(8,128)(2,1)S(1)} collective-permute-done((bf16[64,1024]{1,0:T(8,128)(2,1)S(1)}, bf16[64,1024]{1,0:T(8,128)(2,1)S(1)}, u32[]{:S(2)}, u32[]{:S(2)}) %collective-permute-start.10) | collective-permute-done | bytes 131104 | tf_op jit(solution)/shard_map/ppermute | solution.py:27
  143.9 3.5 %collective-permute-start.11 = (bf16[64,1024]{1,0:T(8,128)(2,1)S(1)}, bf16[64,1024]{1,0:T(8,128)(2,1)S(1)}, u32[]{:S(2)}, u32[]{:S(2)}) collective-permute-start(bf16[64,1024]{1,0:T(8,128)(2,1)S(1)} %get-tuple-element.5), channel_id=1, source_target_pairs={{0,2},{1,3},{2,0},{3,1},{4,6},{5,7},{6,4},{7,5},{8,10},{9,11},{10,... | collective-permute-start | bytes 393224 | tf_op jit(solution)/shard_map/ppermute | solution.py:27
  147.5 2.7 collective-permute-start.17
  152.1 2.8 collective-permute-start.12
  155.8 5.5 %collective-permute-done.21 = bf16[128,1024]{1,0:T(8,128)(2,1)S(1)} collective-permute-done((bf16[128,1024]{1,0:T(8,128)(2,1)S(1)}, bf16[128,1024]{1,0:T(8,128)(2,1)S(1)}, u32[]{:S(2)}, u32[]{:S(2)}) %collective-permute-start.21) | collective-permute-done | bytes 262176 | tf_op jit(solution)/shard_map/ppermute | solution.py:27
  161.4 2.0 collective-permute-start.22
  164.5 7.0 %collective-permute-done.12 = bf16[128,1024]{1,0:T(8,128)(2,1)S(1)} collective-permute-done((bf16[128,1024]{1,0:T(8,128)(2,1)S(1)}, bf16[128,1024]{1,0:T(8,128)(2,1)S(1)}, u32[]{:S(2)}, u32[]{:S(2)}) %collective-permute-start.12) | collective-permute-done | bytes 262176 | tf_op jit(solution)/shard_map/ppermute | solution.py:27
  172.2 2.6 collective-permute-start.23
  175.3 8.8 %collective-permute-done.23 = bf16[64,1024]{1,0:T(8,128)(2,1)S(1)} collective-permute-done((bf16[64,1024]{1,0:T(8,128)(2,1)S(1)}, bf16[64,1024]{1,0:T(8,128)(2,1)S(1)}, u32[]{:S(2)}, u32[]{:S(2)}) %collective-permute-start.23) | collective-permute-done | bytes 131104 | tf_op jit(solution)/shard_map/ppermute | solution.py:27
  184.1 3.4 %collective-permute-start.24 = (bf16[128,1024]{1,0:T(8,128)(2,1)S(1)}, bf16[128,1024]{1,0:T(8,128)(2,1)S(1)}, u32[]{:S(2)}, u32[]{:S(2)}) collective-permute-start(bf16[128,1024]{1,0:T(8,128)(2,1)S(1)} %bitcast.265), channel_id=1, source_target_pairs={{0,1},{1,0},{2,3},{3,2},{4,5},{5,4},{6,7},{7,6},{8,9},{9,8},{10,11... | collective-permute-start | bytes 786440 | tf_op jit(solution)/shard_map/ppermute | solution.py:27
  188.1 6.6 %collective-permute-done.24 = bf16[128,1024]{1,0:T(8,128)(2,1)S(1)} collective-permute-done((bf16[128,1024]{1,0:T(8,128)(2,1)S(1)}, bf16[128,1024]{1,0:T(8,128)(2,1)S(1)}, u32[]{:S(2)}, u32[]{:S(2)}) %collective-permute-start.24) | collective-permute-done | bytes 262176 | tf_op jit(solution)/shard_map/ppermute | solution.py:27
  194.8 2.0 collective-permute-done.30
  197.7 1.3 fusion.18
  199.0 5.0 %collective-permute-done.25 = bf16[256,1024]{1,0:T(8,128)(2,1)S(1)} collective-permute-done((bf16[256,1024]{1,0:T(8,128)(2,1)S(1)}, bf16[256,1024]{1,0:T(8,128)(2,1)S(1)}, u32[]{:S(2)}, u32[]{:S(2)}) %collective-permute-start.25) | collective-permute-done | bytes 524320 | tf_op jit(solution)/shard_map/ppermute | solution.py:27
  204.0 1.3 fusion.12
  205.3 1.3 fusion.46
  206.7 1.3 fusion.52
  208.1 1.3 fusion.16
  209.3 1.3 fusion.10
  210.6 1.6 fusion.43
  212.2 1.4 fusion.49
  214.5 1.4 collective-permute-start.33
  217.8 5.8 %fusion.98 = (pred[1,2048,2048]{2,1,0:T(32,128)(4,1)S(1)}, pred[1,2048,2048]{2,1,0:T(32,128)(4,1)S(1)}) fusion(pred[2,2048,2048]{2,1,0:T(8,128)(4,1)} %broadcast_compare_fusion), kind=kLoop, calls=%fused_computation.171 | loop fusion | bytes 16777216 | tf_op jit(solution)/shard_map/slice | solution.py:207
  223.6 5.5 %collective-permute-done.33 = bf16[128,2048]{1,0:T(8,128)(2,1)} collective-permute-done((bf16[128,2048]{1,0:T(8,128)(2,1)}, bf16[128,2048]{1,0:T(8,128)(2,1)}, u32[]{:S(2)}, u32[]{:S(2)}) %collective-permute-start.33) | collective-permute-done | bytes 524320 | tf_op jit(solution)/shard_map/ppermute | solution.py:27
  230.3 3.7 %convolution_convert_fusion.2 = bf16[4,128,512]{2,1,0:T(8,128)(2,1)} fusion(pred[4,512,2048]{2,1,0:T(32,128)(4,1)S(1)} %bitcast.233, bf16[128,2048]{1,0:T(8,128)(2,1)S(1)} %add_convert_fusion.1), kind=kOutput, calls=%fused_computation.48 | convolution fusion | flops 1074003968 | bytes 5242880 | tf_op jit(solution)/shard_map/dot_general | solution.py:208
  234.0 2.9 convolution_convert_fusion.1
  237.0 7.0 %all-gather.2.cloned.1.call-done = bf16[4,128,1024]{2,1,0:T(8,128)(2,1)} async-done(((bf16[4,32,1024]{2,1,0:T(8,128)(2,1)}), bf16[4,128,1024]{2,1,0:T(8,128)(2,1)}) %all-gather.2.cloned.1.call-update) | async-done | bytes 1048592 | tf_op jit(solution)/shard_map/all_gather | solution.py:202
  245.7 2.1 collective-permute-done.34
  247.9 19.9 %all_to_all.10 = bf16[16,32,512]{2,1,0:T(8,128)(2,1)S(1)} all-to-all(bf16[16,32,512]{2,1,0:T(8,128)(2,1)S(1)} %bitcast.242), channel_id=1, replica_groups=mesh['sect'=2,'wide'=4,'narrow'=4] {'wide','narrow'}, dimensions={0} | all-to-all | bytes 1048576 | tf_op jit(solution)/shard_map/all_to_all | solution.py:214
  268.1 2.5 fusion.99
  270.6 1.4 collective-permute-start.36
  272.1 2.9 collective-permute-start.37
  275.1 8.4 %collective-permute-done.36 = bf16[4,32,512]{2,1,0:T(8,128)(2,1)S(1)} collective-permute-done((bf16[4,32,512]{2,1,0:T(8,128)(2,1)S(1)}, bf16[4,32,512]{2,1,0:T(8,128)(2,1)S(1)}, u32[]{:S(2)}, u32[]{:S(2)}) %collective-permute-start.36) | collective-permute-done | bytes 131104 | tf_op jit(solution)/shard_map/ppermute | solution.py:27
  284.5 1.9 collective-permute-done.38
  286.6 1.2 collective-permute-start.39
  287.8 7.2 %collective-permute-done.39 = bf16[128,1024]{1,0:T(8,128)(2,1)S(1)} collective-permute-done((bf16[128,1024]{1,0:T(8,128)(2,1)S(1)}, bf16[128,1024]{1,0:T(8,128)(2,1)S(1)}, u32[]{:S(2)}, u32[]{:S(2)}) %collective-permute-start.39) | collective-permute-done | bytes 262176 | tf_op jit(solution)/shard_map/ppermute | solution.py:27
  (177 shorter events, 27.3 us)
Async XLA Ops:
  7.2 31.3 %copy-start = (bf16[1024,1024]{1,0:T(8,128)(2,1)S(1)}, bf16[1024,1024]{1,0:T(8,128)(2,1)}, u32[]{:S(2)}) copy-start(bf16[1024,1024]{1,0:T(8,128)(2,1)} %param.8) | copy-start | bytes 6291460
  7.2 9.6 %collective-permute-start = (bf16[128,1024]{1,0:T(8,128)(2,1)}, bf16[128,1024]{1,0:T(8,128)(2,1)S(1)}, u32[]{:S(2)}, u32[]{:S(2)}) collective-permute-start(bf16[128,1024]{1,0:T(8,128)(2,1)} %param.7), channel_id=1, source_target_pairs={{0,8},{4,12},{8,0},{12,4},{1,9},{5,13},{9,1},{13,5},{2,10},{6,14},... | collective-permute-start | bytes 786440 | tf_op jit(solution)/shard_map/ppermute | solution.py:27
  17.7 2.0 collective-permute-start.1
  19.7 3.4 %copy-start.8 = (bf16[512,1024]{1,0:T(8,128)(2,1)}, bf16[512,1024]{1,0:T(8,128)(2,1)S(1)}, u32[]{:S(2)}) copy-start(bf16[512,1024]{1,0:T(8,128)(2,1)S(1)} %constant_dynamic-update-slice_fusion.1) | copy-start | bytes 3145732
  23.1 21.8 %all-to-all-start = ((bf16[16,32,512]{2,1,0:T(8,128)(2,1)}), bf16[16,32,512]{2,1,0:T(8,128)(2,1)S(1)}, u32[]{:S(2)}, u32[]{:S(2)}) async-start(bf16[16,32,512]{2,1,0:T(8,128)(2,1)} %bitcast.5), calls=%async_computation.1 | async-start | bytes 1048576 | tf_op jit(solution)/shard_map/all_to_all | solution.py:179
  29.3 60.5 %reduce-scatter.2.cloned.1.call-start = ((), (), s32[]{:S(2)}) async-start(), calls=%async_computation.3 | async-start | bytes 1310720 | tf_op jit(solution)/shard_map/reduce_scatter | solution.py:189
  45.1 7.2 %collective-permute-start.2 = (bf16[32,2048]{1,0:T(8,128)(2,1)S(1)}, bf16[32,2048]{1,0:T(8,128)(2,1)S(1)}, u32[]{:S(2)}, u32[]{:S(2)}) collective-permute-start(bf16[32,2048]{1,0:T(8,128)(2,1)S(1)} %bitcast.279), channel_id=1, source_target_pairs={{0,1},{1,0},{2,3},{3,2},{4,5},{5,4},{6,7},{7,6},{8,9},{9,8},{10,11... | collective-permute-start | bytes 393224 | tf_op jit(solution)/shard_map/ppermute | solution.py:27
  45.8 12.9 %collective-permute-start.3 = (bf16[32,2048]{1,0:T(8,128)(2,1)S(1)}, bf16[32,2048]{1,0:T(8,128)(2,1)S(1)}, u32[]{:S(2)}, u32[]{:S(2)}) collective-permute-start(bf16[32,2048]{1,0:T(8,128)(2,1)S(1)} %bitcast.280), channel_id=1, source_target_pairs={{0,2},{1,3},{2,0},{3,1},{4,6},{5,7},{6,4},{7,5},{8,10},{9,11},{10,... | collective-permute-start | bytes 393224 | tf_op jit(solution)/shard_map/ppermute | solution.py:27
  48.2 10.6 %collective-permute-start.4 = (bf16[32,2048]{1,0:T(8,128)(2,1)S(1)}, bf16[32,2048]{1,0:T(8,128)(2,1)S(1)}, u32[]{:S(2)}, u32[]{:S(2)}) collective-permute-start(bf16[32,2048]{1,0:T(8,128)(2,1)S(1)} %bitcast.281), channel_id=1, source_target_pairs={{0,3},{1,2},{2,1},{3,0},{4,7},{5,6},{6,5},{7,4},{8,11},{9,10},{10,... | collective-permute-start | bytes 393224 | tf_op jit(solution)/shard_map/ppermute | solution.py:27
  58.9 11.9 %collective-permute-start.5 = (bf16[128,2048]{1,0:T(8,128)(2,1)S(1)}, bf16[128,2048]{1,0:T(8,128)(2,1)}, u32[]{:S(2)}, u32[]{:S(2)}) collective-permute-start(bf16[128,2048]{1,0:T(8,128)(2,1)S(1)} %broadcast_add_fusion), channel_id=1, source_target_pairs={{0,16},{16,0},{1,17},{17,1},{2,18},{18,2},{3,19},{19,3},{4,20},{20... | collective-permute-start | bytes 1572872 | tf_op jit(solution)/shard_map/ppermute | solution.py:27
  60.4 183.5 %all-gather.2.cloned.1.call-start = ((), (), s32[]{:S(2)}) async-start(), calls=%async_computation.4 | async-start | bytes 1310720 | tf_op jit(solution)/shard_map/all_gather | solution.py:202
  78.1 10.9 %copy-start.3 = (bf16[128,2048]{1,0:T(8,128)(2,1)}, bf16[128,2048]{1,0:T(8,128)(2,1)S(1)}, u32[]{:S(2)}) copy-start(bf16[128,2048]{1,0:T(8,128)(2,1)S(1)} %fusion.58) | copy-start | bytes 1572868
  78.1 10.9 %collective-permute-start.6 = (bf16[128,2048]{1,0:T(8,128)(2,1)S(1)}, bf16[128,2048]{1,0:T(8,128)(2,1)S(1)}, u32[]{:S(2)}, u32[]{:S(2)}) collective-permute-start(bf16[128,2048]{1,0:T(8,128)(2,1)S(1)} %fusion.58), channel_id=1, source_target_pairs={{0,8},{4,12},{8,0},{12,4},{1,9},{5,13},{9,1},{13,5},{2,10},{6,14},... | collective-permute-start | bytes 1572872 | tf_op jit(solution)/shard_map/ppermute | solution.py:27
  89.0 0.8 copy-start.5
  89.8 2.8 collective-permute-start.7
  91.6 8.0 %copy-start.4 = (bf16[128,2048]{1,0:T(8,128)(2,1)S(1)}, bf16[128,2048]{1,0:T(8,128)(2,1)}, u32[]{:S(2)}) copy-start(bf16[128,2048]{1,0:T(8,128)(2,1)} %copy-done.3) | copy-start | bytes 1572868
  91.6 8.0 %copy-start.6 = (bf16[128,2048]{1,0:T(8,128)(2,1)S(1)}, bf16[128,2048]{1,0:T(8,128)(2,1)}, u32[]{:S(2)}) copy-start(bf16[128,2048]{1,0:T(8,128)(2,1)} %copy-done.5) | copy-start | bytes 1572868
  92.6 17.2 %slice-start = ((s8[16777216]{0:T(1024)(128)(4,1)}), s8[4194304]{0:T(1024)(128)(4,1)S(1)}, s32[]{:S(2)}) async-start(s8[16777216]{0:T(1024)(128)(4,1)} %bitcast.230), calls=%async_computation.5 | async-start | bytes 8388608
  92.6 17.2 %slice-start.1 = ((s8[16777216]{0:T(1024)(128)(4,1)}), s8[4194304]{0:T(1024)(128)(4,1)S(1)}, s32[]{:S(2)}) async-start(s8[16777216]{0:T(1024)(128)(4,1)} %bitcast.230), calls=%async_computation.6 | async-start | bytes 8388608
  98.0 11.8 %slice-start.2 = ((s8[16777216]{0:T(1024)(128)(4,1)}), s8[4194304]{0:T(1024)(128)(4,1)S(1)}, s32[]{:S(2)}) async-start(s8[16777216]{0:T(1024)(128)(4,1)} %bitcast.230), calls=%async_computation.7 | async-start | bytes 8388608
  98.0 11.8 %slice-start.3 = ((s8[16777216]{0:T(1024)(128)(4,1)}), s8[4194304]{0:T(1024)(128)(4,1)S(1)}, s32[]{:S(2)}) async-start(s8[16777216]{0:T(1024)(128)(4,1)} %bitcast.230), calls=%async_computation.8 | async-start | bytes 8388608
  98.0 19.2 %collective-permute-start.8 = (bf16[256,1024]{1,0:T(8,128)(2,1)S(1)}, bf16[256,1024]{1,0:T(8,128)(2,1)S(1)}, u32[]{:S(2)}, u32[]{:S(2)}) collective-permute-start(bf16[256,1024]{1,0:T(8,128)(2,1)S(1)} %dynamic-slice_bitcast_fusion), channel_id=1, source_target_pairs={{0,16},{16,0},{1,17},{17,1},{2,18},{18,2},{3,19},{19,3},{4,20},{20... | collective-permute-start | bytes 1572872 | tf_op jit(solution)/shard_map/ppermute | solution.py:27
  105.2 17.3 %collective-permute-start.14 = (bf16[256,1024]{1,0:T(8,128)(2,1)S(1)}, bf16[256,1024]{1,0:T(8,128)(2,1)S(1)}, u32[]{:S(2)}, u32[]{:S(2)}) collective-permute-start(bf16[256,1024]{1,0:T(8,128)(2,1)S(1)} %add_bitcast_fusion.2), channel_id=1, source_target_pairs={{0,1},{1,0},{2,3},{3,2},{4,5},{5,4},{6,7},{7,6},{8,9},{9,8},{10,11... | collective-permute-start | bytes 1572872 | tf_op jit(solution)/shard_map/ppermute | solution.py:27
  117.5 11.8 %collective-permute-start.9 = (bf16[128,1024]{1,0:T(8,128)(2,1)S(1)}, bf16[128,1024]{1,0:T(8,128)(2,1)S(1)}, u32[]{:S(2)}, u32[]{:S(2)}) collective-permute-start(bf16[128,1024]{1,0:T(8,128)(2,1)S(1)} %dynamic-slice_bitcast_fusion.4), channel_id=1, source_target_pairs={{0,1},{1,0},{2,3},{3,2},{4,5},{5,4},{6,7},{7,6},{8,9},{9,8},{10,11... | collective-permute-start | bytes 786440 | tf_op jit(solution)/shard_map/ppermute | solution.py:27
  123.8 9.2 %collective-permute-start.15 = (bf16[128,1024]{1,0:T(8,128)(2,1)S(1)}, bf16[128,1024]{1,0:T(8,128)(2,1)S(1)}, u32[]{:S(2)}, u32[]{:S(2)}) collective-permute-start(bf16[128,1024]{1,0:T(8,128)(2,1)S(1)} %dynamic-slice_bitcast_fusion.3), channel_id=1, source_target_pairs={{0,16},{16,0},{1,17},{17,1},{2,18},{18,2},{3,19},{19,3},{4,20},{20... | collective-permute-start | bytes 786440 | tf_op jit(solution)/shard_map/ppermute | solution.py:27
  124.6 25.6 %collective-permute-start.20 = (bf16[256,1024]{1,0:T(8,128)(2,1)S(1)}, bf16[256,1024]{1,0:T(8,128)(2,1)S(1)}, u32[]{:S(2)}, u32[]{:S(2)}) collective-permute-start(bf16[256,1024]{1,0:T(8,128)(2,1)S(1)} %add_bitcast_fusion.1), channel_id=1, source_target_pairs={{0,16},{16,0},{1,17},{17,1},{2,18},{18,2},{3,19},{19,3},{4,20},{20... | collective-permute-start | bytes 1572872 | tf_op jit(solution)/shard_map/ppermute | solution.py:27
  127.2 23.6 %collective-permute-start.26 = (bf16[256,1024]{1,0:T(8,128)(2,1)S(1)}, bf16[256,1024]{1,0:T(8,128)(2,1)S(1)}, u32[]{:S(2)}, u32[]{:S(2)}) collective-permute-start(bf16[256,1024]{1,0:T(8,128)(2,1)S(1)} %add_bitcast_fusion), channel_id=1, source_target_pairs={{0,1},{1,0},{2,3},{3,2},{4,5},{5,4},{6,7},{7,6},{8,9},{9,8},{10,11... | collective-permute-start | bytes 1572872 | tf_op jit(solution)/shard_map/ppermute | solution.py:27
  129.4 14.4 %collective-permute-start.10 = (bf16[64,1024]{1,0:T(8,128)(2,1)S(1)}, bf16[64,1024]{1,0:T(8,128)(2,1)S(1)}, u32[]{:S(2)}, u32[]{:S(2)}) collective-permute-start(bf16[64,1024]{1,0:T(8,128)(2,1)S(1)} %dynamic-slice_bitcast_fusion.8), channel_id=1, source_target_pairs={{0,2},{1,3},{2,0},{3,1},{4,6},{5,7},{6,4},{7,5},{8,10},{9,11},{10,... | collective-permute-start | bytes 393224 | tf_op jit(solution)/shard_map/ppermute | solution.py:27
  133.2 14.3 %collective-permute-start.16 = (bf16[64,1024]{1,0:T(8,128)(2,1)S(1)}, bf16[64,1024]{1,0:T(8,128)(2,1)S(1)}, u32[]{:S(2)}, u32[]{:S(2)}) collective-permute-start(bf16[64,1024]{1,0:T(8,128)(2,1)S(1)} %dynamic-slice_bitcast_fusion.7), channel_id=1, source_target_pairs={{0,2},{1,3},{2,0},{3,1},{4,6},{5,7},{6,4},{7,5},{8,10},{9,11},{10,... | collective-permute-start | bytes 393224 | tf_op jit(solution)/shard_map/ppermute | solution.py:27
  143.9 8.1 %collective-permute-start.11 = (bf16[64,1024]{1,0:T(8,128)(2,1)S(1)}, bf16[64,1024]{1,0:T(8,128)(2,1)S(1)}, u32[]{:S(2)}, u32[]{:S(2)}) collective-permute-start(bf16[64,1024]{1,0:T(8,128)(2,1)S(1)} %get-tuple-element.5), channel_id=1, source_target_pairs={{0,2},{1,3},{2,0},{3,1},{4,6},{5,7},{6,4},{7,5},{8,10},{9,11},{10,... | collective-permute-start | bytes 393224 | tf_op jit(solution)/shard_map/ppermute | solution.py:27
  147.5 7.3 %collective-permute-start.17 = (bf16[64,1024]{1,0:T(8,128)(2,1)S(1)}, bf16[64,1024]{1,0:T(8,128)(2,1)S(1)}, u32[]{:S(2)}, u32[]{:S(2)}) collective-permute-start(bf16[64,1024]{1,0:T(8,128)(2,1)S(1)} %get-tuple-element.7), channel_id=1, source_target_pairs={{0,2},{1,3},{2,0},{3,1},{4,6},{5,7},{6,4},{7,5},{8,10},{9,11},{10,... | collective-permute-start | bytes 393224 | tf_op jit(solution)/shard_map/ppermute | solution.py:27
  150.4 10.8 %collective-permute-start.21 = (bf16[128,1024]{1,0:T(8,128)(2,1)S(1)}, bf16[128,1024]{1,0:T(8,128)(2,1)S(1)}, u32[]{:S(2)}, u32[]{:S(2)}) collective-permute-start(bf16[128,1024]{1,0:T(8,128)(2,1)S(1)} %dynamic-slice_bitcast_fusion.2), channel_id=1, source_target_pairs={{0,1},{1,0},{2,3},{3,2},{4,5},{5,4},{6,7},{7,6},{8,9},{9,8},{10,11... | collective-permute-start | bytes 786440 | tf_op jit(solution)/shard_map/ppermute | solution.py:27
  151.0 12.3 %collective-permute-start.27 = (bf16[128,1024]{1,0:T(8,128)(2,1)S(1)}, bf16[128,1024]{1,0:T(8,128)(2,1)S(1)}, u32[]{:S(2)}, u32[]{:S(2)}) collective-permute-start(bf16[128,1024]{1,0:T(8,128)(2,1)S(1)} %dynamic-slice_bitcast_fusion.1), channel_id=1, source_target_pairs={{0,16},{16,0},{1,17},{17,1},{2,18},{18,2},{3,19},{19,3},{4,20},{20... | collective-permute-start | bytes 786440 | tf_op jit(solution)/shard_map/ppermute | solution.py:27
  152.1 19.4 %collective-permute-start.12 = (bf16[128,1024]{1,0:T(8,128)(2,1)S(1)}, bf16[128,1024]{1,0:T(8,128)(2,1)S(1)}, u32[]{:S(2)}, u32[]{:S(2)}) collective-permute-start(bf16[128,1024]{1,0:T(8,128)(2,1)S(1)} %bitcast.261), channel_id=1, source_target_pairs={{0,1},{1,0},{2,3},{3,2},{4,5},{5,4},{6,7},{7,6},{8,9},{9,8},{10,11... | collective-permute-start | bytes 786440 | tf_op jit(solution)/shard_map/ppermute | solution.py:27
  154.9 16.7 %collective-permute-start.18 = (bf16[128,1024]{1,0:T(8,128)(2,1)S(1)}, bf16[128,1024]{1,0:T(8,128)(2,1)S(1)}, u32[]{:S(2)}, u32[]{:S(2)}) collective-permute-start(bf16[128,1024]{1,0:T(8,128)(2,1)S(1)} %bitcast.263), channel_id=1, source_target_pairs={{0,16},{16,0},{1,17},{17,1},{2,18},{18,2},{3,19},{19,3},{4,20},{20... | collective-permute-start | bytes 786440 | tf_op jit(solution)/shard_map/ppermute | solution.py:27
  161.4 10.7 %collective-permute-start.22 = (bf16[64,1024]{1,0:T(8,128)(2,1)S(1)}, bf16[64,1024]{1,0:T(8,128)(2,1)S(1)}, u32[]{:S(2)}, u32[]{:S(2)}) collective-permute-start(bf16[64,1024]{1,0:T(8,128)(2,1)S(1)} %dynamic-slice_bitcast_fusion.6), channel_id=1, source_target_pairs={{0,2},{1,3},{2,0},{3,1},{4,6},{5,7},{6,4},{7,5},{8,10},{9,11},{10,... | collective-permute-start | bytes 393224 | tf_op jit(solution)/shard_map/ppermute | solution.py:27
  163.4 11.3 %collective-permute-start.28 = (bf16[64,1024]{1,0:T(8,128)(2,1)S(1)}, bf16[64,1024]{1,0:T(8,128)(2,1)S(1)}, u32[]{:S(2)}, u32[]{:S(2)}) collective-permute-start(bf16[64,1024]{1,0:T(8,128)(2,1)S(1)} %dynamic-slice_bitcast_fusion.5), channel_id=1, source_target_pairs={{0,2},{1,3},{2,0},{3,1},{4,6},{5,7},{6,4},{7,5},{8,10},{9,11},{10,... | collective-permute-start | bytes 393224 | tf_op jit(solution)/shard_map/ppermute | solution.py:27
  171.5 25.9 %collective-permute-start.13 = (bf16[256,1024]{1,0:T(8,128)(2,1)S(1)}, bf16[256,1024]{1,0:T(8,128)(2,1)S(1)}, u32[]{:S(2)}, u32[]{:S(2)}) collective-permute-start(bf16[256,1024]{1,0:T(8,128)(2,1)S(1)} %bitcast.244), channel_id=1, source_target_pairs={{0,16},{16,0},{1,17},{17,1},{2,18},{18,2},{3,19},{19,3},{4,20},{20... | collective-permute-start | bytes 1572872 | tf_op jit(solution)/shard_map/ppermute | solution.py:27
  171.6 25.8 %collective-permute-start.19 = (bf16[256,1024]{1,0:T(8,128)(2,1)S(1)}, bf16[256,1024]{1,0:T(8,128)(2,1)S(1)}, u32[]{:S(2)}, u32[]{:S(2)}) collective-permute-start(bf16[256,1024]{1,0:T(8,128)(2,1)S(1)} %bitcast.246), channel_id=1, source_target_pairs={{0,1},{1,0},{2,3},{3,2},{4,5},{5,4},{6,7},{7,6},{8,9},{9,8},{10,11... | collective-permute-start | bytes 1572872 | tf_op jit(solution)/shard_map/ppermute | solution.py:27
  172.2 12.0 %collective-permute-start.23 = (bf16[64,1024]{1,0:T(8,128)(2,1)S(1)}, bf16[64,1024]{1,0:T(8,128)(2,1)S(1)}, u32[]{:S(2)}, u32[]{:S(2)}) collective-permute-start(bf16[64,1024]{1,0:T(8,128)(2,1)S(1)} %get-tuple-element.9), channel_id=1, source_target_pairs={{0,2},{1,3},{2,0},{3,1},{4,6},{5,7},{6,4},{7,5},{8,10},{9,11},{10,... | collective-permute-start | bytes 393224 | tf_op jit(solution)/shard_map/ppermute | solution.py:27
  174.9 12.7 %collective-permute-start.29 = (bf16[64,1024]{1,0:T(8,128)(2,1)S(1)}, bf16[64,1024]{1,0:T(8,128)(2,1)S(1)}, u32[]{:S(2)}, u32[]{:S(2)}) collective-permute-start(bf16[64,1024]{1,0:T(8,128)(2,1)S(1)} %get-tuple-element.3), channel_id=1, source_target_pairs={{0,2},{1,3},{2,0},{3,1},{4,6},{5,7},{6,4},{7,5},{8,10},{9,11},{10,... | collective-permute-start | bytes 393224 | tf_op jit(solution)/shard_map/ppermute | solution.py:27
  184.1 10.5 %collective-permute-start.24 = (bf16[128,1024]{1,0:T(8,128)(2,1)S(1)}, bf16[128,1024]{1,0:T(8,128)(2,1)S(1)}, u32[]{:S(2)}, u32[]{:S(2)}) collective-permute-start(bf16[128,1024]{1,0:T(8,128)(2,1)S(1)} %bitcast.265), channel_id=1, source_target_pairs={{0,1},{1,0},{2,3},{3,2},{4,5},{5,4},{6,7},{7,6},{8,9},{9,8},{10,11... | collective-permute-start | bytes 786440 | tf_op jit(solution)/shard_map/ppermute | solution.py:27
  187.6 9.2 %collective-permute-start.30 = (bf16[128,1024]{1,0:T(8,128)(2,1)S(1)}, bf16[128,1024]{1,0:T(8,128)(2,1)S(1)}, u32[]{:S(2)}, u32[]{:S(2)}) collective-permute-start(bf16[128,1024]{1,0:T(8,128)(2,1)S(1)} %bitcast.259), channel_id=1, source_target_pairs={{0,16},{16,0},{1,17},{17,1},{2,18},{18,2},{3,19},{19,3},{4,20},{20... | collective-permute-start | bytes 786440 | tf_op jit(solution)/shard_map/ppermute | solution.py:27
  194.7 9.2 %collective-permute-start.25 = (bf16[256,1024]{1,0:T(8,128)(2,1)S(1)}, bf16[256,1024]{1,0:T(8,128)(2,1)S(1)}, u32[]{:S(2)}, u32[]{:S(2)}) collective-permute-start(bf16[256,1024]{1,0:T(8,128)(2,1)S(1)} %bitcast.248), channel_id=1, source_target_pairs={{0,16},{16,0},{1,17},{17,1},{2,18},{18,2},{3,19},{19,3},{4,20},{20... | collective-permute-start | bytes 1572872 | tf_op jit(solution)/shard_map/ppermute | solution.py:27
  196.8 9.8 %collective-permute-start.31 = (bf16[256,1024]{1,0:T(8,128)(2,1)S(1)}, bf16[256,1024]{1,0:T(8,128)(2,1)S(1)}, u32[]{:S(2)}, u32[]{:S(2)}) collective-permute-start(bf16[256,1024]{1,0:T(8,128)(2,1)S(1)} %bitcast.250), channel_id=1, source_target_pairs={{0,1},{1,0},{2,3},{3,2},{4,5},{5,4},{6,7},{7,6},{8,9},{9,8},{10,11... | collective-permute-start | bytes 1572872 | tf_op jit(solution)/shard_map/ppermute | solution.py:27
  208.0 4.3 %collective-permute-start.32 = (bf16[256,2048]{1,0:T(8,128)(2,1)S(1)}, bf16[256,2048]{1,0:T(8,128)(2,1)S(1)}, u32[]{:S(2)}, u32[]{:S(2)}) collective-permute-start(bf16[256,2048]{1,0:T(8,128)(2,1)S(1)} %fusion.52), channel_id=1, source_target_pairs={{0,4},{4,0},{8,12},{12,8},{1,5},{5,1},{9,13},{13,9},{2,6},{6,2},{1... | collective-permute-start | bytes 3145736 | tf_op jit(solution)/shard_map/ppermute | solution.py:27
  212.2 4.8 %copy-start.7 = (bf16[4,32,1024]{2,1,0:T(8,128)(2,1)S(1)}, bf16[4,32,1024]{2,1,0:T(8,128)(2,1)}, u32[]{:S(2)}) copy-start(bf16[4,32,1024]{2,1,0:T(8,128)(2,1)} %reduce-scatter.2.cloned.1.call-done) | copy-start | bytes 786436
  214.5 14.6 %collective-permute-start.33 = (bf16[128,2048]{1,0:T(8,128)(2,1)}, bf16[128,2048]{1,0:T(8,128)(2,1)}, u32[]{:S(2)}, u32[]{:S(2)}) collective-permute-start(bf16[128,2048]{1,0:T(8,128)(2,1)} %slice.196), channel_id=1, source_target_pairs={{0,8},{4,12},{8,0},{12,4},{1,9},{5,13},{9,1},{13,5},{2,10},{6,14},... | collective-permute-start | bytes 1572872 | tf_op jit(solution)/shard_map/ppermute | solution.py:27
  230.3 3.8 %copy-start.2 = (bf16[128,2048]{1,0:T(8,128)(2,1)}, bf16[128,2048]{1,0:T(8,128)(2,1)S(1)}, u32[]{:S(2)}) copy-start(bf16[128,2048]{1,0:T(8,128)(2,1)S(1)} %add_convert_fusion.1) | copy-start | bytes 1572868
  234.0 13.7 %collective-permute-start.34 = (bf16[4,128,512]{2,1,0:T(8,128)(2,1)}, bf16[4,128,512]{2,1,0:T(8,128)(2,1)S(1)}, u32[]{:S(2)}, u32[]{:S(2)}) collective-permute-start(bf16[4,128,512]{2,1,0:T(8,128)(2,1)} %convolution_convert_fusion.2), channel_id=1, source_target_pairs={{0,16},{16,0},{1,17},{17,1},{2,18},{18,2},{3,19},{19,3},{4,20},{20... | collective-permute-start | bytes 1572872 | tf_op jit(solution)/shard_map/ppermute | solution.py:27
  268.0 15.6 %copy-start.1 = (bf16[512,1024]{1,0:T(8,128)(2,1)S(1)}, bf16[512,1024]{1,0:T(8,128)(2,1)}, u32[]{:S(2)}) copy-start(bf16[512,1024]{1,0:T(8,128)(2,1)} %param.9) | copy-start | bytes 3145732
  268.0 7.1 %collective-permute-start.35 = (bf16[4,32,512]{2,1,0:T(8,128)(2,1)S(1)}, bf16[4,32,512]{2,1,0:T(8,128)(2,1)S(1)}, u32[]{:S(2)}, u32[]{:S(2)}) collective-permute-start(bf16[4,32,512]{2,1,0:T(8,128)(2,1)S(1)} %pad_maximum_fusion.5), channel_id=1, source_target_pairs={{0,1},{1,0},{2,3},{3,2},{4,5},{5,4},{6,7},{7,6},{8,9},{9,8},{10,11... | collective-permute-start | bytes 393224 | tf_op jit(solution)/shard_map/ppermute | solution.py:27
  270.6 12.9 %collective-permute-start.36 = (bf16[4,32,512]{2,1,0:T(8,128)(2,1)S(1)}, bf16[4,32,512]{2,1,0:T(8,128)(2,1)S(1)}, u32[]{:S(2)}, u32[]{:S(2)}) collective-permute-start(bf16[4,32,512]{2,1,0:T(8,128)(2,1)S(1)} %pad_maximum_fusion.5), channel_id=1, source_target_pairs={{0,2},{1,3},{2,0},{3,1},{4,6},{5,7},{6,4},{7,5},{8,10},{9,11},{10,... | collective-permute-start | bytes 393224 | tf_op jit(solution)/shard_map/ppermute | solution.py:27
  272.1 11.5 %collective-permute-start.37 = (bf16[4,32,512]{2,1,0:T(8,128)(2,1)S(1)}, bf16[4,32,512]{2,1,0:T(8,128)(2,1)S(1)}, u32[]{:S(2)}, u32[]{:S(2)}) collective-permute-start(bf16[4,32,512]{2,1,0:T(8,128)(2,1)S(1)} %pad_maximum_fusion.5), channel_id=1, source_target_pairs={{0,3},{1,2},{2,1},{3,0},{4,7},{5,6},{6,5},{7,4},{8,11},{9,10},{10,... | collective-permute-start | bytes 393224 | tf_op jit(solution)/shard_map/ppermute | solution.py:27
  284.4 2.0 collective-permute-start.38
  286.6 8.4 %collective-permute-start.39 = (bf16[128,1024]{1,0:T(8,128)(2,1)S(1)}, bf16[128,1024]{1,0:T(8,128)(2,1)S(1)}, u32[]{:S(2)}, u32[]{:S(2)}) collective-permute-start(bf16[128,1024]{1,0:T(8,128)(2,1)S(1)} %slice.203), channel_id=1, source_target_pairs={{0,8},{4,12},{8,0},{12,4},{1,9},{5,13},{9,1},{13,5},{2,10},{6,14},... | collective-permute-start | bytes 786440 | tf_op jit(solution)/shard_map/ppermute | solution.py:27
Sparse Core Ops, SparseCore 0:
  60.6 26.9 reduce-scatter.1
  217.9 25.9 all-gather.1

commit v4 on v3

--- a/solution.py
+++ b/solution.py
@@ -119,7 +119,7 @@
     middles, firsts = [], []
     for c in range(CHUNKS):
         product = times_transposed(right, blocks[c]).astype(jnp.bfloat16)
-        others = [firsts[c - len(orders)]] if c >= len(orders) else ([beside] if c == 1 else [])
+        others = [firsts[c - len(orders)]] if c >= len(orders) else ([beside] if c == 0 else [])
         middle, first = sum_all(product, orders[c % len(orders)], others)
         middles.append(middle)
         firsts.append(first)
@@ -184,11 +184,13 @@
 
     updates = direct_gather(hold(border_out, landing), "narrow")
     pivot_terms = times_transposed(piece, leaf_factor).astype(jnp.bfloat16)
-    pivot_terms = pivot_terms.reshape(wide_count, rows, -1)
+    pivot_terms = lax.optimization_barrier(pivot_terms.reshape(wide_count, rows, -1))
     passed = hold(updates, pivot_terms)
+    pivot_terms = hold(pivot_terms, updates)
     leaf_mid = lax.psum_scatter(pivot_terms, "narrow", scatter_dimension=1, tiled=True)
-    others = [swap(passed, "sect", r) for r in range(1, sect_count)]
-    landed = times(jnp.concatenate([updates] + others, axis=1), landing.reshape(-1, root_block))
+    landed = lax.optimization_barrier(times(updates, landing[0]))
+    for r in range(1, sect_count):
+        landed = landed + times(swap(passed, "sect", r), landing[r])
     root_right = (root_rhs.astype(jnp.float32) - landed).astype(jnp.bfloat16)
     right = relative_gather(root_right, "wide", 2)
     right = jnp.concatenate([right, swap(right, "wide", 1)], axis=0)

time: 307 us -> 307 us (level)
  starting transfers between devices: 59.5 us -> 52.8 us
    ppermute x40, waiting for transfers between devices: 112 us -> 102 us  [swap(): return lax.ppermute(value, axis, pairs)]
    reduce_scatter x1, waiting for transfers between devices: 0.01 us -> 8.61 us  [body(): lax.psum_scatter(pivot_terms, 'narrow', scatter_dimension=1, tiled=True)]
    ppermute x40, starting transfers between devices: 53 us -> 46.4 us  [swap(): return lax.ppermute(value, axis, pairs)]
    dot_general x11 -> x12, matrix products: 21.3 us -> 24.3 us  [times(): return jnp.dot(left, right, preferred_element_type=jnp.float32)]
    slice x7 -> x8, local copies, waits for them, and re-layouts: 6.22 us -> 6.18 us  [hold(): lax.slice(o, (0,) * o.ndim, (1,) * o.ndim).reshape(())]
  transfers between devices with their start and end apart: 43 -> 43, of which waited for: 24 -> 26; matrix products, arithmetic and copies ran while one was open for 22% -> 24% of each run, Pallas kernels for 0% -> 0%
where the time goes in v4:
time: 307 us; the launch traced here: 301 us
  waiting for transfers between devices  120 us (39%)
  matrix products  53.7 us (17%)
  starting transfers between devices  52.8 us (17%)
  between operations  20.4 us (7%)
  blocking collectives  20.2 us (7%)
  other arithmetic  16.9 us (6%)
  local copies, waits for them, and re-layouts  16.5 us (5%)
    ppermute x40, waiting for transfers between devices, swap(): return lax.ppermute(value, axis, pairs)  102 us
    ppermute x40, starting transfers between devices, swap(): return lax.ppermute(value, axis, pairs)  46.4 us
    dot_general x12, matrix products, times(): return jnp.dot(left, right, preferred_element_type=jnp.float32)  24.3 us
    dot_general x6, matrix products, times_transposed(): lax.dot_general(left, right, (((1,), (1,)), ((), ())), preferred_element_...  22.8 us
    all_to_all x1, blocking collectives, body(): got = lax.all_to_all(sent, ('wide', 'narrow'), 0, 0, tiled=True)  20.2 us
    reduce_scatter x1, waiting for transfers between devices, body(): lax.psum_scatter(pivot_terms, 'narrow', scatter_dimension=1, tiled=True)  8.61 us
    eq x1, other arithmetic, body(): landing = (near_map[:, :, None] == columns).astype(jnp.bfloat16)  7.31 us
    all_gather x1, waiting for transfers between devices, body(): lax.all_gather(leaf_mid, 'narrow', axis=1, tiled=True)  6.98 us
  transfers between devices with their start and end apart: 43, of which 26 were waited for; matrix products, arithmetic and copies ran while one was open for 24% of the time, Pallas kernels for 0%

profile of v4, /device:TPU:0, one launch (start us, length us, event | category | flops | bytes accessed | tf_op | source)
XLA Modules:
  0.0 300.9 jit_solution(1288673505378346217)
XLA Ops:
  7.2 3.0 %collective-permute-start = (bf16[128,1024]{1,0:T(8,128)(2,1)}, bf16[128,1024]{1,0:T(8,128)(2,1)S(1)}, u32[]{:S(2)}, u32[]{:S(2)}) collective-permute-start(bf16[128,1024]{1,0:T(8,128)(2,1)} %param.7), channel_id=1, source_target_pairs={{0,8},{4,12},{8,0},{12,4},{1,9},{5,13},{9,1},{13,5},{2,10},{6,14},... | collective-permute-start | bytes 786440 | tf_op jit(solution)/shard_map/ppermute | solution.py:27
  12.0 4.7 %collective-permute-done = bf16[128,1024]{1,0:T(8,128)(2,1)S(1)} collective-permute-done((bf16[128,1024]{1,0:T(8,128)(2,1)}, bf16[128,1024]{1,0:T(8,128)(2,1)S(1)}, u32[]{:S(2)}, u32[]{:S(2)}) %collective-permute-start) | collective-permute-done | bytes 262176 | tf_op jit(solution)/shard_map/ppermute | solution.py:27
  17.9 1.8 collective-permute-done.1
  19.7 2.3 convolution_convert_fusion.3
  23.1 6.2 %all-to-all-start = ((bf16[16,32,512]{2,1,0:T(8,128)(2,1)}), bf16[16,32,512]{2,1,0:T(8,128)(2,1)S(1)}, u32[]{:S(2)}, u32[]{:S(2)}) async-start(bf16[16,32,512]{2,1,0:T(8,128)(2,1)} %bitcast.5), calls=%async_computation | async-start | bytes 1048576 | tf_op jit(solution)/shard_map/all_to_all | solution.py:179
  29.3 7.3 %broadcast_compare_fusion = pred[2,2048,2048]{2,1,0:T(8,128)(4,1)} fusion(s32[2048]{0:T(1024)S(1)} %iota_add_fusion, s32[2,2048]{1,0:T(2,128)S(1)} %pad_add_fusion), kind=kLoop, calls=%fused_computation | loop fusion | flops 8388608 | bytes 8413184 | tf_op jit(solution)/shard_map/eq | solution.py:156
  38.4 2.5 convolution_convert_fusion
  42.1 2.8 all-to-all-done
  45.2 1.4 collective-permute-start.3
  46.6 2.9 collective-permute-start.4
  49.8 2.2 collective-permute-done.2
  52.0 6.1 %collective-permute-done.3 = bf16[32,2048]{1,0:T(8,128)(2,1)S(1)} collective-permute-done((bf16[32,2048]{1,0:T(8,128)(2,1)S(1)}, bf16[32,2048]{1,0:T(8,128)(2,1)S(1)}, u32[]{:S(2)}, u32[]{:S(2)}) %collective-permute-start.3) | collective-permute-done | bytes 131104 | tf_op jit(solution)/shard_map/ppermute | solution.py:27
  58.3 1.6 collective-permute-start.5
  59.8 5.8 %fusion.2 = f32[128,2048]{1,0:T(8,128)} fusion(bf16[128,2048]{1,0:T(8,128)(2,1)S(1)} %bitcast.249, pred[2,2048,2048]{2,1,0:T(8,128)(4,1)} %broadcast_compare_fusion), kind=kOutput, calls=%fused_computation.3 | convolution fusion | flops 1073741824 | bytes 5767168 | tf_op jit(solution)/shard_map/dot_general | solution.py:16
  69.2 4.9 %fusion = f32[128,2048]{1,0:T(8,128)S(1)} fusion(bf16[128,2048]{1,0:T(8,128)(2,1)} %collective-permute-done.5, pred[2,2048,2048]{2,1,0:T(8,128)(4,1)} %broadcast_compare_fusion), kind=kOutput, calls=%fused_computation.1 | convolution fusion | flops 1073741824 | bytes 5767168 | tf_op jit(solution)/shard_map/dot_general | solution.py:16
  74.3 1.5 collective-permute-start.6
  75.9 8.4 %collective-permute-done.6 = bf16[128,2048]{1,0:T(8,128)(2,1)S(1)} collective-permute-done((bf16[128,2048]{1,0:T(8,128)(2,1)S(1)}, bf16[128,2048]{1,0:T(8,128)(2,1)S(1)}, u32[]{:S(2)}, u32[]{:S(2)}) %collective-permute-start.6) | collective-permute-done | bytes 524320 | tf_op jit(solution)/shard_map/ppermute | solution.py:27
  85.3 8.6 %reduce-scatter.2.cloned.1.call-done = bf16[4,32,1024]{2,1,0:T(8,128)(2,1)} async-done(((bf16[4,128,1024]{2,1,0:T(8,128)(2,1)}), bf16[4,32,1024]{2,1,0:T(8,128)(2,1)}) %reduce-scatter.2.cloned.1.call-update) | async-done | bytes 262160 | tf_op jit(solution)/shard_map/reduce_scatter | solution.py:190
  95.8 5.0 %fusion.55 = bf16[512,1024]{1,0:T(8,128)(2,1)S(1)} fusion(bf16[4096,2048]{1,0:T(8,128)(2,1)} %param.10, bf16[256,2048]{1,0:T(8,128)(2,1)} %collective-permute-done.7, bf16[128,2048]{1,0:T(8,128)(2,1)S(1)} %collective-permute-done.6, bf16[128,2048]{1,0:T(8,128)(2,1)S(1)} %subtract_convert_fusion), kind=kOutput, calls=%fused_computation.41 | convolution fusion | flops 2154299392 | bytes 7340032 | tf_op jit(solution)/shard_map/dot_general | solution.py:10
  100.9 1.5 collective-permute-start.8
  102.4 5.6 %fusion.58 = bf16[512,1024]{1,0:T(8,128)(2,1)S(1)} fusion(bf16[4096,2048]{1,0:T(8,128)(2,1)} %param.10, bf16[256,2048]{1,0:T(8,128)(2,1)} %collective-permute-done.7, bf16[128,2048]{1,0:T(8,128)(2,1)S(1)} %collective-permute-done.6, bf16[128,2048]{1,0:T(8,128)(2,1)S(1)} %subtract_convert_fusion), kind=kOutput, calls=%fused_computation.42 | convolution fusion | flops 2154299392 | bytes 7340032 | tf_op jit(solution)/shard_map/dot_general | solution.py:10
  108.2 3.7 %fusion.61 = bf16[512,1024]{1,0:T(8,128)(2,1)S(1)} fusion(bf16[4096,2048]{1,0:T(8,128)(2,1)S(1)} %bitcast.237, bf16[256,2048]{1,0:T(8,128)(2,1)} %collective-permute-done.7, bf16[128,2048]{1,0:T(8,128)(2,1)S(1)} %collective-permute-done.6, bf16[128,2048]{1,0:T(8,128)(2,1)S(1)} %subtract_convert_fusion), kind=kOutput, calls=%fused_computation.43 | convolution fusion | flops 2154299392 | bytes 7340032 | tf_op jit(solution)/shard_map/dot_general | solution.py:10
  111.8 3.7 %fusion.64 = bf16[512,1024]{1,0:T(8,128)(2,1)S(1)} fusion(bf16[4096,2048]{1,0:T(8,128)(2,1)S(1)} %bitcast.237, bf16[256,2048]{1,0:T(8,128)(2,1)} %collective-permute-done.7, bf16[128,2048]{1,0:T(8,128)(2,1)S(1)} %collective-permute-done.6, bf16[128,2048]{1,0:T(8,128)(2,1)S(1)} %subtract_convert_fusion), kind=kOutput, calls=%fused_computation.44 | convolution fusion | flops 2154299392 | bytes 7340032 | tf_op jit(solution)/shard_map/dot_general | solution.py:10
  115.8 2.0 collective-permute-start.9
  117.8 5.2 %collective-permute-done.14 = bf16[256,1024]{1,0:T(8,128)(2,1)S(1)} collective-permute-done((bf16[256,1024]{1,0:T(8,128)(2,1)S(1)}, bf16[256,1024]{1,0:T(8,128)(2,1)S(1)}, u32[]{:S(2)}, u32[]{:S(2)}) %collective-permute-start.14) | collective-permute-done | bytes 524320 | tf_op jit(solution)/shard_map/ppermute | solution.py:27
  125.1 1.9 collective-permute-start.20
  127.8 1.7 collective-permute-start.10
  129.5 4.0 %collective-permute-done.15 = bf16[128,1024]{1,0:T(8,128)(2,1)S(1)} collective-permute-done((bf16[128,1024]{1,0:T(8,128)(2,1)S(1)}, bf16[128,1024]{1,0:T(8,128)(2,1)S(1)}, u32[]{:S(2)}, u32[]{:S(2)}) %collective-permute-start.15) | collective-permute-done | bytes 262176 | tf_op jit(solution)/shard_map/ppermute | solution.py:27
  134.6 7.4 %collective-permute-done.10 = bf16[64,1024]{1,0:T(8,128)(2,1)S(1)} collective-permute-done((bf16[64,1024]{1,0:T(8,128)(2,1)S(1)}, bf16[64,1024]{1,0:T(8,128)(2,1)S(1)}, u32[]{:S(2)}, u32[]{:S(2)}) %collective-permute-start.10) | collective-permute-done | bytes 131104 | tf_op jit(solution)/shard_map/ppermute | solution.py:27
  142.3 3.5 %collective-permute-start.11 = (bf16[64,1024]{1,0:T(8,128)(2,1)S(1)}, bf16[64,1024]{1,0:T(8,128)(2,1)S(1)}, u32[]{:S(2)}, u32[]{:S(2)}) collective-permute-start(bf16[64,1024]{1,0:T(8,128)(2,1)S(1)} %get-tuple-element.5), channel_id=1, source_target_pairs={{0,2},{1,3},{2,0},{3,1},{4,6},{5,7},{6,4},{7,5},{8,10},{9,11},{10,... | collective-permute-start | bytes 393224 | tf_op jit(solution)/shard_map/ppermute | solution.py:27
  145.9 2.5 collective-permute-start.17
  150.9 2.4 collective-permute-start.12
  154.0 6.5 %collective-permute-done.21 = bf16[128,1024]{1,0:T(8,128)(2,1)S(1)} collective-permute-done((bf16[128,1024]{1,0:T(8,128)(2,1)S(1)}, bf16[128,1024]{1,0:T(8,128)(2,1)S(1)}, u32[]{:S(2)}, u32[]{:S(2)}) %collective-permute-start.21) | collective-permute-done | bytes 262176 | tf_op jit(solution)/shard_map/ppermute | solution.py:27
  161.9 1.9 collective-permute-start.28
  163.8 5.1 %collective-permute-done.12 = bf16[128,1024]{1,0:T(8,128)(2,1)S(1)} collective-permute-done((bf16[128,1024]{1,0:T(8,128)(2,1)S(1)}, bf16[128,1024]{1,0:T(8,128)(2,1)S(1)}, u32[]{:S(2)}, u32[]{:S(2)}) %collective-permute-start.12) | collective-permute-done | bytes 262176 | tf_op jit(solution)/shard_map/ppermute | solution.py:27
  169.5 1.5 collective-permute-start.23
  172.7 9.6 %collective-permute-done.23 = bf16[64,1024]{1,0:T(8,128)(2,1)S(1)} collective-permute-done((bf16[64,1024]{1,0:T(8,128)(2,1)S(1)}, bf16[64,1024]{1,0:T(8,128)(2,1)S(1)}, u32[]{:S(2)}, u32[]{:S(2)}) %collective-permute-start.23) | collective-permute-done | bytes 131104 | tf_op jit(solution)/shard_map/ppermute | solution.py:27
  182.3 3.5 %collective-permute-start.24 = (bf16[128,1024]{1,0:T(8,128)(2,1)S(1)}, bf16[128,1024]{1,0:T(8,128)(2,1)S(1)}, u32[]{:S(2)}, u32[]{:S(2)}) collective-permute-start(bf16[128,1024]{1,0:T(8,128)(2,1)S(1)} %bitcast.274), channel_id=1, source_target_pairs={{0,1},{1,0},{2,3},{3,2},{4,5},{5,4},{6,7},{7,6},{8,9},{9,8},{10,11... | collective-permute-start | bytes 786440 | tf_op jit(solution)/shard_map/ppermute | solution.py:27
  186.2 6.4 %collective-permute-done.24 = bf16[128,1024]{1,0:T(8,128)(2,1)S(1)} collective-permute-done((bf16[128,1024]{1,0:T(8,128)(2,1)S(1)}, bf16[128,1024]{1,0:T(8,128)(2,1)S(1)}, u32[]{:S(2)}, u32[]{:S(2)}) %collective-permute-start.24) | collective-permute-done | bytes 262176 | tf_op jit(solution)/shard_map/ppermute | solution.py:27
  192.7 2.5 collective-permute-done.30
  196.2 1.3 fusion.18
  197.5 4.3 %collective-permute-done.25 = bf16[256,1024]{1,0:T(8,128)(2,1)S(1)} collective-permute-done((bf16[256,1024]{1,0:T(8,128)(2,1)S(1)}, bf16[256,1024]{1,0:T(8,128)(2,1)S(1)}, u32[]{:S(2)}, u32[]{:S(2)}) %collective-permute-start.25) | collective-permute-done | bytes 524320 | tf_op jit(solution)/shard_map/ppermute | solution.py:27
  201.9 1.3 fusion.12
  203.2 1.3 fusion.46
  204.5 1.3 fusion.52
  205.9 1.3 fusion.16
  207.2 1.3 fusion.10
  208.5 1.3 fusion.43
  209.8 1.4 fusion.49
  212.1 1.7 collective-permute-start.33
  215.6 6.1 %fusion.89 = (pred[1,2048,2048]{2,1,0:T(32,128)(4,1)S(1)}, pred[1,2048,2048]{2,1,0:T(32,128)(4,1)S(1)}) fusion(pred[2,2048,2048]{2,1,0:T(8,128)(4,1)} %broadcast_compare_fusion), kind=kLoop, calls=%fused_computation.168 | loop fusion | bytes 16777216 | tf_op jit(solution)/shard_map/slice | solution.py:193
  221.7 5.0 %collective-permute-done.33 = bf16[128,2048]{1,0:T(8,128)(2,1)} collective-permute-done((bf16[128,2048]{1,0:T(8,128)(2,1)}, bf16[128,2048]{1,0:T(8,128)(2,1)}, u32[]{:S(2)}, u32[]{:S(2)}) %collective-permute-start.33) | collective-permute-done | bytes 524320 | tf_op jit(solution)/shard_map/ppermute | solution.py:27
  227.9 3.7 %convolution_convert_fusion.2 = bf16[4,128,512]{2,1,0:T(8,128)(2,1)} fusion(pred[4,512,2048]{2,1,0:T(32,128)(4,1)S(1)} %bitcast.239, bf16[128,2048]{1,0:T(8,128)(2,1)S(1)} %add_convert_fusion.1), kind=kOutput, calls=%fused_computation.46 | convolution fusion | flops 1074003968 | bytes 5242880 | tf_op jit(solution)/shard_map/dot_general | solution.py:210
  231.8 2.9 convolution_convert_fusion.1
  234.7 7.0 %all-gather.2.cloned.1.call-done = bf16[4,128,1024]{2,1,0:T(8,128)(2,1)} async-done(((bf16[4,32,1024]{2,1,0:T(8,128)(2,1)}), bf16[4,128,1024]{2,1,0:T(8,128)(2,1)}) %all-gather.2.cloned.1.call-update) | async-done | bytes 1048592 | tf_op jit(solution)/shard_map/all_gather | solution.py:204
  243.5 1.9 collective-permute-done.34
  245.5 20.2 %all_to_all.10 = bf16[16,32,512]{2,1,0:T(8,128)(2,1)S(1)} all-to-all(bf16[16,32,512]{2,1,0:T(8,128)(2,1)S(1)} %bitcast.248), channel_id=1, replica_groups=mesh['sect'=2,'wide'=4,'narrow'=4] {'wide','narrow'}, dimensions={0} | all-to-all | bytes 1048576 | tf_op jit(solution)/shard_map/all_to_all | solution.py:216
  266.0 2.5 fusion.90
  268.5 1.4 collective-permute-start.36
  270.0 2.9 collective-permute-start.37
  273.0 8.4 %collective-permute-done.36 = bf16[4,32,512]{2,1,0:T(8,128)(2,1)S(1)} collective-permute-done((bf16[4,32,512]{2,1,0:T(8,128)(2,1)S(1)}, bf16[4,32,512]{2,1,0:T(8,128)(2,1)S(1)}, u32[]{:S(2)}, u32[]{:S(2)}) %collective-permute-start.36) | collective-permute-done | bytes 131104 | tf_op jit(solution)/shard_map/ppermute | solution.py:27
  282.4 1.9 collective-permute-done.38
  284.5 1.2 collective-permute-start.39
  285.7 7.2 %collective-permute-done.39 = bf16[128,1024]{1,0:T(8,128)(2,1)S(1)} collective-permute-done((bf16[128,1024]{1,0:T(8,128)(2,1)S(1)}, bf16[128,1024]{1,0:T(8,128)(2,1)S(1)}, u32[]{:S(2)}, u32[]{:S(2)}) %collective-permute-start.39) | collective-permute-done | bytes 262176 | tf_op jit(solution)/shard_map/ppermute | solution.py:27
  (180 shorter events, 30.6 us)
Async XLA Ops:
  7.2 31.3 %copy-start = (bf16[1024,1024]{1,0:T(8,128)(2,1)S(1)}, bf16[1024,1024]{1,0:T(8,128)(2,1)}, u32[]{:S(2)}) copy-start(bf16[1024,1024]{1,0:T(8,128)(2,1)} %param.8) | copy-start | bytes 6291460
  7.2 9.6 %collective-permute-start = (bf16[128,1024]{1,0:T(8,128)(2,1)}, bf16[128,1024]{1,0:T(8,128)(2,1)S(1)}, u32[]{:S(2)}, u32[]{:S(2)}) collective-permute-start(bf16[128,1024]{1,0:T(8,128)(2,1)} %param.7), channel_id=1, source_target_pairs={{0,8},{4,12},{8,0},{12,4},{1,9},{5,13},{9,1},{13,5},{2,10},{6,14},... | collective-permute-start | bytes 786440 | tf_op jit(solution)/shard_map/ppermute | solution.py:27
  17.7 2.0 collective-permute-start.1
  19.7 3.4 %copy-start.8 = (bf16[512,1024]{1,0:T(8,128)(2,1)}, bf16[512,1024]{1,0:T(8,128)(2,1)S(1)}, u32[]{:S(2)}) copy-start(bf16[512,1024]{1,0:T(8,128)(2,1)S(1)} %constant_dynamic-update-slice_fusion.1) | copy-start | bytes 3145732
  23.1 21.8 %all-to-all-start = ((bf16[16,32,512]{2,1,0:T(8,128)(2,1)}), bf16[16,32,512]{2,1,0:T(8,128)(2,1)S(1)}, u32[]{:S(2)}, u32[]{:S(2)}) async-start(bf16[16,32,512]{2,1,0:T(8,128)(2,1)} %bitcast.5), calls=%async_computation | async-start | bytes 1048576 | tf_op jit(solution)/shard_map/all_to_all | solution.py:179
  29.3 64.7 %reduce-scatter.2.cloned.1.call-start = ((), (), s32[]{:S(2)}) async-start(), calls=%async_computation.3 | async-start | bytes 1310720 | tf_op jit(solution)/shard_map/reduce_scatter | solution.py:190
  41.0 1.2 copy-start.2
  45.1 6.9 %collective-permute-start.2 = (bf16[32,2048]{1,0:T(8,128)(2,1)S(1)}, bf16[32,2048]{1,0:T(8,128)(2,1)S(1)}, u32[]{:S(2)}, u32[]{:S(2)}) collective-permute-start(bf16[32,2048]{1,0:T(8,128)(2,1)S(1)} %bitcast.286), channel_id=1, source_target_pairs={{0,1},{1,0},{2,3},{3,2},{4,5},{5,4},{6,7},{7,6},{8,9},{9,8},{10,11... | collective-permute-start | bytes 393224 | tf_op jit(solution)/shard_map/ppermute | solution.py:27
  45.2 12.9 %collective-permute-start.3 = (bf16[32,2048]{1,0:T(8,128)(2,1)S(1)}, bf16[32,2048]{1,0:T(8,128)(2,1)S(1)}, u32[]{:S(2)}, u32[]{:S(2)}) collective-permute-start(bf16[32,2048]{1,0:T(8,128)(2,1)S(1)} %bitcast.287), channel_id=1, source_target_pairs={{0,2},{1,3},{2,0},{3,1},{4,6},{5,7},{6,4},{7,5},{8,10},{9,11},{10,... | collective-permute-start | bytes 393224 | tf_op jit(solution)/shard_map/ppermute | solution.py:27
  46.6 11.5 %collective-permute-start.4 = (bf16[32,2048]{1,0:T(8,128)(2,1)S(1)}, bf16[32,2048]{1,0:T(8,128)(2,1)S(1)}, u32[]{:S(2)}, u32[]{:S(2)}) collective-permute-start(bf16[32,2048]{1,0:T(8,128)(2,1)S(1)} %bitcast.288), channel_id=1, source_target_pairs={{0,3},{1,2},{2,1},{3,0},{4,7},{5,6},{6,5},{7,4},{8,11},{9,10},{10,... | collective-permute-start | bytes 393224 | tf_op jit(solution)/shard_map/ppermute | solution.py:27
  58.3 11.0 %collective-permute-start.5 = (bf16[128,2048]{1,0:T(8,128)(2,1)S(1)}, bf16[128,2048]{1,0:T(8,128)(2,1)}, u32[]{:S(2)}, u32[]{:S(2)}) collective-permute-start(bf16[128,2048]{1,0:T(8,128)(2,1)S(1)} %broadcast_add_fusion.1), channel_id=1, source_target_pairs={{0,16},{16,0},{1,17},{17,1},{2,18},{18,2},{3,19},{19,3},{4,20},{20... | collective-permute-start | bytes 1572872 | tf_op jit(solution)/shard_map/ppermute | solution.py:27
  59.8 6.9 %copy-start.3 = (bf16[512,1024]{1,0:T(8,128)(2,1)S(1)}, bf16[512,1024]{1,0:T(8,128)(2,1)}, u32[]{:S(2)}) copy-start(bf16[512,1024]{1,0:T(8,128)(2,1)} %copy-done.2) | copy-start | bytes 3145732
  67.8 6.3 %copy-start.6 = (bf16[128,2048]{1,0:T(8,128)(2,1)S(1)}, bf16[128,2048]{1,0:T(8,128)(2,1)}, u32[]{:S(2)}) copy-start(bf16[128,2048]{1,0:T(8,128)(2,1)} %param.11) | copy-start | bytes 1572868
  67.8 173.9 %all-gather.2.cloned.1.call-start = ((), (), s32[]{:S(2)}) async-start(), calls=%async_computation.4 | async-start | bytes 1310720 | tf_op jit(solution)/shard_map/all_gather | solution.py:204
  68.0 6.1 %copy-start.1 = (f32[128,2048]{1,0:T(8,128)S(1)}, f32[128,2048]{1,0:T(8,128)}, u32[]{:S(2)}) copy-start(f32[128,2048]{1,0:T(8,128)} %fusion.2) | copy-start | bytes 3145732
  74.3 9.9 %collective-permute-start.6 = (bf16[128,2048]{1,0:T(8,128)(2,1)S(1)}, bf16[128,2048]{1,0:T(8,128)(2,1)S(1)}, u32[]{:S(2)}, u32[]{:S(2)}) collective-permute-start(bf16[128,2048]{1,0:T(8,128)(2,1)S(1)} %subtract_convert_fusion), channel_id=1, source_target_pairs={{0,8},{4,12},{8,0},{12,4},{1,9},{5,13},{9,1},{13,5},{2,10},{6,14},... | collective-permute-start | bytes 1572872 | tf_op jit(solution)/shard_map/ppermute | solution.py:27
  85.3 10.4 %collective-permute-start.7 = (bf16[256,2048]{1,0:T(8,128)(2,1)}, bf16[256,2048]{1,0:T(8,128)(2,1)}, u32[]{:S(2)}, u32[]{:S(2)}) collective-permute-start(bf16[256,2048]{1,0:T(8,128)(2,1)} %pad_maximum_fusion.1), channel_id=1, source_target_pairs={{0,4},{4,0},{8,12},{12,8},{1,5},{5,1},{9,13},{13,9},{2,6},{6,2},{1... | collective-permute-start | bytes 3145736 | tf_op jit(solution)/shard_map/ppermute | solution.py:27
  95.8 12.4 %slice-start = ((s8[16777216]{0:T(1024)(128)(4,1)}), s8[4194304]{0:T(1024)(128)(4,1)S(1)}, s32[]{:S(2)}) async-start(s8[16777216]{0:T(1024)(128)(4,1)} %bitcast.236), calls=%async_computation.5 | async-start | bytes 8388608
  95.8 12.4 %slice-start.1 = ((s8[16777216]{0:T(1024)(128)(4,1)}), s8[4194304]{0:T(1024)(128)(4,1)S(1)}, s32[]{:S(2)}) async-start(s8[16777216]{0:T(1024)(128)(4,1)} %bitcast.236), calls=%async_computation.6 | async-start | bytes 8388608
  100.8 7.3 %slice-start.2 = ((s8[16777216]{0:T(1024)(128)(4,1)}), s8[4194304]{0:T(1024)(128)(4,1)S(1)}, s32[]{:S(2)}) async-start(s8[16777216]{0:T(1024)(128)(4,1)} %bitcast.236), calls=%async_computation.7 | async-start | bytes 8388608
  100.8 7.3 %slice-start.3 = ((s8[16777216]{0:T(1024)(128)(4,1)}), s8[4194304]{0:T(1024)(128)(4,1)S(1)}, s32[]{:S(2)}) async-start(s8[16777216]{0:T(1024)(128)(4,1)} %bitcast.236), calls=%async_computation.8 | async-start | bytes 8388608
  100.9 14.6 %collective-permute-start.8 = (bf16[256,1024]{1,0:T(8,128)(2,1)S(1)}, bf16[256,1024]{1,0:T(8,128)(2,1)S(1)}, u32[]{:S(2)}, u32[]{:S(2)}) collective-permute-start(bf16[256,1024]{1,0:T(8,128)(2,1)S(1)} %add_bitcast_fusion.2), channel_id=1, source_target_pairs={{0,16},{16,0},{1,17},{17,1},{2,18},{18,2},{3,19},{19,3},{4,20},{20... | collective-permute-start | bytes 1572872 | tf_op jit(solution)/shard_map/ppermute | solution.py:27
  108.0 14.9 %collective-permute-start.14 = (bf16[256,1024]{1,0:T(8,128)(2,1)S(1)}, bf16[256,1024]{1,0:T(8,128)(2,1)S(1)}, u32[]{:S(2)}, u32[]{:S(2)}) collective-permute-start(bf16[256,1024]{1,0:T(8,128)(2,1)S(1)} %dynamic-slice_bitcast_fusion), channel_id=1, source_target_pairs={{0,1},{1,0},{2,3},{3,2},{4,5},{5,4},{6,7},{7,6},{8,9},{9,8},{10,11... | collective-permute-start | bytes 1572872 | tf_op jit(solution)/shard_map/ppermute | solution.py:27
  115.8 11.9 %collective-permute-start.9 = (bf16[128,1024]{1,0:T(8,128)(2,1)S(1)}, bf16[128,1024]{1,0:T(8,128)(2,1)S(1)}, u32[]{:S(2)}, u32[]{:S(2)}) collective-permute-start(bf16[128,1024]{1,0:T(8,128)(2,1)S(1)} %dynamic-slice_bitcast_fusion.4), channel_id=1, source_target_pairs={{0,1},{1,0},{2,3},{3,2},{4,5},{5,4},{6,7},{7,6},{8,9},{9,8},{10,11... | collective-permute-start | bytes 786440 | tf_op jit(solution)/shard_map/ppermute | solution.py:27
  124.2 9.2 %collective-permute-start.15 = (bf16[128,1024]{1,0:T(8,128)(2,1)S(1)}, bf16[128,1024]{1,0:T(8,128)(2,1)S(1)}, u32[]{:S(2)}, u32[]{:S(2)}) collective-permute-start(bf16[128,1024]{1,0:T(8,128)(2,1)S(1)} %dynamic-slice_bitcast_fusion.3), channel_id=1, source_target_pairs={{0,16},{16,0},{1,17},{17,1},{2,18},{18,2},{3,19},{19,3},{4,20},{20... | collective-permute-start | bytes 786440 | tf_op jit(solution)/shard_map/ppermute | solution.py:27
  125.1 23.3 %collective-permute-start.20 = (bf16[256,1024]{1,0:T(8,128)(2,1)S(1)}, bf16[256,1024]{1,0:T(8,128)(2,1)S(1)}, u32[]{:S(2)}, u32[]{:S(2)}) collective-permute-start(bf16[256,1024]{1,0:T(8,128)(2,1)S(1)} %add_bitcast_fusion.1), channel_id=1, source_target_pairs={{0,16},{16,0},{1,17},{17,1},{2,18},{18,2},{3,19},{19,3},{4,20},{20... | collective-permute-start | bytes 1572872 | tf_op jit(solution)/shard_map/ppermute | solution.py:27
  127.6 21.7 %collective-permute-start.26 = (bf16[256,1024]{1,0:T(8,128)(2,1)S(1)}, bf16[256,1024]{1,0:T(8,128)(2,1)S(1)}, u32[]{:S(2)}, u32[]{:S(2)}) collective-permute-start(bf16[256,1024]{1,0:T(8,128)(2,1)S(1)} %add_bitcast_fusion), channel_id=1, source_target_pairs={{0,1},{1,0},{2,3},{3,2},{4,5},{5,4},{6,7},{7,6},{8,9},{9,8},{10,11... | collective-permute-start | bytes 1572872 | tf_op jit(solution)/shard_map/ppermute | solution.py:27
  127.8 14.2 %collective-permute-start.10 = (bf16[64,1024]{1,0:T(8,128)(2,1)S(1)}, bf16[64,1024]{1,0:T(8,128)(2,1)S(1)}, u32[]{:S(2)}, u32[]{:S(2)}) collective-permute-start(bf16[64,1024]{1,0:T(8,128)(2,1)S(1)} %dynamic-slice_bitcast_fusion.8), channel_id=1, source_target_pairs={{0,2},{1,3},{2,0},{3,1},{4,6},{5,7},{6,4},{7,5},{8,10},{9,11},{10,... | collective-permute-start | bytes 393224 | tf_op jit(solution)/shard_map/ppermute | solution.py:27
  133.6 12.2 %collective-permute-start.16 = (bf16[64,1024]{1,0:T(8,128)(2,1)S(1)}, bf16[64,1024]{1,0:T(8,128)(2,1)S(1)}, u32[]{:S(2)}, u32[]{:S(2)}) collective-permute-start(bf16[64,1024]{1,0:T(8,128)(2,1)S(1)} %dynamic-slice_bitcast_fusion.7), channel_id=1, source_target_pairs={{0,2},{1,3},{2,0},{3,1},{4,6},{5,7},{6,4},{7,5},{8,10},{9,11},{10,... | collective-permute-start | bytes 393224 | tf_op jit(solution)/shard_map/ppermute | solution.py:27
  142.3 8.6 %collective-permute-start.11 = (bf16[64,1024]{1,0:T(8,128)(2,1)S(1)}, bf16[64,1024]{1,0:T(8,128)(2,1)S(1)}, u32[]{:S(2)}, u32[]{:S(2)}) collective-permute-start(bf16[64,1024]{1,0:T(8,128)(2,1)S(1)} %get-tuple-element.5), channel_id=1, source_target_pairs={{0,2},{1,3},{2,0},{3,1},{4,6},{5,7},{6,4},{7,5},{8,10},{9,11},{10,... | collective-permute-start | bytes 393224 | tf_op jit(solution)/shard_map/ppermute | solution.py:27
  145.9 7.8 %collective-permute-start.17 = (bf16[64,1024]{1,0:T(8,128)(2,1)S(1)}, bf16[64,1024]{1,0:T(8,128)(2,1)S(1)}, u32[]{:S(2)}, u32[]{:S(2)}) collective-permute-start(bf16[64,1024]{1,0:T(8,128)(2,1)S(1)} %get-tuple-element.7), channel_id=1, source_target_pairs={{0,2},{1,3},{2,0},{3,1},{4,6},{5,7},{6,4},{7,5},{8,10},{9,11},{10,... | collective-permute-start | bytes 393224 | tf_op jit(solution)/shard_map/ppermute | solution.py:27
  148.6 12.0 %collective-permute-start.21 = (bf16[128,1024]{1,0:T(8,128)(2,1)S(1)}, bf16[128,1024]{1,0:T(8,128)(2,1)S(1)}, u32[]{:S(2)}, u32[]{:S(2)}) collective-permute-start(bf16[128,1024]{1,0:T(8,128)(2,1)S(1)} %dynamic-slice_bitcast_fusion.2), channel_id=1, source_target_pairs={{0,1},{1,0},{2,3},{3,2},{4,5},{5,4},{6,7},{7,6},{8,9},{9,8},{10,11... | collective-permute-start | bytes 786440 | tf_op jit(solution)/shard_map/ppermute | solution.py:27
  149.5 12.3 %collective-permute-start.27 = (bf16[128,1024]{1,0:T(8,128)(2,1)S(1)}, bf16[128,1024]{1,0:T(8,128)(2,1)S(1)}, u32[]{:S(2)}, u32[]{:S(2)}) collective-permute-start(bf16[128,1024]{1,0:T(8,128)(2,1)S(1)} %dynamic-slice_bitcast_fusion.1), channel_id=1, source_target_pairs={{0,16},{16,0},{1,17},{17,1},{2,18},{18,2},{3,19},{19,3},{4,20},{20... | collective-permute-start | bytes 786440 | tf_op jit(solution)/shard_map/ppermute | solution.py:27
  150.9 17.9 %collective-permute-start.12 = (bf16[128,1024]{1,0:T(8,128)(2,1)S(1)}, bf16[128,1024]{1,0:T(8,128)(2,1)S(1)}, u32[]{:S(2)}, u32[]{:S(2)}) collective-permute-start(bf16[128,1024]{1,0:T(8,128)(2,1)S(1)} %bitcast.270), channel_id=1, source_target_pairs={{0,1},{1,0},{2,3},{3,2},{4,5},{5,4},{6,7},{7,6},{8,9},{9,8},{10,11... | collective-permute-start | bytes 786440 | tf_op jit(solution)/shard_map/ppermute | solution.py:27
  153.7 15.2 %collective-permute-start.18 = (bf16[128,1024]{1,0:T(8,128)(2,1)S(1)}, bf16[128,1024]{1,0:T(8,128)(2,1)S(1)}, u32[]{:S(2)}, u32[]{:S(2)}) collective-permute-start(bf16[128,1024]{1,0:T(8,128)(2,1)S(1)} %bitcast.272), channel_id=1, source_target_pairs={{0,16},{16,0},{1,17},{17,1},{2,18},{18,2},{3,19},{19,3},{4,20},{20... | collective-permute-start | bytes 786440 | tf_op jit(solution)/shard_map/ppermute | solution.py:27
  160.6 8.8 %collective-permute-start.22 = (bf16[64,1024]{1,0:T(8,128)(2,1)S(1)}, bf16[64,1024]{1,0:T(8,128)(2,1)S(1)}, u32[]{:S(2)}, u32[]{:S(2)}) collective-permute-start(bf16[64,1024]{1,0:T(8,128)(2,1)S(1)} %dynamic-slice_bitcast_fusion.6), channel_id=1, source_target_pairs={{0,2},{1,3},{2,0},{3,1},{4,6},{5,7},{6,4},{7,5},{8,10},{9,11},{10,... | collective-permute-start | bytes 393224 | tf_op jit(solution)/shard_map/ppermute | solution.py:27
  161.9 9.6 %collective-permute-start.28 = (bf16[64,1024]{1,0:T(8,128)(2,1)S(1)}, bf16[64,1024]{1,0:T(8,128)(2,1)S(1)}, u32[]{:S(2)}, u32[]{:S(2)}) collective-permute-start(bf16[64,1024]{1,0:T(8,128)(2,1)S(1)} %dynamic-slice_bitcast_fusion.5), channel_id=1, source_target_pairs={{0,2},{1,3},{2,0},{3,1},{4,6},{5,7},{6,4},{7,5},{8,10},{9,11},{10,... | collective-permute-start | bytes 393224 | tf_op jit(solution)/shard_map/ppermute | solution.py:27
  168.9 27.0 %collective-permute-start.13 = (bf16[256,1024]{1,0:T(8,128)(2,1)S(1)}, bf16[256,1024]{1,0:T(8,128)(2,1)S(1)}, u32[]{:S(2)}, u32[]{:S(2)}) collective-permute-start(bf16[256,1024]{1,0:T(8,128)(2,1)S(1)} %bitcast.251), channel_id=1, source_target_pairs={{0,16},{16,0},{1,17},{17,1},{2,18},{18,2},{3,19},{19,3},{4,20},{20... | collective-permute-start | bytes 1572872 | tf_op jit(solution)/shard_map/ppermute | solution.py:27
  169.0 27.0 %collective-permute-start.19 = (bf16[256,1024]{1,0:T(8,128)(2,1)S(1)}, bf16[256,1024]{1,0:T(8,128)(2,1)S(1)}, u32[]{:S(2)}, u32[]{:S(2)}) collective-permute-start(bf16[256,1024]{1,0:T(8,128)(2,1)S(1)} %bitcast.253), channel_id=1, source_target_pairs={{0,1},{1,0},{2,3},{3,2},{4,5},{5,4},{6,7},{7,6},{8,9},{9,8},{10,11... | collective-permute-start | bytes 1572872 | tf_op jit(solution)/shard_map/ppermute | solution.py:27
  169.5 12.7 %collective-permute-start.23 = (bf16[64,1024]{1,0:T(8,128)(2,1)S(1)}, bf16[64,1024]{1,0:T(8,128)(2,1)S(1)}, u32[]{:S(2)}, u32[]{:S(2)}) collective-permute-start(bf16[64,1024]{1,0:T(8,128)(2,1)S(1)} %get-tuple-element.9), channel_id=1, source_target_pairs={{0,2},{1,3},{2,0},{3,1},{4,6},{5,7},{6,4},{7,5},{8,10},{9,11},{10,... | collective-permute-start | bytes 393224 | tf_op jit(solution)/shard_map/ppermute | solution.py:27
  171.6 14.2 %collective-permute-start.29 = (bf16[64,1024]{1,0:T(8,128)(2,1)S(1)}, bf16[64,1024]{1,0:T(8,128)(2,1)S(1)}, u32[]{:S(2)}, u32[]{:S(2)}) collective-permute-start(bf16[64,1024]{1,0:T(8,128)(2,1)S(1)} %get-tuple-element.3), channel_id=1, source_target_pairs={{0,2},{1,3},{2,0},{3,1},{4,6},{5,7},{6,4},{7,5},{8,10},{9,11},{10,... | collective-permute-start | bytes 393224 | tf_op jit(solution)/shard_map/ppermute | solution.py:27
  182.3 10.3 %collective-permute-start.24 = (bf16[128,1024]{1,0:T(8,128)(2,1)S(1)}, bf16[128,1024]{1,0:T(8,128)(2,1)S(1)}, u32[]{:S(2)}, u32[]{:S(2)}) collective-permute-start(bf16[128,1024]{1,0:T(8,128)(2,1)S(1)} %bitcast.274), channel_id=1, source_target_pairs={{0,1},{1,0},{2,3},{3,2},{4,5},{5,4},{6,7},{7,6},{8,9},{9,8},{10,11... | collective-permute-start | bytes 786440 | tf_op jit(solution)/shard_map/ppermute | solution.py:27
  185.8 9.3 %collective-permute-start.30 = (bf16[128,1024]{1,0:T(8,128)(2,1)S(1)}, bf16[128,1024]{1,0:T(8,128)(2,1)S(1)}, u32[]{:S(2)}, u32[]{:S(2)}) collective-permute-start(bf16[128,1024]{1,0:T(8,128)(2,1)S(1)} %bitcast.268), channel_id=1, source_target_pairs={{0,16},{16,0},{1,17},{17,1},{2,18},{18,2},{3,19},{19,3},{4,20},{20... | collective-permute-start | bytes 786440 | tf_op jit(solution)/shard_map/ppermute | solution.py:27
  192.6 9.2 %collective-permute-start.25 = (bf16[256,1024]{1,0:T(8,128)(2,1)S(1)}, bf16[256,1024]{1,0:T(8,128)(2,1)S(1)}, u32[]{:S(2)}, u32[]{:S(2)}) collective-permute-start(bf16[256,1024]{1,0:T(8,128)(2,1)S(1)} %bitcast.255), channel_id=1, source_target_pairs={{0,16},{16,0},{1,17},{17,1},{2,18},{18,2},{3,19},{19,3},{4,20},{20... | collective-permute-start | bytes 1572872 | tf_op jit(solution)/shard_map/ppermute | solution.py:27
  195.2 9.3 %collective-permute-start.31 = (bf16[256,1024]{1,0:T(8,128)(2,1)S(1)}, bf16[256,1024]{1,0:T(8,128)(2,1)S(1)}, u32[]{:S(2)}, u32[]{:S(2)}) collective-permute-start(bf16[256,1024]{1,0:T(8,128)(2,1)S(1)} %bitcast.257), channel_id=1, source_target_pairs={{0,1},{1,0},{2,3},{3,2},{4,5},{5,4},{6,7},{7,6},{8,9},{9,8},{10,11... | collective-permute-start | bytes 1572872 | tf_op jit(solution)/shard_map/ppermute | solution.py:27
  205.8 4.0 %collective-permute-start.32 = (bf16[256,2048]{1,0:T(8,128)(2,1)S(1)}, bf16[256,2048]{1,0:T(8,128)(2,1)S(1)}, u32[]{:S(2)}, u32[]{:S(2)}) collective-permute-start(bf16[256,2048]{1,0:T(8,128)(2,1)S(1)} %fusion.52), channel_id=1, source_target_pairs={{0,4},{4,0},{8,12},{12,8},{1,5},{5,1},{9,13},{13,9},{2,6},{6,2},{1... | collective-permute-start | bytes 3145736 | tf_op jit(solution)/shard_map/ppermute | solution.py:27
  209.8 5.0 %copy-start.7 = (bf16[4,32,1024]{2,1,0:T(8,128)(2,1)S(1)}, bf16[4,32,1024]{2,1,0:T(8,128)(2,1)}, u32[]{:S(2)}) copy-start(bf16[4,32,1024]{2,1,0:T(8,128)(2,1)} %reduce-scatter.2.cloned.1.call-done) | copy-start | bytes 786436
  212.1 14.6 %collective-permute-start.33 = (bf16[128,2048]{1,0:T(8,128)(2,1)}, bf16[128,2048]{1,0:T(8,128)(2,1)}, u32[]{:S(2)}, u32[]{:S(2)}) collective-permute-start(bf16[128,2048]{1,0:T(8,128)(2,1)} %slice.205), channel_id=1, source_target_pairs={{0,8},{4,12},{8,0},{12,4},{1,9},{5,13},{9,1},{13,5},{2,10},{6,14},... | collective-permute-start | bytes 1572872 | tf_op jit(solution)/shard_map/ppermute | solution.py:27
  227.9 3.9 %copy-start.5 = (bf16[128,2048]{1,0:T(8,128)(2,1)}, bf16[128,2048]{1,0:T(8,128)(2,1)S(1)}, u32[]{:S(2)}) copy-start(bf16[128,2048]{1,0:T(8,128)(2,1)S(1)} %add_convert_fusion.1) | copy-start | bytes 1572868
  231.6 13.8 %collective-permute-start.34 = (bf16[4,128,512]{2,1,0:T(8,128)(2,1)}, bf16[4,128,512]{2,1,0:T(8,128)(2,1)S(1)}, u32[]{:S(2)}, u32[]{:S(2)}) collective-permute-start(bf16[4,128,512]{2,1,0:T(8,128)(2,1)} %convolution_convert_fusion.2), channel_id=1, source_target_pairs={{0,16},{16,0},{1,17},{17,1},{2,18},{18,2},{3,19},{19,3},{4,20},{20... | collective-permute-start | bytes 1572872 | tf_op jit(solution)/shard_map/ppermute | solution.py:27
  265.9 15.6 %copy-start.4 = (bf16[512,1024]{1,0:T(8,128)(2,1)S(1)}, bf16[512,1024]{1,0:T(8,128)(2,1)}, u32[]{:S(2)}) copy-start(bf16[512,1024]{1,0:T(8,128)(2,1)} %param.9) | copy-start | bytes 3145732
  265.9 7.1 %collective-permute-start.35 = (bf16[4,32,512]{2,1,0:T(8,128)(2,1)S(1)}, bf16[4,32,512]{2,1,0:T(8,128)(2,1)S(1)}, u32[]{:S(2)}, u32[]{:S(2)}) collective-permute-start(bf16[4,32,512]{2,1,0:T(8,128)(2,1)S(1)} %pad_maximum_fusion.5), channel_id=1, source_target_pairs={{0,1},{1,0},{2,3},{3,2},{4,5},{5,4},{6,7},{7,6},{8,9},{9,8},{10,11... | collective-permute-start | bytes 393224 | tf_op jit(solution)/shard_map/ppermute | solution.py:27
  268.5 12.9 %collective-permute-start.36 = (bf16[4,32,512]{2,1,0:T(8,128)(2,1)S(1)}, bf16[4,32,512]{2,1,0:T(8,128)(2,1)S(1)}, u32[]{:S(2)}, u32[]{:S(2)}) collective-permute-start(bf16[4,32,512]{2,1,0:T(8,128)(2,1)S(1)} %pad_maximum_fusion.5), channel_id=1, source_target_pairs={{0,2},{1,3},{2,0},{3,1},{4,6},{5,7},{6,4},{7,5},{8,10},{9,11},{10,... | collective-permute-start | bytes 393224 | tf_op jit(solution)/shard_map/ppermute | solution.py:27
  270.0 11.5 %collective-permute-start.37 = (bf16[4,32,512]{2,1,0:T(8,128)(2,1)S(1)}, bf16[4,32,512]{2,1,0:T(8,128)(2,1)S(1)}, u32[]{:S(2)}, u32[]{:S(2)}) collective-permute-start(bf16[4,32,512]{2,1,0:T(8,128)(2,1)S(1)} %pad_maximum_fusion.5), channel_id=1, source_target_pairs={{0,3},{1,2},{2,1},{3,0},{4,7},{5,6},{6,5},{7,4},{8,11},{9,10},{10,... | collective-permute-start | bytes 393224 | tf_op jit(solution)/shard_map/ppermute | solution.py:27
  282.3 2.0 collective-permute-start.38
  284.5 8.4 %collective-permute-start.39 = (bf16[128,1024]{1,0:T(8,128)(2,1)S(1)}, bf16[128,1024]{1,0:T(8,128)(2,1)S(1)}, u32[]{:S(2)}, u32[]{:S(2)}) collective-permute-start(bf16[128,1024]{1,0:T(8,128)(2,1)S(1)} %slice.210), channel_id=1, source_target_pairs={{0,8},{4,12},{8,0},{12,4},{1,9},{5,13},{9,1},{13,5},{2,10},{6,14},... | collective-permute-start | bytes 786440 | tf_op jit(solution)/shard_map/ppermute | solution.py:27
Sparse Core Ops, SparseCore 0:
  67.9 26.0 reduce-scatter.1
  215.7 25.9 all-gather.1

commit v5 on v4

--- a/solution.py
+++ b/solution.py
@@ -216,10 +216,25 @@
     got = lax.all_to_all(sent, ("wide", "narrow"), 0, 0, tiled=True)
     got = got.reshape(wide_count, narrow_count, small, border_block)
     own = jnp.sum(got.astype(jnp.float32), axis=1).astype(jnp.bfloat16)
-    returned = direct_gather(by_relation(own), "narrow", 1).reshape(wide_count * rows, border_block)
-
-    back_leaf = times(leaf_mid, leaf_factor) - times(returned, leaf_coupling)
-    leaf_solution = relative_scatter(back_leaf, "wide")
+    own = by_relation(own)
+    pieces = [swap(own, "narrow", k) if k else own for k in range(narrow_count)]
+    middles = leaf_mid.reshape(wide_count, narrow_count, small, -1)
+    leaf_solution = jnp.zeros((narrow_count, small, leaf_factor.shape[1]), jnp.bfloat16)
+    group = max(1, narrow_count // 2)
+    for first in range(0, narrow_count, group):
+        near = range(first, first + group)
+        returned = jnp.concatenate([pieces[k] for k in near], axis=1)
+        middle = jnp.concatenate(
+            [lax.dynamic_index_in_dim(middles, narrow_index ^ k, 1, keepdims=False) for k in near], axis=1
+        )
+        height = wide_count * group * small
+        back_leaf = times(middle.reshape(height, -1), leaf_factor) - times(
+            returned.reshape(height, -1), leaf_coupling
+        )
+        part = relative_scatter(back_leaf, "wide").reshape(group, small, -1)
+        for k in near:
+            leaf_solution = lax.dynamic_update_index_in_dim(leaf_solution, part[k - first], narrow_index ^ k, 0)
+    leaf_solution = leaf_solution.reshape(rows, -1)
     return (leaf_solution, root_solution)
 
 

time: 307 us -> 306 us (level)
  blocking collectives: 20.2 us -> 0 us
  waiting for transfers between devices: 120 us -> 130 us
  starting transfers between devices: 52.8 us -> 58.7 us
    all_to_all x1 -> x0, blocking collectives: 20.2 us -> none  [body(): got = lax.all_to_all(sent, ('wide', 'narrow'), 0, 0, tiled=True)]
    all_to_all x1 -> x2, waiting for transfers between devices: 2.85 us -> 15.8 us  [body(): got = lax.all_to_all(sent, ('wide', 'narrow'), 0, 0, tiled=True)]
    all_to_all x1 -> x2, starting transfers between devices: 6.15 us -> 10.7 us  [body(): got = lax.all_to_all(sent, ('wide', 'narrow'), 0, 0, tiled=True)]
    ppermute x40 -> x42, waiting for transfers between devices: 102 us -> 99 us  [swap(): return lax.ppermute(value, axis, pairs)]
    ppermute x40 -> x42, starting transfers between devices: 46.4 us -> 47.8 us  [swap(): return lax.ppermute(value, axis, pairs)]
    dot_general x12 -> x14, matrix products: 24.3 us -> 24.4 us  [times(): return jnp.dot(left, right, preferred_element_type=jnp.float32)]
  transfers between devices with their start and end apart: 43 -> 46, of which waited for: 26 -> 28; matrix products, arithmetic and copies ran while one was open for 24% -> 25% of each run, Pallas kernels for 0% -> 0%
where the time goes in v5:
time: 306 us; the launch traced here: 300 us
  waiting for transfers between devices  130 us (42%)
  starting transfers between devices  58.7 us (19%)
  matrix products  53.9 us (18%)
  between operations  20.5 us (7%)
  other arithmetic  19 us (6%)
  local copies, waits for them, and re-layouts  18.4 us (6%)
    ppermute x42, waiting for transfers between devices, swap(): return lax.ppermute(value, axis, pairs)  99 us
    ppermute x42, starting transfers between devices, swap(): return lax.ppermute(value, axis, pairs)  47.8 us
    dot_general x14, matrix products, times(): return jnp.dot(left, right, preferred_element_type=jnp.float32)  24.4 us
    dot_general x6, matrix products, times_transposed(): lax.dot_general(left, right, (((1,), (1,)), ((), ())), preferred_element_...  22.8 us
    all_to_all x2, waiting for transfers between devices, body(): got = lax.all_to_all(sent, ('wide', 'narrow'), 0, 0, tiled=True)  15.8 us
    all_to_all x2, starting transfers between devices, body(): got = lax.all_to_all(sent, ('wide', 'narrow'), 0, 0, tiled=True)  10.7 us
    reduce_scatter x1, waiting for transfers between devices, body(): lax.psum_scatter(pivot_terms, 'narrow', scatter_dimension=1, tiled=True)  8.49 us
    eq x1, other arithmetic, body(): landing = (near_map[:, :, None] == columns).astype(jnp.bfloat16)  7.31 us
  transfers between devices with their start and end apart: 46, of which 28 were waited for; matrix products, arithmetic and copies ran while one was open for 25% of the time, Pallas kernels for 0%

profile of v5, /device:TPU:0, one launch (start us, length us, event | category | flops | bytes accessed | tf_op | source)
XLA Modules:
  0.0 300.4 jit_solution(16385931855675147618)
XLA Ops:
  7.2 3.0 %collective-permute-start = (bf16[128,1024]{1,0:T(8,128)(2,1)}, bf16[128,1024]{1,0:T(8,128)(2,1)S(1)}, u32[]{:S(2)}, u32[]{:S(2)}) collective-permute-start(bf16[128,1024]{1,0:T(8,128)(2,1)} %param.7), channel_id=1, source_target_pairs={{0,8},{4,12},{8,0},{12,4},{1,9},{5,13},{9,1},{13,5},{2,10},{6,14},... | collective-permute-start | bytes 786440 | tf_op jit(solution)/shard_map/ppermute | solution.py:27
  12.0 4.7 %collective-permute-done = bf16[128,1024]{1,0:T(8,128)(2,1)S(1)} collective-permute-done((bf16[128,1024]{1,0:T(8,128)(2,1)}, bf16[128,1024]{1,0:T(8,128)(2,1)S(1)}, u32[]{:S(2)}, u32[]{:S(2)}) %collective-permute-start) | collective-permute-done | bytes 262176 | tf_op jit(solution)/shard_map/ppermute | solution.py:27
  17.9 1.8 collective-permute-done.1
  19.7 2.3 convolution_convert_fusion.3
  23.1 6.2 %all-to-all-start = ((bf16[16,32,512]{2,1,0:T(8,128)(2,1)}), bf16[16,32,512]{2,1,0:T(8,128)(2,1)S(1)}, u32[]{:S(2)}, u32[]{:S(2)}) async-start(bf16[16,32,512]{2,1,0:T(8,128)(2,1)} %bitcast.5), calls=%async_computation | async-start | bytes 1048576 | tf_op jit(solution)/shard_map/all_to_all | solution.py:179
  29.3 7.3 %broadcast_compare_fusion = pred[2,2048,2048]{2,1,0:T(8,128)(4,1)} fusion(s32[2048]{0:T(1024)S(1)} %iota_add_fusion, s32[2,2048]{1,0:T(2,128)S(1)} %pad_add_fusion), kind=kLoop, calls=%fused_computation | loop fusion | flops 8388608 | bytes 8413184 | tf_op jit(solution)/shard_map/eq | solution.py:156
  38.4 2.5 convolution_convert_fusion
  42.0 3.0 all-to-all-done
  45.2 1.4 collective-permute-start.3
  46.6 2.9 collective-permute-start.4
  49.8 2.2 collective-permute-done.2
  52.0 6.2 %collective-permute-done.3 = bf16[32,2048]{1,0:T(8,128)(2,1)S(1)} collective-permute-done((bf16[32,2048]{1,0:T(8,128)(2,1)S(1)}, bf16[32,2048]{1,0:T(8,128)(2,1)S(1)}, u32[]{:S(2)}, u32[]{:S(2)}) %collective-permute-start.3) | collective-permute-done | bytes 131104 | tf_op jit(solution)/shard_map/ppermute | solution.py:27
  58.3 1.6 collective-permute-start.5
  59.9 5.8 %fusion.2 = f32[128,2048]{1,0:T(8,128)} fusion(bf16[128,2048]{1,0:T(8,128)(2,1)S(1)} %bitcast.269, pred[2,2048,2048]{2,1,0:T(8,128)(4,1)} %broadcast_compare_fusion), kind=kOutput, calls=%fused_computation.3 | convolution fusion | flops 1073741824 | bytes 5767168 | tf_op jit(solution)/shard_map/dot_general | solution.py:16
  69.3 4.9 %fusion = f32[128,2048]{1,0:T(8,128)S(1)} fusion(bf16[128,2048]{1,0:T(8,128)(2,1)} %collective-permute-done.5, pred[2,2048,2048]{2,1,0:T(8,128)(4,1)} %broadcast_compare_fusion), kind=kOutput, calls=%fused_computation.1 | convolution fusion | flops 1073741824 | bytes 5767168 | tf_op jit(solution)/shard_map/dot_general | solution.py:16
  74.4 1.4 collective-permute-start.6
  75.8 8.5 %collective-permute-done.6 = bf16[128,2048]{1,0:T(8,128)(2,1)S(1)} collective-permute-done((bf16[128,2048]{1,0:T(8,128)(2,1)S(1)}, bf16[128,2048]{1,0:T(8,128)(2,1)S(1)}, u32[]{:S(2)}, u32[]{:S(2)}) %collective-permute-start.6) | collective-permute-done | bytes 524320 | tf_op jit(solution)/shard_map/ppermute | solution.py:27
  85.4 8.5 %reduce-scatter.2.cloned.1.call-done = bf16[4,32,1024]{2,1,0:T(8,128)(2,1)} async-done(((bf16[4,128,1024]{2,1,0:T(8,128)(2,1)}), bf16[4,32,1024]{2,1,0:T(8,128)(2,1)}) %reduce-scatter.2.cloned.1.call-update) | async-done | bytes 262160 | tf_op jit(solution)/shard_map/reduce_scatter | solution.py:190
  95.7 5.0 %fusion.55 = bf16[512,1024]{1,0:T(8,128)(2,1)S(1)} fusion(bf16[4096,2048]{1,0:T(8,128)(2,1)} %param.10, bf16[256,2048]{1,0:T(8,128)(2,1)} %collective-permute-done.7, bf16[128,2048]{1,0:T(8,128)(2,1)S(1)} %collective-permute-done.6, bf16[128,2048]{1,0:T(8,128)(2,1)S(1)} %subtract_convert_fusion), kind=kOutput, calls=%fused_computation.40 | convolution fusion | flops 2154299392 | bytes 7340032 | tf_op jit(solution)/shard_map/dot_general | solution.py:10
  100.8 1.5 collective-permute-start.8
  102.3 5.6 %fusion.58 = bf16[512,1024]{1,0:T(8,128)(2,1)S(1)} fusion(bf16[4096,2048]{1,0:T(8,128)(2,1)} %param.10, bf16[256,2048]{1,0:T(8,128)(2,1)} %collective-permute-done.7, bf16[128,2048]{1,0:T(8,128)(2,1)S(1)} %collective-permute-done.6, bf16[128,2048]{1,0:T(8,128)(2,1)S(1)} %subtract_convert_fusion), kind=kOutput, calls=%fused_computation.41 | convolution fusion | flops 2154299392 | bytes 7340032 | tf_op jit(solution)/shard_map/dot_general | solution.py:10
  108.1 3.7 %fusion.61 = bf16[512,1024]{1,0:T(8,128)(2,1)S(1)} fusion(bf16[4096,2048]{1,0:T(8,128)(2,1)S(1)} %bitcast.256, bf16[256,2048]{1,0:T(8,128)(2,1)} %collective-permute-done.7, bf16[128,2048]{1,0:T(8,128)(2,1)S(1)} %collective-permute-done.6, bf16[128,2048]{1,0:T(8,128)(2,1)S(1)} %subtract_convert_fusion), kind=kOutput, calls=%fused_computation.42 | convolution fusion | flops 2154299392 | bytes 7340032 | tf_op jit(solution)/shard_map/dot_general | solution.py:10
  111.8 3.7 %fusion.64 = bf16[512,1024]{1,0:T(8,128)(2,1)S(1)} fusion(bf16[4096,2048]{1,0:T(8,128)(2,1)S(1)} %bitcast.256, bf16[256,2048]{1,0:T(8,128)(2,1)} %collective-permute-done.7, bf16[128,2048]{1,0:T(8,128)(2,1)S(1)} %collective-permute-done.6, bf16[128,2048]{1,0:T(8,128)(2,1)S(1)} %subtract_convert_fusion), kind=kOutput, calls=%fused_computation.43 | convolution fusion | flops 2154299392 | bytes 7340032 | tf_op jit(solution)/shard_map/dot_general | solution.py:10
  115.7 2.0 collective-permute-start.9
  117.7 5.2 %collective-permute-done.14 = bf16[256,1024]{1,0:T(8,128)(2,1)S(1)} collective-permute-done((bf16[256,1024]{1,0:T(8,128)(2,1)S(1)}, bf16[256,1024]{1,0:T(8,128)(2,1)S(1)}, u32[]{:S(2)}, u32[]{:S(2)}) %collective-permute-start.14) | collective-permute-done | bytes 524320 | tf_op jit(solution)/shard_map/ppermute | solution.py:27
  125.0 1.9 collective-permute-start.20
  127.7 1.7 collective-permute-start.10
  129.4 4.0 %collective-permute-done.15 = bf16[128,1024]{1,0:T(8,128)(2,1)S(1)} collective-permute-done((bf16[128,1024]{1,0:T(8,128)(2,1)S(1)}, bf16[128,1024]{1,0:T(8,128)(2,1)S(1)}, u32[]{:S(2)}, u32[]{:S(2)}) %collective-permute-start.15) | collective-permute-done | bytes 262176 | tf_op jit(solution)/shard_map/ppermute | solution.py:27
  134.6 7.3 %collective-permute-done.10 = bf16[64,1024]{1,0:T(8,128)(2,1)S(1)} collective-permute-done((bf16[64,1024]{1,0:T(8,128)(2,1)S(1)}, bf16[64,1024]{1,0:T(8,128)(2,1)S(1)}, u32[]{:S(2)}, u32[]{:S(2)}) %collective-permute-start.10) | collective-permute-done | bytes 131104 | tf_op jit(solution)/shard_map/ppermute | solution.py:27
  142.2 3.5 %collective-permute-start.11 = (bf16[64,1024]{1,0:T(8,128)(2,1)S(1)}, bf16[64,1024]{1,0:T(8,128)(2,1)S(1)}, u32[]{:S(2)}, u32[]{:S(2)}) collective-permute-start(bf16[64,1024]{1,0:T(8,128)(2,1)S(1)} %get-tuple-element.5), channel_id=1, source_target_pairs={{0,2},{1,3},{2,0},{3,1},{4,6},{5,7},{6,4},{7,5},{8,10},{9,11},{10,... | collective-permute-start | bytes 393224 | tf_op jit(solution)/shard_map/ppermute | solution.py:27
  145.8 2.5 collective-permute-start.17
  150.8 2.5 collective-permute-start.12
  153.9 6.5 %collective-permute-done.21 = bf16[128,1024]{1,0:T(8,128)(2,1)S(1)} collective-permute-done((bf16[128,1024]{1,0:T(8,128)(2,1)S(1)}, bf16[128,1024]{1,0:T(8,128)(2,1)S(1)}, u32[]{:S(2)}, u32[]{:S(2)}) %collective-permute-start.21) | collective-permute-done | bytes 262176 | tf_op jit(solution)/shard_map/ppermute | solution.py:27
  161.9 1.8 collective-permute-start.28
  163.7 4.7 %collective-permute-done.12 = bf16[128,1024]{1,0:T(8,128)(2,1)S(1)} collective-permute-done((bf16[128,1024]{1,0:T(8,128)(2,1)S(1)}, bf16[128,1024]{1,0:T(8,128)(2,1)S(1)}, u32[]{:S(2)}, u32[]{:S(2)}) %collective-permute-start.12) | collective-permute-done | bytes 262176 | tf_op jit(solution)/shard_map/ppermute | solution.py:27
  169.0 1.8 collective-permute-start.23
  172.2 10.0 %collective-permute-done.23 = bf16[64,1024]{1,0:T(8,128)(2,1)S(1)} collective-permute-done((bf16[64,1024]{1,0:T(8,128)(2,1)S(1)}, bf16[64,1024]{1,0:T(8,128)(2,1)S(1)}, u32[]{:S(2)}, u32[]{:S(2)}) %collective-permute-start.23) | collective-permute-done | bytes 131104 | tf_op jit(solution)/shard_map/ppermute | solution.py:27
  182.2 3.5 %collective-permute-start.24 = (bf16[128,1024]{1,0:T(8,128)(2,1)S(1)}, bf16[128,1024]{1,0:T(8,128)(2,1)S(1)}, u32[]{:S(2)}, u32[]{:S(2)}) collective-permute-start(bf16[128,1024]{1,0:T(8,128)(2,1)S(1)} %bitcast.295), channel_id=1, source_target_pairs={{0,1},{1,0},{2,3},{3,2},{4,5},{5,4},{6,7},{7,6},{8,9},{9,8},{10,11... | collective-permute-start | bytes 786440 | tf_op jit(solution)/shard_map/ppermute | solution.py:27
  186.1 6.3 %collective-permute-done.24 = bf16[128,1024]{1,0:T(8,128)(2,1)S(1)} collective-permute-done((bf16[128,1024]{1,0:T(8,128)(2,1)S(1)}, bf16[128,1024]{1,0:T(8,128)(2,1)S(1)}, u32[]{:S(2)}, u32[]{:S(2)}) %collective-permute-start.24) | collective-permute-done | bytes 262176 | tf_op jit(solution)/shard_map/ppermute | solution.py:27
  192.5 2.5 collective-permute-done.30
  196.5 1.3 fusion.18
  197.8 4.2 %collective-permute-done.25 = bf16[256,1024]{1,0:T(8,128)(2,1)S(1)} collective-permute-done((bf16[256,1024]{1,0:T(8,128)(2,1)S(1)}, bf16[256,1024]{1,0:T(8,128)(2,1)S(1)}, u32[]{:S(2)}, u32[]{:S(2)}) %collective-permute-start.25) | collective-permute-done | bytes 524320 | tf_op jit(solution)/shard_map/ppermute | solution.py:27
  203.4 1.3 fusion.46
  204.8 1.3 fusion.52
  206.1 1.3 fusion.16
  207.4 1.3 fusion.10
  208.7 1.3 fusion.43
  210.1 1.4 fusion.49
  212.3 1.3 collective-permute-start.33
  215.5 6.1 %fusion.94 = (pred[1,2048,2048]{2,1,0:T(32,128)(4,1)S(1)}, pred[1,2048,2048]{2,1,0:T(32,128)(4,1)S(1)}) fusion(pred[2,2048,2048]{2,1,0:T(8,128)(4,1)} %broadcast_compare_fusion), kind=kLoop, calls=%fused_computation.185 | loop fusion | bytes 16777216 | tf_op jit(solution)/shard_map/slice | solution.py:193
  221.6 5.4 %collective-permute-done.33 = bf16[128,2048]{1,0:T(8,128)(2,1)} collective-permute-done((bf16[128,2048]{1,0:T(8,128)(2,1)}, bf16[128,2048]{1,0:T(8,128)(2,1)}, u32[]{:S(2)}, u32[]{:S(2)}) %collective-permute-start.33) | collective-permute-done | bytes 524320 | tf_op jit(solution)/shard_map/ppermute | solution.py:27
  228.1 3.7 %convolution_convert_fusion.2 = bf16[4,128,512]{2,1,0:T(8,128)(2,1)} fusion(pred[4,512,2048]{2,1,0:T(32,128)(4,1)S(1)} %bitcast.258, bf16[128,2048]{1,0:T(8,128)(2,1)S(1)} %add_convert_fusion.1), kind=kOutput, calls=%fused_computation.47 | convolution fusion | flops 1074003968 | bytes 5242880 | tf_op jit(solution)/shard_map/dot_general | solution.py:210
  232.2 2.9 convolution_convert_fusion.1
  235.1 6.6 %all-gather.2.cloned.1.call-done = bf16[4,128,1024]{2,1,0:T(8,128)(2,1)} async-done(((bf16[4,32,1024]{2,1,0:T(8,128)(2,1)}), bf16[4,128,1024]{2,1,0:T(8,128)(2,1)}) %all-gather.2.cloned.1.call-update) | async-done | bytes 1048592 | tf_op jit(solution)/shard_map/all_gather | solution.py:204
  243.5 2.2 collective-permute-done.34
  246.6 4.5 %all-to-all-start.1 = ((bf16[16,32,512]{2,1,0:T(8,128)(2,1)}), bf16[16,32,512]{2,1,0:T(8,128)(2,1)}, u32[]{:S(2)}, u32[]{:S(2)}) async-start(bf16[16,32,512]{2,1,0:T(8,128)(2,1)} %bitcast.105), calls=%async_computation.2 | async-start | bytes 1048576 | tf_op jit(solution)/shard_map/all_to_all | solution.py:216
  251.1 1.3 dynamic-slice_bitcast_fusion.2
  254.0 12.8 %all-to-all-done.1 = bf16[16,32,512]{2,1,0:T(8,128)(2,1)} async-done(((bf16[16,32,512]{2,1,0:T(8,128)(2,1)}), bf16[16,32,512]{2,1,0:T(8,128)(2,1)}, u32[]{:S(2)}, u32[]{:S(2)}) %all-to-all-start.1) | async-done | bytes 524320 | tf_op jit(solution)/shard_map/all_to_all | solution.py:216
  268.2 1.7 fusion.95
  269.9 1.5 collective-permute-start.38
  271.4 2.9 collective-permute-start.39
  275.0 7.9 %collective-permute-done.38 = bf16[4,32,512]{2,1,0:T(8,128)(2,1)S(1)} collective-permute-done((bf16[4,32,512]{2,1,0:T(8,128)(2,1)S(1)}, bf16[4,32,512]{2,1,0:T(8,128)(2,1)S(1)}, u32[]{:S(2)}, u32[]{:S(2)}) %collective-permute-start.38) | collective-permute-done | bytes 131104 | tf_op jit(solution)/shard_map/ppermute | solution.py:27
  286.4 3.6 %collective-permute-done.37 = bf16[64,1024]{1,0:T(8,128)(2,1)S(1)} collective-permute-done((bf16[64,1024]{1,0:T(8,128)(2,1)S(1)}, bf16[64,1024]{1,0:T(8,128)(2,1)S(1)}, u32[]{:S(2)}, u32[]{:S(2)}) %collective-permute-start.37) | collective-permute-done | bytes 131104 | tf_op jit(solution)/shard_map/ppermute | solution.py:27
  290.1 2.3 collective-permute-done.41
  (197 shorter events, 38.3 us)
Async XLA Ops:
  7.2 31.2 %copy-start = (bf16[1024,1024]{1,0:T(8,128)(2,1)S(1)}, bf16[1024,1024]{1,0:T(8,128)(2,1)}, u32[]{:S(2)}) copy-start(bf16[1024,1024]{1,0:T(8,128)(2,1)} %param.8) | copy-start | bytes 6291460
  7.2 9.6 %collective-permute-start = (bf16[128,1024]{1,0:T(8,128)(2,1)}, bf16[128,1024]{1,0:T(8,128)(2,1)S(1)}, u32[]{:S(2)}, u32[]{:S(2)}) collective-permute-start(bf16[128,1024]{1,0:T(8,128)(2,1)} %param.7), channel_id=1, source_target_pairs={{0,8},{4,12},{8,0},{12,4},{1,9},{5,13},{9,1},{13,5},{2,10},{6,14},... | collective-permute-start | bytes 786440 | tf_op jit(solution)/shard_map/ppermute | solution.py:27
  17.7 2.0 collective-permute-start.1
  19.7 3.4 %copy-start.9 = (bf16[512,1024]{1,0:T(8,128)(2,1)}, bf16[512,1024]{1,0:T(8,128)(2,1)S(1)}, u32[]{:S(2)}) copy-start(bf16[512,1024]{1,0:T(8,128)(2,1)S(1)} %constant_dynamic-update-slice_fusion.1) | copy-start | bytes 3145732
  23.1 21.8 %all-to-all-start = ((bf16[16,32,512]{2,1,0:T(8,128)(2,1)}), bf16[16,32,512]{2,1,0:T(8,128)(2,1)S(1)}, u32[]{:S(2)}, u32[]{:S(2)}) async-start(bf16[16,32,512]{2,1,0:T(8,128)(2,1)} %bitcast.5), calls=%async_computation | async-start | bytes 1048576 | tf_op jit(solution)/shard_map/all_to_all | solution.py:179
  29.3 64.6 %reduce-scatter.2.cloned.1.call-start = ((), (), s32[]{:S(2)}) async-start(), calls=%async_computation.3 | async-start | bytes 1310720 | tf_op jit(solution)/shard_map/reduce_scatter | solution.py:190
  40.9 1.1 copy-start.3
  45.1 6.9 %collective-permute-start.2 = (bf16[32,2048]{1,0:T(8,128)(2,1)S(1)}, bf16[32,2048]{1,0:T(8,128)(2,1)S(1)}, u32[]{:S(2)}, u32[]{:S(2)}) collective-permute-start(bf16[32,2048]{1,0:T(8,128)(2,1)S(1)} %bitcast.310), channel_id=1, source_target_pairs={{0,1},{1,0},{2,3},{3,2},{4,5},{5,4},{6,7},{7,6},{8,9},{9,8},{10,11... | collective-permute-start | bytes 393224 | tf_op jit(solution)/shard_map/ppermute | solution.py:27
  45.2 13.0 %collective-permute-start.3 = (bf16[32,2048]{1,0:T(8,128)(2,1)S(1)}, bf16[32,2048]{1,0:T(8,128)(2,1)S(1)}, u32[]{:S(2)}, u32[]{:S(2)}) collective-permute-start(bf16[32,2048]{1,0:T(8,128)(2,1)S(1)} %bitcast.311), channel_id=1, source_target_pairs={{0,2},{1,3},{2,0},{3,1},{4,6},{5,7},{6,4},{7,5},{8,10},{9,11},{10,... | collective-permute-start | bytes 393224 | tf_op jit(solution)/shard_map/ppermute | solution.py:27
  46.6 11.6 %collective-permute-start.4 = (bf16[32,2048]{1,0:T(8,128)(2,1)S(1)}, bf16[32,2048]{1,0:T(8,128)(2,1)S(1)}, u32[]{:S(2)}, u32[]{:S(2)}) collective-permute-start(bf16[32,2048]{1,0:T(8,128)(2,1)S(1)} %bitcast.312), channel_id=1, source_target_pairs={{0,3},{1,2},{2,1},{3,0},{4,7},{5,6},{6,5},{7,4},{8,11},{9,10},{10,... | collective-permute-start | bytes 393224 | tf_op jit(solution)/shard_map/ppermute | solution.py:27
  58.3 11.0 %collective-permute-start.5 = (bf16[128,2048]{1,0:T(8,128)(2,1)S(1)}, bf16[128,2048]{1,0:T(8,128)(2,1)}, u32[]{:S(2)}, u32[]{:S(2)}) collective-permute-start(bf16[128,2048]{1,0:T(8,128)(2,1)S(1)} %broadcast_add_fusion.1), channel_id=1, source_target_pairs={{0,16},{16,0},{1,17},{17,1},{2,18},{18,2},{3,19},{19,3},{4,20},{20... | collective-permute-start | bytes 1572872 | tf_op jit(solution)/shard_map/ppermute | solution.py:27
  59.9 6.9 %copy-start.4 = (bf16[512,1024]{1,0:T(8,128)(2,1)S(1)}, bf16[512,1024]{1,0:T(8,128)(2,1)}, u32[]{:S(2)}) copy-start(bf16[512,1024]{1,0:T(8,128)(2,1)} %copy-done.3) | copy-start | bytes 3145732
  67.8 6.3 %copy-start.6 = (bf16[128,2048]{1,0:T(8,128)(2,1)S(1)}, bf16[128,2048]{1,0:T(8,128)(2,1)}, u32[]{:S(2)}) copy-start(bf16[128,2048]{1,0:T(8,128)(2,1)} %param.11) | copy-start | bytes 1572868
  67.8 173.8 %all-gather.2.cloned.1.call-start = ((), (), s32[]{:S(2)}) async-start(), calls=%async_computation.4 | async-start | bytes 1310720 | tf_op jit(solution)/shard_map/all_gather | solution.py:204
  68.1 6.1 %copy-start.2 = (f32[128,2048]{1,0:T(8,128)S(1)}, f32[128,2048]{1,0:T(8,128)}, u32[]{:S(2)}) copy-start(f32[128,2048]{1,0:T(8,128)} %fusion.2) | copy-start | bytes 3145732
  74.4 9.9 %collective-permute-start.6 = (bf16[128,2048]{1,0:T(8,128)(2,1)S(1)}, bf16[128,2048]{1,0:T(8,128)(2,1)S(1)}, u32[]{:S(2)}, u32[]{:S(2)}) collective-permute-start(bf16[128,2048]{1,0:T(8,128)(2,1)S(1)} %subtract_convert_fusion), channel_id=1, source_target_pairs={{0,8},{4,12},{8,0},{12,4},{1,9},{5,13},{9,1},{13,5},{2,10},{6,14},... | collective-permute-start | bytes 1572872 | tf_op jit(solution)/shard_map/ppermute | solution.py:27
  85.4 10.3 %collective-permute-start.7 = (bf16[256,2048]{1,0:T(8,128)(2,1)}, bf16[256,2048]{1,0:T(8,128)(2,1)}, u32[]{:S(2)}, u32[]{:S(2)}) collective-permute-start(bf16[256,2048]{1,0:T(8,128)(2,1)} %pad_maximum_fusion.1), channel_id=1, source_target_pairs={{0,4},{4,0},{8,12},{12,8},{1,5},{5,1},{9,13},{13,9},{2,6},{6,2},{1... | collective-permute-start | bytes 3145736 | tf_op jit(solution)/shard_map/ppermute | solution.py:27
  95.7 12.4 %slice-start = ((s8[16777216]{0:T(1024)(128)(4,1)}), s8[4194304]{0:T(1024)(128)(4,1)S(1)}, s32[]{:S(2)}) async-start(s8[16777216]{0:T(1024)(128)(4,1)} %bitcast.255), calls=%async_computation.5 | async-start | bytes 8388608
  95.7 12.4 %slice-start.1 = ((s8[16777216]{0:T(1024)(128)(4,1)}), s8[4194304]{0:T(1024)(128)(4,1)S(1)}, s32[]{:S(2)}) async-start(s8[16777216]{0:T(1024)(128)(4,1)} %bitcast.255), calls=%async_computation.6 | async-start | bytes 8388608
  100.7 7.4 %slice-start.2 = ((s8[16777216]{0:T(1024)(128)(4,1)}), s8[4194304]{0:T(1024)(128)(4,1)S(1)}, s32[]{:S(2)}) async-start(s8[16777216]{0:T(1024)(128)(4,1)} %bitcast.255), calls=%async_computation.7 | async-start | bytes 8388608
  100.8 7.3 %slice-start.3 = ((s8[16777216]{0:T(1024)(128)(4,1)}), s8[4194304]{0:T(1024)(128)(4,1)S(1)}, s32[]{:S(2)}) async-start(s8[16777216]{0:T(1024)(128)(4,1)} %bitcast.255), calls=%async_computation.8 | async-start | bytes 8388608
  100.8 14.7 %collective-permute-start.8 = (bf16[256,1024]{1,0:T(8,128)(2,1)S(1)}, bf16[256,1024]{1,0:T(8,128)(2,1)S(1)}, u32[]{:S(2)}, u32[]{:S(2)}) collective-permute-start(bf16[256,1024]{1,0:T(8,128)(2,1)S(1)} %add_bitcast_fusion.2), channel_id=1, source_target_pairs={{0,16},{16,0},{1,17},{17,1},{2,18},{18,2},{3,19},{19,3},{4,20},{20... | collective-permute-start | bytes 1572872 | tf_op jit(solution)/shard_map/ppermute | solution.py:27
  108.0 14.9 %collective-permute-start.14 = (bf16[256,1024]{1,0:T(8,128)(2,1)S(1)}, bf16[256,1024]{1,0:T(8,128)(2,1)S(1)}, u32[]{:S(2)}, u32[]{:S(2)}) collective-permute-start(bf16[256,1024]{1,0:T(8,128)(2,1)S(1)} %dynamic-slice_bitcast_fusion), channel_id=1, source_target_pairs={{0,1},{1,0},{2,3},{3,2},{4,5},{5,4},{6,7},{7,6},{8,9},{9,8},{10,11... | collective-permute-start | bytes 1572872 | tf_op jit(solution)/shard_map/ppermute | solution.py:27
  115.7 12.0 %collective-permute-start.9 = (bf16[128,1024]{1,0:T(8,128)(2,1)S(1)}, bf16[128,1024]{1,0:T(8,128)(2,1)S(1)}, u32[]{:S(2)}, u32[]{:S(2)}) collective-permute-start(bf16[128,1024]{1,0:T(8,128)(2,1)S(1)} %dynamic-slice_bitcast_fusion.8), channel_id=1, source_target_pairs={{0,1},{1,0},{2,3},{3,2},{4,5},{5,4},{6,7},{7,6},{8,9},{9,8},{10,11... | collective-permute-start | bytes 786440 | tf_op jit(solution)/shard_map/ppermute | solution.py:27
  124.2 9.2 %collective-permute-start.15 = (bf16[128,1024]{1,0:T(8,128)(2,1)S(1)}, bf16[128,1024]{1,0:T(8,128)(2,1)S(1)}, u32[]{:S(2)}, u32[]{:S(2)}) collective-permute-start(bf16[128,1024]{1,0:T(8,128)(2,1)S(1)} %dynamic-slice_bitcast_fusion.7), channel_id=1, source_target_pairs={{0,16},{16,0},{1,17},{17,1},{2,18},{18,2},{3,19},{19,3},{4,20},{20... | collective-permute-start | bytes 786440 | tf_op jit(solution)/shard_map/ppermute | solution.py:27
  125.0 23.3 %collective-permute-start.20 = (bf16[256,1024]{1,0:T(8,128)(2,1)S(1)}, bf16[256,1024]{1,0:T(8,128)(2,1)S(1)}, u32[]{:S(2)}, u32[]{:S(2)}) collective-permute-start(bf16[256,1024]{1,0:T(8,128)(2,1)S(1)} %add_bitcast_fusion.1), channel_id=1, source_target_pairs={{0,16},{16,0},{1,17},{17,1},{2,18},{18,2},{3,19},{19,3},{4,20},{20... | collective-permute-start | bytes 1572872 | tf_op jit(solution)/shard_map/ppermute | solution.py:27
  127.6 21.7 %collective-permute-start.26 = (bf16[256,1024]{1,0:T(8,128)(2,1)S(1)}, bf16[256,1024]{1,0:T(8,128)(2,1)S(1)}, u32[]{:S(2)}, u32[]{:S(2)}) collective-permute-start(bf16[256,1024]{1,0:T(8,128)(2,1)S(1)} %add_bitcast_fusion), channel_id=1, source_target_pairs={{0,1},{1,0},{2,3},{3,2},{4,5},{5,4},{6,7},{7,6},{8,9},{9,8},{10,11... | collective-permute-start | bytes 1572872 | tf_op jit(solution)/shard_map/ppermute | solution.py:27
  127.7 14.2 %collective-permute-start.10 = (bf16[64,1024]{1,0:T(8,128)(2,1)S(1)}, bf16[64,1024]{1,0:T(8,128)(2,1)S(1)}, u32[]{:S(2)}, u32[]{:S(2)}) collective-permute-start(bf16[64,1024]{1,0:T(8,128)(2,1)S(1)} %dynamic-slice_bitcast_fusion.12), channel_id=1, source_target_pairs={{0,2},{1,3},{2,0},{3,1},{4,6},{5,7},{6,4},{7,5},{8,10},{9,11},{10,... | collective-permute-start | bytes 393224 | tf_op jit(solution)/shard_map/ppermute | solution.py:27
  133.5 12.2 %collective-permute-start.16 = (bf16[64,1024]{1,0:T(8,128)(2,1)S(1)}, bf16[64,1024]{1,0:T(8,128)(2,1)S(1)}, u32[]{:S(2)}, u32[]{:S(2)}) collective-permute-start(bf16[64,1024]{1,0:T(8,128)(2,1)S(1)} %dynamic-slice_bitcast_fusion.11), channel_id=1, source_target_pairs={{0,2},{1,3},{2,0},{3,1},{4,6},{5,7},{6,4},{7,5},{8,10},{9,11},{10,... | collective-permute-start | bytes 393224 | tf_op jit(solution)/shard_map/ppermute | solution.py:27
  142.2 8.5 %collective-permute-start.11 = (bf16[64,1024]{1,0:T(8,128)(2,1)S(1)}, bf16[64,1024]{1,0:T(8,128)(2,1)S(1)}, u32[]{:S(2)}, u32[]{:S(2)}) collective-permute-start(bf16[64,1024]{1,0:T(8,128)(2,1)S(1)} %get-tuple-element.5), channel_id=1, source_target_pairs={{0,2},{1,3},{2,0},{3,1},{4,6},{5,7},{6,4},{7,5},{8,10},{9,11},{10,... | collective-permute-start | bytes 393224 | tf_op jit(solution)/shard_map/ppermute | solution.py:27
  145.8 7.7 %collective-permute-start.17 = (bf16[64,1024]{1,0:T(8,128)(2,1)S(1)}, bf16[64,1024]{1,0:T(8,128)(2,1)S(1)}, u32[]{:S(2)}, u32[]{:S(2)}) collective-permute-start(bf16[64,1024]{1,0:T(8,128)(2,1)S(1)} %get-tuple-element.7), channel_id=1, source_target_pairs={{0,2},{1,3},{2,0},{3,1},{4,6},{5,7},{6,4},{7,5},{8,10},{9,11},{10,... | collective-permute-start | bytes 393224 | tf_op jit(solution)/shard_map/ppermute | solution.py:27
  148.5 11.9 %collective-permute-start.21 = (bf16[128,1024]{1,0:T(8,128)(2,1)S(1)}, bf16[128,1024]{1,0:T(8,128)(2,1)S(1)}, u32[]{:S(2)}, u32[]{:S(2)}) collective-permute-start(bf16[128,1024]{1,0:T(8,128)(2,1)S(1)} %dynamic-slice_bitcast_fusion.6), channel_id=1, source_target_pairs={{0,1},{1,0},{2,3},{3,2},{4,5},{5,4},{6,7},{7,6},{8,9},{9,8},{10,11... | collective-permute-start | bytes 786440 | tf_op jit(solution)/shard_map/ppermute | solution.py:27
  149.5 12.3 %collective-permute-start.27 = (bf16[128,1024]{1,0:T(8,128)(2,1)S(1)}, bf16[128,1024]{1,0:T(8,128)(2,1)S(1)}, u32[]{:S(2)}, u32[]{:S(2)}) collective-permute-start(bf16[128,1024]{1,0:T(8,128)(2,1)S(1)} %dynamic-slice_bitcast_fusion.5), channel_id=1, source_target_pairs={{0,16},{16,0},{1,17},{17,1},{2,18},{18,2},{3,19},{19,3},{4,20},{20... | collective-permute-start | bytes 786440 | tf_op jit(solution)/shard_map/ppermute | solution.py:27
  150.8 17.6 %collective-permute-start.12 = (bf16[128,1024]{1,0:T(8,128)(2,1)S(1)}, bf16[128,1024]{1,0:T(8,128)(2,1)S(1)}, u32[]{:S(2)}, u32[]{:S(2)}) collective-permute-start(bf16[128,1024]{1,0:T(8,128)(2,1)S(1)} %bitcast.291), channel_id=1, source_target_pairs={{0,1},{1,0},{2,3},{3,2},{4,5},{5,4},{6,7},{7,6},{8,9},{9,8},{10,11... | collective-permute-start | bytes 786440 | tf_op jit(solution)/shard_map/ppermute | solution.py:27
  153.6 14.9 %collective-permute-start.18 = (bf16[128,1024]{1,0:T(8,128)(2,1)S(1)}, bf16[128,1024]{1,0:T(8,128)(2,1)S(1)}, u32[]{:S(2)}, u32[]{:S(2)}) collective-permute-start(bf16[128,1024]{1,0:T(8,128)(2,1)S(1)} %bitcast.293), channel_id=1, source_target_pairs={{0,16},{16,0},{1,17},{17,1},{2,18},{18,2},{3,19},{19,3},{4,20},{20... | collective-permute-start | bytes 786440 | tf_op jit(solution)/shard_map/ppermute | solution.py:27
  160.6 8.4 %collective-permute-start.22 = (bf16[64,1024]{1,0:T(8,128)(2,1)S(1)}, bf16[64,1024]{1,0:T(8,128)(2,1)S(1)}, u32[]{:S(2)}, u32[]{:S(2)}) collective-permute-start(bf16[64,1024]{1,0:T(8,128)(2,1)S(1)} %dynamic-slice_bitcast_fusion.10), channel_id=1, source_target_pairs={{0,2},{1,3},{2,0},{3,1},{4,6},{5,7},{6,4},{7,5},{8,10},{9,11},{10,... | collective-permute-start | bytes 393224 | tf_op jit(solution)/shard_map/ppermute | solution.py:27
  161.9 9.7 %collective-permute-start.28 = (bf16[64,1024]{1,0:T(8,128)(2,1)S(1)}, bf16[64,1024]{1,0:T(8,128)(2,1)S(1)}, u32[]{:S(2)}, u32[]{:S(2)}) collective-permute-start(bf16[64,1024]{1,0:T(8,128)(2,1)S(1)} %dynamic-slice_bitcast_fusion.9), channel_id=1, source_target_pairs={{0,2},{1,3},{2,0},{3,1},{4,6},{5,7},{6,4},{7,5},{8,10},{9,11},{10,... | collective-permute-start | bytes 393224 | tf_op jit(solution)/shard_map/ppermute | solution.py:27
  168.4 27.9 %collective-permute-start.13 = (bf16[256,1024]{1,0:T(8,128)(2,1)S(1)}, bf16[256,1024]{1,0:T(8,128)(2,1)S(1)}, u32[]{:S(2)}, u32[]{:S(2)}) collective-permute-start(bf16[256,1024]{1,0:T(8,128)(2,1)S(1)} %bitcast.271), channel_id=1, source_target_pairs={{0,16},{16,0},{1,17},{17,1},{2,18},{18,2},{3,19},{19,3},{4,20},{20... | collective-permute-start | bytes 1572872 | tf_op jit(solution)/shard_map/ppermute | solution.py:27
  168.5 27.8 %collective-permute-start.19 = (bf16[256,1024]{1,0:T(8,128)(2,1)S(1)}, bf16[256,1024]{1,0:T(8,128)(2,1)S(1)}, u32[]{:S(2)}, u32[]{:S(2)}) collective-permute-start(bf16[256,1024]{1,0:T(8,128)(2,1)S(1)} %bitcast.273), channel_id=1, source_target_pairs={{0,1},{1,0},{2,3},{3,2},{4,5},{5,4},{6,7},{7,6},{8,9},{9,8},{10,11... | collective-permute-start | bytes 1572872 | tf_op jit(solution)/shard_map/ppermute | solution.py:27
  169.0 13.1 %collective-permute-start.23 = (bf16[64,1024]{1,0:T(8,128)(2,1)S(1)}, bf16[64,1024]{1,0:T(8,128)(2,1)S(1)}, u32[]{:S(2)}, u32[]{:S(2)}) collective-permute-start(bf16[64,1024]{1,0:T(8,128)(2,1)S(1)} %get-tuple-element.9), channel_id=1, source_target_pairs={{0,2},{1,3},{2,0},{3,1},{4,6},{5,7},{6,4},{7,5},{8,10},{9,11},{10,... | collective-permute-start | bytes 393224 | tf_op jit(solution)/shard_map/ppermute | solution.py:27
  171.7 14.0 %collective-permute-start.29 = (bf16[64,1024]{1,0:T(8,128)(2,1)S(1)}, bf16[64,1024]{1,0:T(8,128)(2,1)S(1)}, u32[]{:S(2)}, u32[]{:S(2)}) collective-permute-start(bf16[64,1024]{1,0:T(8,128)(2,1)S(1)} %get-tuple-element.3), channel_id=1, source_target_pairs={{0,2},{1,3},{2,0},{3,1},{4,6},{5,7},{6,4},{7,5},{8,10},{9,11},{10,... | collective-permute-start | bytes 393224 | tf_op jit(solution)/shard_map/ppermute | solution.py:27
  182.2 10.2 %collective-permute-start.24 = (bf16[128,1024]{1,0:T(8,128)(2,1)S(1)}, bf16[128,1024]{1,0:T(8,128)(2,1)S(1)}, u32[]{:S(2)}, u32[]{:S(2)}) collective-permute-start(bf16[128,1024]{1,0:T(8,128)(2,1)S(1)} %bitcast.295), channel_id=1, source_target_pairs={{0,1},{1,0},{2,3},{3,2},{4,5},{5,4},{6,7},{7,6},{8,9},{9,8},{10,11... | collective-permute-start | bytes 786440 | tf_op jit(solution)/shard_map/ppermute | solution.py:27
  185.7 9.3 %collective-permute-start.30 = (bf16[128,1024]{1,0:T(8,128)(2,1)S(1)}, bf16[128,1024]{1,0:T(8,128)(2,1)S(1)}, u32[]{:S(2)}, u32[]{:S(2)}) collective-permute-start(bf16[128,1024]{1,0:T(8,128)(2,1)S(1)} %bitcast.289), channel_id=1, source_target_pairs={{0,16},{16,0},{1,17},{17,1},{2,18},{18,2},{3,19},{19,3},{4,20},{20... | collective-permute-start | bytes 786440 | tf_op jit(solution)/shard_map/ppermute | solution.py:27
  192.4 9.7 %collective-permute-start.25 = (bf16[256,1024]{1,0:T(8,128)(2,1)S(1)}, bf16[256,1024]{1,0:T(8,128)(2,1)S(1)}, u32[]{:S(2)}, u32[]{:S(2)}) collective-permute-start(bf16[256,1024]{1,0:T(8,128)(2,1)S(1)} %bitcast.275), channel_id=1, source_target_pairs={{0,16},{16,0},{1,17},{17,1},{2,18},{18,2},{3,19},{19,3},{4,20},{20... | collective-permute-start | bytes 1572872 | tf_op jit(solution)/shard_map/ppermute | solution.py:27
  195.0 9.7 %collective-permute-start.31 = (bf16[256,1024]{1,0:T(8,128)(2,1)S(1)}, bf16[256,1024]{1,0:T(8,128)(2,1)S(1)}, u32[]{:S(2)}, u32[]{:S(2)}) collective-permute-start(bf16[256,1024]{1,0:T(8,128)(2,1)S(1)} %bitcast.277), channel_id=1, source_target_pairs={{0,1},{1,0},{2,3},{3,2},{4,5},{5,4},{6,7},{7,6},{8,9},{9,8},{10,11... | collective-permute-start | bytes 1572872 | tf_op jit(solution)/shard_map/ppermute | solution.py:27
  206.1 4.0 %collective-permute-start.32 = (bf16[256,2048]{1,0:T(8,128)(2,1)S(1)}, bf16[256,2048]{1,0:T(8,128)(2,1)S(1)}, u32[]{:S(2)}, u32[]{:S(2)}) collective-permute-start(bf16[256,2048]{1,0:T(8,128)(2,1)S(1)} %fusion.52), channel_id=1, source_target_pairs={{0,4},{4,0},{8,12},{12,8},{1,5},{5,1},{9,13},{13,9},{2,6},{6,2},{1... | collective-permute-start | bytes 3145736 | tf_op jit(solution)/shard_map/ppermute | solution.py:27
  210.0 4.7 %copy-start.7 = (bf16[4,32,1024]{2,1,0:T(8,128)(2,1)S(1)}, bf16[4,32,1024]{2,1,0:T(8,128)(2,1)}, u32[]{:S(2)}) copy-start(bf16[4,32,1024]{2,1,0:T(8,128)(2,1)} %reduce-scatter.2.cloned.1.call-done) | copy-start | bytes 786436
  212.3 14.6 %collective-permute-start.33 = (bf16[128,2048]{1,0:T(8,128)(2,1)}, bf16[128,2048]{1,0:T(8,128)(2,1)}, u32[]{:S(2)}, u32[]{:S(2)}) collective-permute-start(bf16[128,2048]{1,0:T(8,128)(2,1)} %slice.254), channel_id=1, source_target_pairs={{0,8},{4,12},{8,0},{12,4},{1,9},{5,13},{9,1},{13,5},{2,10},{6,14},... | collective-permute-start | bytes 1572872 | tf_op jit(solution)/shard_map/ppermute | solution.py:27
  228.1 4.0 %copy-start.5 = (bf16[128,2048]{1,0:T(8,128)(2,1)}, bf16[128,2048]{1,0:T(8,128)(2,1)S(1)}, u32[]{:S(2)}) copy-start(bf16[128,2048]{1,0:T(8,128)(2,1)S(1)} %add_convert_fusion.1) | copy-start | bytes 1572868
  231.9 13.7 %collective-permute-start.34 = (bf16[4,128,512]{2,1,0:T(8,128)(2,1)}, bf16[4,128,512]{2,1,0:T(8,128)(2,1)S(1)}, u32[]{:S(2)}, u32[]{:S(2)}) collective-permute-start(bf16[4,128,512]{2,1,0:T(8,128)(2,1)} %convolution_convert_fusion.2), channel_id=1, source_target_pairs={{0,16},{16,0},{1,17},{17,1},{2,18},{18,2},{3,19},{19,3},{4,20},{20... | collective-permute-start | bytes 1572872 | tf_op jit(solution)/shard_map/ppermute | solution.py:27
  246.6 20.3 %all-to-all-start.1 = ((bf16[16,32,512]{2,1,0:T(8,128)(2,1)}), bf16[16,32,512]{2,1,0:T(8,128)(2,1)}, u32[]{:S(2)}, u32[]{:S(2)}) async-start(bf16[16,32,512]{2,1,0:T(8,128)(2,1)} %bitcast.105), calls=%async_computation.2 | async-start | bytes 1048576 | tf_op jit(solution)/shard_map/all_to_all | solution.py:216
  266.9 7.6 %copy-start.1 = (bf16[512,1024]{1,0:T(8,128)(2,1)S(1)}, bf16[512,1024]{1,0:T(8,128)(2,1)}, u32[]{:S(2)}) copy-start(bf16[512,1024]{1,0:T(8,128)(2,1)} %param.9) | copy-start | bytes 3145732
  268.1 6.3 %collective-permute-start.35 = (bf16[4,32,512]{2,1,0:T(8,128)(2,1)S(1)}, bf16[4,32,512]{2,1,0:T(8,128)(2,1)S(1)}, u32[]{:S(2)}, u32[]{:S(2)}) collective-permute-start(bf16[4,32,512]{2,1,0:T(8,128)(2,1)S(1)} %pad_maximum_fusion.9), channel_id=1, source_target_pairs={{0,1},{1,0},{2,3},{3,2},{4,5},{5,4},{6,7},{7,6},{8,9},{9,8},{10,11... | collective-permute-start | bytes 393224 | tf_op jit(solution)/shard_map/ppermute | solution.py:27
  269.9 13.0 %collective-permute-start.38 = (bf16[4,32,512]{2,1,0:T(8,128)(2,1)S(1)}, bf16[4,32,512]{2,1,0:T(8,128)(2,1)S(1)}, u32[]{:S(2)}, u32[]{:S(2)}) collective-permute-start(bf16[4,32,512]{2,1,0:T(8,128)(2,1)S(1)} %pad_maximum_fusion.9), channel_id=1, source_target_pairs={{0,2},{1,3},{2,0},{3,1},{4,6},{5,7},{6,4},{7,5},{8,10},{9,11},{10,... | collective-permute-start | bytes 393224 | tf_op jit(solution)/shard_map/ppermute | solution.py:27
  271.4 11.5 %collective-permute-start.39 = (bf16[4,32,512]{2,1,0:T(8,128)(2,1)S(1)}, bf16[4,32,512]{2,1,0:T(8,128)(2,1)S(1)}, u32[]{:S(2)}, u32[]{:S(2)}) collective-permute-start(bf16[4,32,512]{2,1,0:T(8,128)(2,1)S(1)} %pad_maximum_fusion.9), channel_id=1, source_target_pairs={{0,3},{1,2},{2,1},{3,0},{4,7},{5,6},{6,5},{7,4},{8,11},{9,10},{10,... | collective-permute-start | bytes 393224 | tf_op jit(solution)/shard_map/ppermute | solution.py:27
  274.9 8.6 %collective-permute-start.36 = (bf16[128,1024]{1,0:T(8,128)(2,1)S(1)}, bf16[128,1024]{1,0:T(8,128)(2,1)S(1)}, u32[]{:S(2)}, u32[]{:S(2)}) collective-permute-start(bf16[128,1024]{1,0:T(8,128)(2,1)S(1)} %slice.370), channel_id=1, source_target_pairs={{0,4},{4,0},{8,12},{12,8},{1,5},{5,1},{9,13},{13,9},{2,6},{6,2},{1... | collective-permute-start | bytes 786440 | tf_op jit(solution)/shard_map/ppermute | solution.py:27
  283.4 1.6 collective-permute-start.40
  283.6 6.4 %collective-permute-start.37 = (bf16[64,1024]{1,0:T(8,128)(2,1)S(1)}, bf16[64,1024]{1,0:T(8,128)(2,1)S(1)}, u32[]{:S(2)}, u32[]{:S(2)}) collective-permute-start(bf16[64,1024]{1,0:T(8,128)(2,1)S(1)} %slice.259), channel_id=1, source_target_pairs={{0,8},{4,12},{8,0},{12,4},{1,9},{5,13},{9,1},{13,5},{2,10},{6,14},... | collective-permute-start | bytes 393224 | tf_op jit(solution)/shard_map/ppermute | solution.py:27
  285.1 7.3 %collective-permute-start.41 = (bf16[64,1024]{1,0:T(8,128)(2,1)S(1)}, bf16[64,1024]{1,0:T(8,128)(2,1)S(1)}, u32[]{:S(2)}, u32[]{:S(2)}) collective-permute-start(bf16[64,1024]{1,0:T(8,128)(2,1)S(1)} %slice.265), channel_id=1, source_target_pairs={{0,8},{4,12},{8,0},{12,4},{1,9},{5,13},{9,1},{13,5},{2,10},{6,14},... | collective-permute-start | bytes 393224 | tf_op jit(solution)/shard_map/ppermute | solution.py:27
  292.4 0.7 copy-start.8
Sparse Core Ops, SparseCore 0:
  67.9 25.8 reduce-scatter.1
  215.6 26.0 all-gather.1

commit v6 on v5

--- a/solution.py
+++ b/solution.py
@@ -42,12 +42,15 @@
     return value
 
 
-def relative_scatter(value, axis, distance=1):
+def relative_scatter(low, high, axis):
+    first = got = swap(high.astype(jnp.bfloat16), axis, 1)
+    distance = 2
     while distance < lax.axis_size(axis):
-        half = value.shape[0] // 2
-        value = total([value[:half], swap(value[half:].astype(jnp.bfloat16), axis, distance)])
+        half = low.shape[0] // 2
+        low, high = total([low[:half], got[:half]]), total([low[half:], got[half:]])
+        got = swap(high, axis, distance)
         distance *= 2
-    return value
+    return total([low, got]), first
 
 
 def relative_places(axis):
@@ -196,10 +199,8 @@
     right = jnp.concatenate([right, swap(right, "wide", 1)], axis=0)
 
     (given, kept), late = root_solve(right, root_factor, leaf_mid)
-    given = swap(given.astype(jnp.bfloat16), "wide", 1)
-    leaf_mid = hold(leaf_mid, given)
-    kept = total([kept, given])
-    root_solution = relative_scatter(kept, "wide", 2)
+    root_solution, brought = relative_scatter(kept, given, "wide")
+    leaf_mid = hold(leaf_mid, brought)
 
     leaf_mid = lax.all_gather(leaf_mid, "narrow", axis=1, tiled=True).reshape(wide_count * rows, -1)
 
@@ -231,7 +232,8 @@
         back_leaf = times(middle.reshape(height, -1), leaf_factor) - times(
             returned.reshape(height, -1), leaf_coupling
         )
-        part = relative_scatter(back_leaf, "wide").reshape(group, small, -1)
+        part, _ = relative_scatter(back_leaf[: height // 2], back_leaf[height // 2 :], "wide")
+        part = part.reshape(group, small, -1)
         for k in near:
             leaf_solution = lax.dynamic_update_index_in_dim(leaf_solution, part[k - first], narrow_index ^ k, 0)
     leaf_solution = leaf_solution.reshape(rows, -1)

time: 306 us -> 306 us (level)
  transfers between devices with their start and end apart: 46 -> 46, of which waited for: 28 -> 28; matrix products, arithmetic and copies ran while one was open for 25% -> 26% of each run, Pallas kernels for 0% -> 0%
where the time goes in v6:
time: 306 us; the launch traced here: 301 us
  waiting for transfers between devices  129 us (42%)
  starting transfers between devices  58.3 us (19%)
  matrix products  53.9 us (18%)
  between operations  20.5 us (7%)
  other arithmetic  20.1 us (7%)
  local copies, waits for them, and re-layouts  19.1 us (6%)
    ppermute x42, waiting for transfers between devices, swap(): return lax.ppermute(value, axis, pairs)  97.6 us
    ppermute x42, starting transfers between devices, swap(): return lax.ppermute(value, axis, pairs)  47.5 us
    dot_general x14, matrix products, times(): return jnp.dot(left, right, preferred_element_type=jnp.float32)  24.5 us
    dot_general x6, matrix products, times_transposed(): lax.dot_general(left, right, (((1,), (1,)), ((), ())), preferred_element_...  22.8 us
    all_to_all x2, waiting for transfers between devices, body(): got = lax.all_to_all(sent, ('wide', 'narrow'), 0, 0, tiled=True)  15.7 us
    all_to_all x2, starting transfers between devices, body(): got = lax.all_to_all(sent, ('wide', 'narrow'), 0, 0, tiled=True)  10.6 us
    reduce_scatter x1, waiting for transfers between devices, body(): lax.psum_scatter(pivot_terms, 'narrow', scatter_dimension=1, tiled=True)  8.61 us
    eq x1, other arithmetic, body(): landing = (near_map[:, :, None] == columns).astype(jnp.bfloat16)  7.35 us
  transfers between devices with their start and end apart: 46, of which 28 were waited for; matrix products, arithmetic and copies ran while one was open for 26% of the time, Pallas kernels for 0%

profile of v6, /device:TPU:0, one launch (start us, length us, event | category | flops | bytes accessed | tf_op | source)
XLA Modules:
  0.0 300.6 jit_solution(13978132719360964353)
XLA Ops:
  7.2 3.0 %collective-permute-start = (bf16[128,1024]{1,0:T(8,128)(2,1)}, bf16[128,1024]{1,0:T(8,128)(2,1)S(1)}, u32[]{:S(2)}, u32[]{:S(2)}) collective-permute-start(bf16[128,1024]{1,0:T(8,128)(2,1)} %param.7), channel_id=1, source_target_pairs={{0,8},{4,12},{8,0},{12,4},{1,9},{5,13},{9,1},{13,5},{2,10},{6,14},... | collective-permute-start | bytes 786440 | tf_op jit(solution)/shard_map/ppermute | solution.py:27
  12.0 4.7 %collective-permute-done = bf16[128,1024]{1,0:T(8,128)(2,1)S(1)} collective-permute-done((bf16[128,1024]{1,0:T(8,128)(2,1)}, bf16[128,1024]{1,0:T(8,128)(2,1)S(1)}, u32[]{:S(2)}, u32[]{:S(2)}) %collective-permute-start) | collective-permute-done | bytes 262176 | tf_op jit(solution)/shard_map/ppermute | solution.py:27
  17.9 1.8 collective-permute-done.1
  19.7 2.3 convolution_convert_fusion.3
  23.1 6.2 %all-to-all-start = ((bf16[16,32,512]{2,1,0:T(8,128)(2,1)}), bf16[16,32,512]{2,1,0:T(8,128)(2,1)S(1)}, u32[]{:S(2)}, u32[]{:S(2)}) async-start(bf16[16,32,512]{2,1,0:T(8,128)(2,1)} %bitcast.5), calls=%async_computation | async-start | bytes 1048576 | tf_op jit(solution)/shard_map/all_to_all | solution.py:182
  29.3 7.3 %broadcast_compare_fusion = pred[2,2048,2048]{2,1,0:T(8,128)(4,1)} fusion(s32[2048]{0:T(1024)S(1)} %iota_add_fusion, s32[2,2048]{1,0:T(2,128)S(1)} %pad_add_fusion), kind=kLoop, calls=%fused_computation | loop fusion | flops 8388608 | bytes 8413184 | tf_op jit(solution)/shard_map/eq | solution.py:159
  38.5 2.5 convolution_convert_fusion
  42.1 2.9 all-to-all-done
  45.2 1.4 collective-permute-start.3
  46.6 2.9 collective-permute-start.4
  49.8 2.2 collective-permute-done.2
  52.0 6.2 %collective-permute-done.3 = bf16[32,2048]{1,0:T(8,128)(2,1)S(1)} collective-permute-done((bf16[32,2048]{1,0:T(8,128)(2,1)S(1)}, bf16[32,2048]{1,0:T(8,128)(2,1)S(1)}, u32[]{:S(2)}, u32[]{:S(2)}) %collective-permute-start.3) | collective-permute-done | bytes 131104 | tf_op jit(solution)/shard_map/ppermute | solution.py:27
  58.3 1.6 collective-permute-start.5
  59.9 5.8 %fusion.2 = f32[128,2048]{1,0:T(8,128)} fusion(bf16[128,2048]{1,0:T(8,128)(2,1)S(1)} %bitcast.269, pred[2,2048,2048]{2,1,0:T(8,128)(4,1)} %broadcast_compare_fusion), kind=kOutput, calls=%fused_computation.3 | convolution fusion | flops 1073741824 | bytes 5767168 | tf_op jit(solution)/shard_map/dot_general | solution.py:16
  69.2 4.9 %fusion = f32[128,2048]{1,0:T(8,128)S(1)} fusion(bf16[128,2048]{1,0:T(8,128)(2,1)} %collective-permute-done.5, pred[2,2048,2048]{2,1,0:T(8,128)(4,1)} %broadcast_compare_fusion), kind=kOutput, calls=%fused_computation.1 | convolution fusion | flops 1073741824 | bytes 5767168 | tf_op jit(solution)/shard_map/dot_general | solution.py:16
  74.3 1.5 collective-permute-start.6
  75.8 8.4 %collective-permute-done.6 = bf16[128,2048]{1,0:T(8,128)(2,1)S(1)} collective-permute-done((bf16[128,2048]{1,0:T(8,128)(2,1)S(1)}, bf16[128,2048]{1,0:T(8,128)(2,1)S(1)}, u32[]{:S(2)}, u32[]{:S(2)}) %collective-permute-start.6) | collective-permute-done | bytes 524320 | tf_op jit(solution)/shard_map/ppermute | solution.py:27
  85.3 8.6 %reduce-scatter.2.cloned.1.call-done = bf16[4,32,1024]{2,1,0:T(8,128)(2,1)} async-done(((bf16[4,128,1024]{2,1,0:T(8,128)(2,1)}), bf16[4,32,1024]{2,1,0:T(8,128)(2,1)}) %reduce-scatter.2.cloned.1.call-update) | async-done | bytes 262160 | tf_op jit(solution)/shard_map/reduce_scatter | solution.py:193
  95.7 5.0 %fusion.49 = bf16[512,1024]{1,0:T(8,128)(2,1)S(1)} fusion(bf16[4096,2048]{1,0:T(8,128)(2,1)} %param.10, bf16[256,2048]{1,0:T(8,128)(2,1)} %collective-permute-done.7, bf16[128,2048]{1,0:T(8,128)(2,1)S(1)} %collective-permute-done.6, bf16[128,2048]{1,0:T(8,128)(2,1)S(1)} %subtract_convert_fusion), kind=kOutput, calls=%fused_computation.38 | convolution fusion | flops 2154299392 | bytes 7340032 | tf_op jit(solution)/shard_map/dot_general | solution.py:10
  100.8 1.5 collective-permute-start.8
  102.4 5.6 %fusion.52 = bf16[512,1024]{1,0:T(8,128)(2,1)S(1)} fusion(bf16[4096,2048]{1,0:T(8,128)(2,1)} %param.10, bf16[256,2048]{1,0:T(8,128)(2,1)} %collective-permute-done.7, bf16[128,2048]{1,0:T(8,128)(2,1)S(1)} %collective-permute-done.6, bf16[128,2048]{1,0:T(8,128)(2,1)S(1)} %subtract_convert_fusion), kind=kOutput, calls=%fused_computation.39 | convolution fusion | flops 2154299392 | bytes 7340032 | tf_op jit(solution)/shard_map/dot_general | solution.py:10
  108.2 3.7 %fusion.55 = bf16[512,1024]{1,0:T(8,128)(2,1)S(1)} fusion(bf16[4096,2048]{1,0:T(8,128)(2,1)S(1)} %bitcast.256, bf16[256,2048]{1,0:T(8,128)(2,1)} %collective-permute-done.7, bf16[128,2048]{1,0:T(8,128)(2,1)S(1)} %collective-permute-done.6, bf16[128,2048]{1,0:T(8,128)(2,1)S(1)} %subtract_convert_fusion), kind=kOutput, calls=%fused_computation.40 | convolution fusion | flops 2154299392 | bytes 7340032 | tf_op jit(solution)/shard_map/dot_general | solution.py:10
  111.8 3.7 %fusion.58 = bf16[512,1024]{1,0:T(8,128)(2,1)S(1)} fusion(bf16[4096,2048]{1,0:T(8,128)(2,1)S(1)} %bitcast.256, bf16[256,2048]{1,0:T(8,128)(2,1)} %collective-permute-done.7, bf16[128,2048]{1,0:T(8,128)(2,1)S(1)} %collective-permute-done.6, bf16[128,2048]{1,0:T(8,128)(2,1)S(1)} %subtract_convert_fusion), kind=kOutput, calls=%fused_computation.41 | convolution fusion | flops 2154299392 | bytes 7340032 | tf_op jit(solution)/shard_map/dot_general | solution.py:10
  115.8 2.1 collective-permute-start.9
  117.8 5.1 %collective-permute-done.14 = bf16[256,1024]{1,0:T(8,128)(2,1)S(1)} collective-permute-done((bf16[256,1024]{1,0:T(8,128)(2,1)S(1)}, bf16[256,1024]{1,0:T(8,128)(2,1)S(1)}, u32[]{:S(2)}, u32[]{:S(2)}) %collective-permute-start.14) | collective-permute-done | bytes 524320 | tf_op jit(solution)/shard_map/ppermute | solution.py:27
  125.0 2.0 collective-permute-start.20
  127.8 1.7 collective-permute-start.10
  129.5 4.0 %collective-permute-done.15 = bf16[128,1024]{1,0:T(8,128)(2,1)S(1)} collective-permute-done((bf16[128,1024]{1,0:T(8,128)(2,1)S(1)}, bf16[128,1024]{1,0:T(8,128)(2,1)S(1)}, u32[]{:S(2)}, u32[]{:S(2)}) %collective-permute-start.15) | collective-permute-done | bytes 262176 | tf_op jit(solution)/shard_map/ppermute | solution.py:27
  134.6 7.4 %collective-permute-done.10 = bf16[64,1024]{1,0:T(8,128)(2,1)S(1)} collective-permute-done((bf16[64,1024]{1,0:T(8,128)(2,1)S(1)}, bf16[64,1024]{1,0:T(8,128)(2,1)S(1)}, u32[]{:S(2)}, u32[]{:S(2)}) %collective-permute-start.10) | collective-permute-done | bytes 131104 | tf_op jit(solution)/shard_map/ppermute | solution.py:27
  142.3 3.5 %collective-permute-start.11 = (bf16[64,1024]{1,0:T(8,128)(2,1)S(1)}, bf16[64,1024]{1,0:T(8,128)(2,1)S(1)}, u32[]{:S(2)}, u32[]{:S(2)}) collective-permute-start(bf16[64,1024]{1,0:T(8,128)(2,1)S(1)} %get-tuple-element.5), channel_id=1, source_target_pairs={{0,2},{1,3},{2,0},{3,1},{4,6},{5,7},{6,4},{7,5},{8,10},{9,11},{10,... | collective-permute-start | bytes 393224 | tf_op jit(solution)/shard_map/ppermute | solution.py:27
  145.9 2.5 collective-permute-start.17
  151.0 2.4 collective-permute-start.12
  154.0 6.5 %collective-permute-done.21 = bf16[128,1024]{1,0:T(8,128)(2,1)S(1)} collective-permute-done((bf16[128,1024]{1,0:T(8,128)(2,1)S(1)}, bf16[128,1024]{1,0:T(8,128)(2,1)S(1)}, u32[]{:S(2)}, u32[]{:S(2)}) %collective-permute-start.21) | collective-permute-done | bytes 262176 | tf_op jit(solution)/shard_map/ppermute | solution.py:27
  161.9 1.8 collective-permute-start.28
  163.8 5.4 %collective-permute-done.12 = bf16[128,1024]{1,0:T(8,128)(2,1)S(1)} collective-permute-done((bf16[128,1024]{1,0:T(8,128)(2,1)S(1)}, bf16[128,1024]{1,0:T(8,128)(2,1)S(1)}, u32[]{:S(2)}, u32[]{:S(2)}) %collective-permute-start.12) | collective-permute-done | bytes 262176 | tf_op jit(solution)/shard_map/ppermute | solution.py:27
  169.8 1.3 collective-permute-start.23
  171.4 1.6 collective-permute-start.29
  173.0 9.2 %collective-permute-done.23 = bf16[64,1024]{1,0:T(8,128)(2,1)S(1)} collective-permute-done((bf16[64,1024]{1,0:T(8,128)(2,1)S(1)}, bf16[64,1024]{1,0:T(8,128)(2,1)S(1)}, u32[]{:S(2)}, u32[]{:S(2)}) %collective-permute-start.23) | collective-permute-done | bytes 131104 | tf_op jit(solution)/shard_map/ppermute | solution.py:27
  182.2 3.5 %collective-permute-start.24 = (bf16[128,1024]{1,0:T(8,128)(2,1)S(1)}, bf16[128,1024]{1,0:T(8,128)(2,1)S(1)}, u32[]{:S(2)}, u32[]{:S(2)}) collective-permute-start(bf16[128,1024]{1,0:T(8,128)(2,1)S(1)} %bitcast.295), channel_id=1, source_target_pairs={{0,1},{1,0},{2,3},{3,2},{4,5},{5,4},{6,7},{7,6},{8,9},{9,8},{10,11... | collective-permute-start | bytes 786440 | tf_op jit(solution)/shard_map/ppermute | solution.py:27
  186.2 6.7 %collective-permute-done.24 = bf16[128,1024]{1,0:T(8,128)(2,1)S(1)} collective-permute-done((bf16[128,1024]{1,0:T(8,128)(2,1)S(1)}, bf16[128,1024]{1,0:T(8,128)(2,1)S(1)}, u32[]{:S(2)}, u32[]{:S(2)}) %collective-permute-start.24) | collective-permute-done | bytes 262176 | tf_op jit(solution)/shard_map/ppermute | solution.py:27
  193.0 2.2 collective-permute-done.30
  195.8 1.3 fusion.16
  198.6 3.5 %collective-permute-done.25 = bf16[256,1024]{1,0:T(8,128)(2,1)S(1)} collective-permute-done((bf16[256,1024]{1,0:T(8,128)(2,1)S(1)}, bf16[256,1024]{1,0:T(8,128)(2,1)S(1)}, u32[]{:S(2)}, u32[]{:S(2)}) %collective-permute-start.25) | collective-permute-done | bytes 524320 | tf_op jit(solution)/shard_map/ppermute | solution.py:27
  204.7 1.3 fusion.43
  206.1 1.3 fusion.46
  207.5 1.4 fusion.40
  208.9 1.3 fusion.37
  210.3 1.3 copy-done.1
  212.5 1.5 collective-permute-start.33
  215.9 6.2 %fusion.92 = (pred[1,2048,2048]{2,1,0:T(32,128)(4,1)S(1)}, pred[1,2048,2048]{2,1,0:T(32,128)(4,1)S(1)}) fusion(pred[2,2048,2048]{2,1,0:T(8,128)(4,1)} %broadcast_compare_fusion), kind=kLoop, calls=%fused_computation.191 | loop fusion | bytes 16777216 | tf_op jit(solution)/shard_map/slice | solution.py:196
  222.1 5.1 %collective-permute-done.33 = bf16[128,2048]{1,0:T(8,128)(2,1)} collective-permute-done((bf16[128,2048]{1,0:T(8,128)(2,1)}, bf16[128,2048]{1,0:T(8,128)(2,1)}, u32[]{:S(2)}, u32[]{:S(2)}) %collective-permute-start.33) | collective-permute-done | bytes 524320 | tf_op jit(solution)/shard_map/ppermute | solution.py:27
  228.4 3.7 %convolution_convert_fusion.2 = bf16[4,128,512]{2,1,0:T(8,128)(2,1)} fusion(pred[4,512,2048]{2,1,0:T(32,128)(4,1)S(1)} %bitcast.258, bf16[128,2048]{1,0:T(8,128)(2,1)S(1)} %add_convert_fusion.1), kind=kOutput, calls=%fused_computation.45 | convolution fusion | flops 1074003968 | bytes 5242880 | tf_op jit(solution)/shard_map/dot_general | solution.py:211
  232.2 2.9 convolution_convert_fusion.1
  235.1 6.8 %all-gather.2.cloned.1.call-done = bf16[4,128,1024]{2,1,0:T(8,128)(2,1)} async-done(((bf16[4,32,1024]{2,1,0:T(8,128)(2,1)}), bf16[4,128,1024]{2,1,0:T(8,128)(2,1)}) %all-gather.2.cloned.1.call-update) | async-done | bytes 1048592 | tf_op jit(solution)/shard_map/all_gather | solution.py:205
  243.7 2.2 collective-permute-done.34
  246.9 4.4 %all-to-all-start.1 = ((bf16[16,32,512]{2,1,0:T(8,128)(2,1)}), bf16[16,32,512]{2,1,0:T(8,128)(2,1)}, u32[]{:S(2)}, u32[]{:S(2)}) async-start(bf16[16,32,512]{2,1,0:T(8,128)(2,1)} %bitcast.105), calls=%async_computation.2 | async-start | bytes 1048576 | tf_op jit(solution)/shard_map/all_to_all | solution.py:217
  251.3 1.3 dynamic-slice_bitcast_fusion.2
  254.2 12.8 %all-to-all-done.1 = bf16[16,32,512]{2,1,0:T(8,128)(2,1)} async-done(((bf16[16,32,512]{2,1,0:T(8,128)(2,1)}), bf16[16,32,512]{2,1,0:T(8,128)(2,1)}, u32[]{:S(2)}, u32[]{:S(2)}) %all-to-all-start.1) | async-done | bytes 524320 | tf_op jit(solution)/shard_map/all_to_all | solution.py:217
  268.4 1.7 fusion.93
  270.2 1.5 collective-permute-start.38
  271.6 2.9 collective-permute-start.39
  275.2 7.9 %collective-permute-done.38 = bf16[4,32,512]{2,1,0:T(8,128)(2,1)S(1)} collective-permute-done((bf16[4,32,512]{2,1,0:T(8,128)(2,1)S(1)}, bf16[4,32,512]{2,1,0:T(8,128)(2,1)S(1)}, u32[]{:S(2)}, u32[]{:S(2)}) %collective-permute-start.38) | collective-permute-done | bytes 131104 | tf_op jit(solution)/shard_map/ppermute | solution.py:27
  286.5 3.6 %collective-permute-done.37 = bf16[64,1024]{1,0:T(8,128)(2,1)S(1)} collective-permute-done((bf16[64,1024]{1,0:T(8,128)(2,1)S(1)}, bf16[64,1024]{1,0:T(8,128)(2,1)S(1)}, u32[]{:S(2)}, u32[]{:S(2)}) %collective-permute-start.37) | collective-permute-done | bytes 131104 | tf_op jit(solution)/shard_map/ppermute | solution.py:27
  290.2 2.3 collective-permute-done.41
  (199 shorter events, 39.2 us)
Async XLA Ops:
  7.2 31.3 %copy-start = (bf16[1024,1024]{1,0:T(8,128)(2,1)S(1)}, bf16[1024,1024]{1,0:T(8,128)(2,1)}, u32[]{:S(2)}) copy-start(bf16[1024,1024]{1,0:T(8,128)(2,1)} %param.8) | copy-start | bytes 6291460
  7.2 9.6 %collective-permute-start = (bf16[128,1024]{1,0:T(8,128)(2,1)}, bf16[128,1024]{1,0:T(8,128)(2,1)S(1)}, u32[]{:S(2)}, u32[]{:S(2)}) collective-permute-start(bf16[128,1024]{1,0:T(8,128)(2,1)} %param.7), channel_id=1, source_target_pairs={{0,8},{4,12},{8,0},{12,4},{1,9},{5,13},{9,1},{13,5},{2,10},{6,14},... | collective-permute-start | bytes 786440 | tf_op jit(solution)/shard_map/ppermute | solution.py:27
  17.7 2.0 collective-permute-start.1
  19.7 3.4 %copy-start.11 = (bf16[512,1024]{1,0:T(8,128)(2,1)}, bf16[512,1024]{1,0:T(8,128)(2,1)S(1)}, u32[]{:S(2)}) copy-start(bf16[512,1024]{1,0:T(8,128)(2,1)S(1)} %constant_dynamic-update-slice_fusion.1) | copy-start | bytes 3145732
  23.1 21.8 %all-to-all-start = ((bf16[16,32,512]{2,1,0:T(8,128)(2,1)}), bf16[16,32,512]{2,1,0:T(8,128)(2,1)S(1)}, u32[]{:S(2)}, u32[]{:S(2)}) async-start(bf16[16,32,512]{2,1,0:T(8,128)(2,1)} %bitcast.5), calls=%async_computation | async-start | bytes 1048576 | tf_op jit(solution)/shard_map/all_to_all | solution.py:182
  29.3 64.6 %reduce-scatter.2.cloned.1.call-start = ((), (), s32[]{:S(2)}) async-start(), calls=%async_computation.3 | async-start | bytes 1310720 | tf_op jit(solution)/shard_map/reduce_scatter | solution.py:193
  41.0 1.1 copy-start.5
  45.1 6.9 %collective-permute-start.2 = (bf16[32,2048]{1,0:T(8,128)(2,1)S(1)}, bf16[32,2048]{1,0:T(8,128)(2,1)S(1)}, u32[]{:S(2)}, u32[]{:S(2)}) collective-permute-start(bf16[32,2048]{1,0:T(8,128)(2,1)S(1)} %bitcast.310), channel_id=1, source_target_pairs={{0,1},{1,0},{2,3},{3,2},{4,5},{5,4},{6,7},{7,6},{8,9},{9,8},{10,11... | collective-permute-start | bytes 393224 | tf_op jit(solution)/shard_map/ppermute | solution.py:27
  45.2 13.0 %collective-permute-start.3 = (bf16[32,2048]{1,0:T(8,128)(2,1)S(1)}, bf16[32,2048]{1,0:T(8,128)(2,1)S(1)}, u32[]{:S(2)}, u32[]{:S(2)}) collective-permute-start(bf16[32,2048]{1,0:T(8,128)(2,1)S(1)} %bitcast.311), channel_id=1, source_target_pairs={{0,2},{1,3},{2,0},{3,1},{4,6},{5,7},{6,4},{7,5},{8,10},{9,11},{10,... | collective-permute-start | bytes 393224 | tf_op jit(solution)/shard_map/ppermute | solution.py:27
  46.6 11.6 %collective-permute-start.4 = (bf16[32,2048]{1,0:T(8,128)(2,1)S(1)}, bf16[32,2048]{1,0:T(8,128)(2,1)S(1)}, u32[]{:S(2)}, u32[]{:S(2)}) collective-permute-start(bf16[32,2048]{1,0:T(8,128)(2,1)S(1)} %bitcast.312), channel_id=1, source_target_pairs={{0,3},{1,2},{2,1},{3,0},{4,7},{5,6},{6,5},{7,4},{8,11},{9,10},{10,... | collective-permute-start | bytes 393224 | tf_op jit(solution)/shard_map/ppermute | solution.py:27
  58.3 10.9 %collective-permute-start.5 = (bf16[128,2048]{1,0:T(8,128)(2,1)S(1)}, bf16[128,2048]{1,0:T(8,128)(2,1)}, u32[]{:S(2)}, u32[]{:S(2)}) collective-permute-start(bf16[128,2048]{1,0:T(8,128)(2,1)S(1)} %broadcast_add_fusion.1), channel_id=1, source_target_pairs={{0,16},{16,0},{1,17},{17,1},{2,18},{18,2},{3,19},{19,3},{4,20},{20... | collective-permute-start | bytes 1572872 | tf_op jit(solution)/shard_map/ppermute | solution.py:27
  59.9 6.9 %copy-start.6 = (bf16[512,1024]{1,0:T(8,128)(2,1)S(1)}, bf16[512,1024]{1,0:T(8,128)(2,1)}, u32[]{:S(2)}) copy-start(bf16[512,1024]{1,0:T(8,128)(2,1)} %copy-done.5) | copy-start | bytes 3145732
  67.9 6.3 %copy-start.8 = (bf16[128,2048]{1,0:T(8,128)(2,1)S(1)}, bf16[128,2048]{1,0:T(8,128)(2,1)}, u32[]{:S(2)}) copy-start(bf16[128,2048]{1,0:T(8,128)(2,1)} %param.11) | copy-start | bytes 1572868
  67.9 174.0 %all-gather.2.cloned.1.call-start = ((), (), s32[]{:S(2)}) async-start(), calls=%async_computation.4 | async-start | bytes 1310720 | tf_op jit(solution)/shard_map/all_gather | solution.py:205
  68.1 6.0 %copy-start.4 = (f32[128,2048]{1,0:T(8,128)S(1)}, f32[128,2048]{1,0:T(8,128)}, u32[]{:S(2)}) copy-start(f32[128,2048]{1,0:T(8,128)} %fusion.2) | copy-start | bytes 3145732
  74.3 9.9 %collective-permute-start.6 = (bf16[128,2048]{1,0:T(8,128)(2,1)S(1)}, bf16[128,2048]{1,0:T(8,128)(2,1)S(1)}, u32[]{:S(2)}, u32[]{:S(2)}) collective-permute-start(bf16[128,2048]{1,0:T(8,128)(2,1)S(1)} %subtract_convert_fusion), channel_id=1, source_target_pairs={{0,8},{4,12},{8,0},{12,4},{1,9},{5,13},{9,1},{13,5},{2,10},{6,14},... | collective-permute-start | bytes 1572872 | tf_op jit(solution)/shard_map/ppermute | solution.py:27
  85.3 10.4 %collective-permute-start.7 = (bf16[256,2048]{1,0:T(8,128)(2,1)}, bf16[256,2048]{1,0:T(8,128)(2,1)}, u32[]{:S(2)}, u32[]{:S(2)}) collective-permute-start(bf16[256,2048]{1,0:T(8,128)(2,1)} %pad_maximum_fusion.1), channel_id=1, source_target_pairs={{0,4},{4,0},{8,12},{12,8},{1,5},{5,1},{9,13},{13,9},{2,6},{6,2},{1... | collective-permute-start | bytes 3145736 | tf_op jit(solution)/shard_map/ppermute | solution.py:27
  95.7 12.4 %slice-start = ((s8[16777216]{0:T(1024)(128)(4,1)}), s8[4194304]{0:T(1024)(128)(4,1)S(1)}, s32[]{:S(2)}) async-start(s8[16777216]{0:T(1024)(128)(4,1)} %bitcast.255), calls=%async_computation.5 | async-start | bytes 8388608
  95.7 12.4 %slice-start.1 = ((s8[16777216]{0:T(1024)(128)(4,1)}), s8[4194304]{0:T(1024)(128)(4,1)S(1)}, s32[]{:S(2)}) async-start(s8[16777216]{0:T(1024)(128)(4,1)} %bitcast.255), calls=%async_computation.6 | async-start | bytes 8388608
  100.8 7.4 %slice-start.2 = ((s8[16777216]{0:T(1024)(128)(4,1)}), s8[4194304]{0:T(1024)(128)(4,1)S(1)}, s32[]{:S(2)}) async-start(s8[16777216]{0:T(1024)(128)(4,1)} %bitcast.255), calls=%async_computation.7 | async-start | bytes 8388608
  100.8 7.3 %slice-start.3 = ((s8[16777216]{0:T(1024)(128)(4,1)}), s8[4194304]{0:T(1024)(128)(4,1)S(1)}, s32[]{:S(2)}) async-start(s8[16777216]{0:T(1024)(128)(4,1)} %bitcast.255), calls=%async_computation.8 | async-start | bytes 8388608
  100.8 14.7 %collective-permute-start.8 = (bf16[256,1024]{1,0:T(8,128)(2,1)S(1)}, bf16[256,1024]{1,0:T(8,128)(2,1)S(1)}, u32[]{:S(2)}, u32[]{:S(2)}) collective-permute-start(bf16[256,1024]{1,0:T(8,128)(2,1)S(1)} %add_bitcast_fusion.2), channel_id=1, source_target_pairs={{0,16},{16,0},{1,17},{17,1},{2,18},{18,2},{3,19},{19,3},{4,20},{20... | collective-permute-start | bytes 1572872 | tf_op jit(solution)/shard_map/ppermute | solution.py:27
  108.0 14.9 %collective-permute-start.14 = (bf16[256,1024]{1,0:T(8,128)(2,1)S(1)}, bf16[256,1024]{1,0:T(8,128)(2,1)S(1)}, u32[]{:S(2)}, u32[]{:S(2)}) collective-permute-start(bf16[256,1024]{1,0:T(8,128)(2,1)S(1)} %dynamic-slice_bitcast_fusion), channel_id=1, source_target_pairs={{0,1},{1,0},{2,3},{3,2},{4,5},{5,4},{6,7},{7,6},{8,9},{9,8},{10,11... | collective-permute-start | bytes 1572872 | tf_op jit(solution)/shard_map/ppermute | solution.py:27
  115.8 12.0 %collective-permute-start.9 = (bf16[128,1024]{1,0:T(8,128)(2,1)S(1)}, bf16[128,1024]{1,0:T(8,128)(2,1)S(1)}, u32[]{:S(2)}, u32[]{:S(2)}) collective-permute-start(bf16[128,1024]{1,0:T(8,128)(2,1)S(1)} %dynamic-slice_bitcast_fusion.8), channel_id=1, source_target_pairs={{0,1},{1,0},{2,3},{3,2},{4,5},{5,4},{6,7},{7,6},{8,9},{9,8},{10,11... | collective-permute-start | bytes 786440 | tf_op jit(solution)/shard_map/ppermute | solution.py:27
  124.2 9.2 %collective-permute-start.15 = (bf16[128,1024]{1,0:T(8,128)(2,1)S(1)}, bf16[128,1024]{1,0:T(8,128)(2,1)S(1)}, u32[]{:S(2)}, u32[]{:S(2)}) collective-permute-start(bf16[128,1024]{1,0:T(8,128)(2,1)S(1)} %dynamic-slice_bitcast_fusion.7), channel_id=1, source_target_pairs={{0,16},{16,0},{1,17},{17,1},{2,18},{18,2},{3,19},{19,3},{4,20},{20... | collective-permute-start | bytes 786440 | tf_op jit(solution)/shard_map/ppermute | solution.py:27
  125.0 23.3 %collective-permute-start.20 = (bf16[256,1024]{1,0:T(8,128)(2,1)S(1)}, bf16[256,1024]{1,0:T(8,128)(2,1)S(1)}, u32[]{:S(2)}, u32[]{:S(2)}) collective-permute-start(bf16[256,1024]{1,0:T(8,128)(2,1)S(1)} %add_bitcast_fusion.1), channel_id=1, source_target_pairs={{0,16},{16,0},{1,17},{17,1},{2,18},{18,2},{3,19},{19,3},{4,20},{20... | collective-permute-start | bytes 1572872 | tf_op jit(solution)/shard_map/ppermute | solution.py:27
  127.6 21.6 %collective-permute-start.26 = (bf16[256,1024]{1,0:T(8,128)(2,1)S(1)}, bf16[256,1024]{1,0:T(8,128)(2,1)S(1)}, u32[]{:S(2)}, u32[]{:S(2)}) collective-permute-start(bf16[256,1024]{1,0:T(8,128)(2,1)S(1)} %add_bitcast_fusion), channel_id=1, source_target_pairs={{0,1},{1,0},{2,3},{3,2},{4,5},{5,4},{6,7},{7,6},{8,9},{9,8},{10,11... | collective-permute-start | bytes 1572872 | tf_op jit(solution)/shard_map/ppermute | solution.py:27
  127.8 14.2 %collective-permute-start.10 = (bf16[64,1024]{1,0:T(8,128)(2,1)S(1)}, bf16[64,1024]{1,0:T(8,128)(2,1)S(1)}, u32[]{:S(2)}, u32[]{:S(2)}) collective-permute-start(bf16[64,1024]{1,0:T(8,128)(2,1)S(1)} %dynamic-slice_bitcast_fusion.12), channel_id=1, source_target_pairs={{0,2},{1,3},{2,0},{3,1},{4,6},{5,7},{6,4},{7,5},{8,10},{9,11},{10,... | collective-permute-start | bytes 393224 | tf_op jit(solution)/shard_map/ppermute | solution.py:27
  133.6 12.2 %collective-permute-start.16 = (bf16[64,1024]{1,0:T(8,128)(2,1)S(1)}, bf16[64,1024]{1,0:T(8,128)(2,1)S(1)}, u32[]{:S(2)}, u32[]{:S(2)}) collective-permute-start(bf16[64,1024]{1,0:T(8,128)(2,1)S(1)} %dynamic-slice_bitcast_fusion.11), channel_id=1, source_target_pairs={{0,2},{1,3},{2,0},{3,1},{4,6},{5,7},{6,4},{7,5},{8,10},{9,11},{10,... | collective-permute-start | bytes 393224 | tf_op jit(solution)/shard_map/ppermute | solution.py:27
  142.3 8.6 %collective-permute-start.11 = (bf16[64,1024]{1,0:T(8,128)(2,1)S(1)}, bf16[64,1024]{1,0:T(8,128)(2,1)S(1)}, u32[]{:S(2)}, u32[]{:S(2)}) collective-permute-start(bf16[64,1024]{1,0:T(8,128)(2,1)S(1)} %get-tuple-element.5), channel_id=1, source_target_pairs={{0,2},{1,3},{2,0},{3,1},{4,6},{5,7},{6,4},{7,5},{8,10},{9,11},{10,... | collective-permute-start | bytes 393224 | tf_op jit(solution)/shard_map/ppermute | solution.py:27
  145.9 7.9 %collective-permute-start.17 = (bf16[64,1024]{1,0:T(8,128)(2,1)S(1)}, bf16[64,1024]{1,0:T(8,128)(2,1)S(1)}, u32[]{:S(2)}, u32[]{:S(2)}) collective-permute-start(bf16[64,1024]{1,0:T(8,128)(2,1)S(1)} %get-tuple-element.7), channel_id=1, source_target_pairs={{0,2},{1,3},{2,0},{3,1},{4,6},{5,7},{6,4},{7,5},{8,10},{9,11},{10,... | collective-permute-start | bytes 393224 | tf_op jit(solution)/shard_map/ppermute | solution.py:27
  148.6 11.9 %collective-permute-start.21 = (bf16[128,1024]{1,0:T(8,128)(2,1)S(1)}, bf16[128,1024]{1,0:T(8,128)(2,1)S(1)}, u32[]{:S(2)}, u32[]{:S(2)}) collective-permute-start(bf16[128,1024]{1,0:T(8,128)(2,1)S(1)} %dynamic-slice_bitcast_fusion.6), channel_id=1, source_target_pairs={{0,1},{1,0},{2,3},{3,2},{4,5},{5,4},{6,7},{7,6},{8,9},{9,8},{10,11... | collective-permute-start | bytes 786440 | tf_op jit(solution)/shard_map/ppermute | solution.py:27
  149.5 12.3 %collective-permute-start.27 = (bf16[128,1024]{1,0:T(8,128)(2,1)S(1)}, bf16[128,1024]{1,0:T(8,128)(2,1)S(1)}, u32[]{:S(2)}, u32[]{:S(2)}) collective-permute-start(bf16[128,1024]{1,0:T(8,128)(2,1)S(1)} %dynamic-slice_bitcast_fusion.5), channel_id=1, source_target_pairs={{0,16},{16,0},{1,17},{17,1},{2,18},{18,2},{3,19},{19,3},{4,20},{20... | collective-permute-start | bytes 786440 | tf_op jit(solution)/shard_map/ppermute | solution.py:27
  151.0 18.2 %collective-permute-start.12 = (bf16[128,1024]{1,0:T(8,128)(2,1)S(1)}, bf16[128,1024]{1,0:T(8,128)(2,1)S(1)}, u32[]{:S(2)}, u32[]{:S(2)}) collective-permute-start(bf16[128,1024]{1,0:T(8,128)(2,1)S(1)} %bitcast.291), channel_id=1, source_target_pairs={{0,1},{1,0},{2,3},{3,2},{4,5},{5,4},{6,7},{7,6},{8,9},{9,8},{10,11... | collective-permute-start | bytes 786440 | tf_op jit(solution)/shard_map/ppermute | solution.py:27
  153.8 15.5 %collective-permute-start.18 = (bf16[128,1024]{1,0:T(8,128)(2,1)S(1)}, bf16[128,1024]{1,0:T(8,128)(2,1)S(1)}, u32[]{:S(2)}, u32[]{:S(2)}) collective-permute-start(bf16[128,1024]{1,0:T(8,128)(2,1)S(1)} %bitcast.293), channel_id=1, source_target_pairs={{0,16},{16,0},{1,17},{17,1},{2,18},{18,2},{3,19},{19,3},{4,20},{20... | collective-permute-start | bytes 786440 | tf_op jit(solution)/shard_map/ppermute | solution.py:27
  160.6 9.2 %collective-permute-start.22 = (bf16[64,1024]{1,0:T(8,128)(2,1)S(1)}, bf16[64,1024]{1,0:T(8,128)(2,1)S(1)}, u32[]{:S(2)}, u32[]{:S(2)}) collective-permute-start(bf16[64,1024]{1,0:T(8,128)(2,1)S(1)} %dynamic-slice_bitcast_fusion.10), channel_id=1, source_target_pairs={{0,2},{1,3},{2,0},{3,1},{4,6},{5,7},{6,4},{7,5},{8,10},{9,11},{10,... | collective-permute-start | bytes 393224 | tf_op jit(solution)/shard_map/ppermute | solution.py:27
  161.9 9.4 %collective-permute-start.28 = (bf16[64,1024]{1,0:T(8,128)(2,1)S(1)}, bf16[64,1024]{1,0:T(8,128)(2,1)S(1)}, u32[]{:S(2)}, u32[]{:S(2)}) collective-permute-start(bf16[64,1024]{1,0:T(8,128)(2,1)S(1)} %dynamic-slice_bitcast_fusion.9), channel_id=1, source_target_pairs={{0,2},{1,3},{2,0},{3,1},{4,6},{5,7},{6,4},{7,5},{8,10},{9,11},{10,... | collective-permute-start | bytes 393224 | tf_op jit(solution)/shard_map/ppermute | solution.py:27
  169.2 27.9 %collective-permute-start.13 = (bf16[256,1024]{1,0:T(8,128)(2,1)S(1)}, bf16[256,1024]{1,0:T(8,128)(2,1)S(1)}, u32[]{:S(2)}, u32[]{:S(2)}) collective-permute-start(bf16[256,1024]{1,0:T(8,128)(2,1)S(1)} %bitcast.271), channel_id=1, source_target_pairs={{0,16},{16,0},{1,17},{17,1},{2,18},{18,2},{3,19},{19,3},{4,20},{20... | collective-permute-start | bytes 1572872 | tf_op jit(solution)/shard_map/ppermute | solution.py:27
  169.3 26.2 %collective-permute-start.19 = (bf16[256,1024]{1,0:T(8,128)(2,1)S(1)}, bf16[256,1024]{1,0:T(8,128)(2,1)S(1)}, u32[]{:S(2)}, u32[]{:S(2)}) collective-permute-start(bf16[256,1024]{1,0:T(8,128)(2,1)S(1)} %bitcast.273), channel_id=1, source_target_pairs={{0,1},{1,0},{2,3},{3,2},{4,5},{5,4},{6,7},{7,6},{8,9},{9,8},{10,11... | collective-permute-start | bytes 1572872 | tf_op jit(solution)/shard_map/ppermute | solution.py:27
  169.8 12.4 %collective-permute-start.23 = (bf16[64,1024]{1,0:T(8,128)(2,1)S(1)}, bf16[64,1024]{1,0:T(8,128)(2,1)S(1)}, u32[]{:S(2)}, u32[]{:S(2)}) collective-permute-start(bf16[64,1024]{1,0:T(8,128)(2,1)S(1)} %get-tuple-element.9), channel_id=1, source_target_pairs={{0,2},{1,3},{2,0},{3,1},{4,6},{5,7},{6,4},{7,5},{8,10},{9,11},{10,... | collective-permute-start | bytes 393224 | tf_op jit(solution)/shard_map/ppermute | solution.py:27
  171.4 14.4 %collective-permute-start.29 = (bf16[64,1024]{1,0:T(8,128)(2,1)S(1)}, bf16[64,1024]{1,0:T(8,128)(2,1)S(1)}, u32[]{:S(2)}, u32[]{:S(2)}) collective-permute-start(bf16[64,1024]{1,0:T(8,128)(2,1)S(1)} %get-tuple-element.3), channel_id=1, source_target_pairs={{0,2},{1,3},{2,0},{3,1},{4,6},{5,7},{6,4},{7,5},{8,10},{9,11},{10,... | collective-permute-start | bytes 393224 | tf_op jit(solution)/shard_map/ppermute | solution.py:27
  182.2 10.6 %collective-permute-start.24 = (bf16[128,1024]{1,0:T(8,128)(2,1)S(1)}, bf16[128,1024]{1,0:T(8,128)(2,1)S(1)}, u32[]{:S(2)}, u32[]{:S(2)}) collective-permute-start(bf16[128,1024]{1,0:T(8,128)(2,1)S(1)} %bitcast.295), channel_id=1, source_target_pairs={{0,1},{1,0},{2,3},{3,2},{4,5},{5,4},{6,7},{7,6},{8,9},{9,8},{10,11... | collective-permute-start | bytes 786440 | tf_op jit(solution)/shard_map/ppermute | solution.py:27
  185.8 9.3 %collective-permute-start.30 = (bf16[128,1024]{1,0:T(8,128)(2,1)S(1)}, bf16[128,1024]{1,0:T(8,128)(2,1)S(1)}, u32[]{:S(2)}, u32[]{:S(2)}) collective-permute-start(bf16[128,1024]{1,0:T(8,128)(2,1)S(1)} %bitcast.289), channel_id=1, source_target_pairs={{0,16},{16,0},{1,17},{17,1},{2,18},{18,2},{3,19},{19,3},{4,20},{20... | collective-permute-start | bytes 786440 | tf_op jit(solution)/shard_map/ppermute | solution.py:27
  192.9 9.2 %collective-permute-start.25 = (bf16[256,1024]{1,0:T(8,128)(2,1)S(1)}, bf16[256,1024]{1,0:T(8,128)(2,1)S(1)}, u32[]{:S(2)}, u32[]{:S(2)}) collective-permute-start(bf16[256,1024]{1,0:T(8,128)(2,1)S(1)} %bitcast.275), channel_id=1, source_target_pairs={{0,16},{16,0},{1,17},{17,1},{2,18},{18,2},{3,19},{19,3},{4,20},{20... | collective-permute-start | bytes 1572872 | tf_op jit(solution)/shard_map/ppermute | solution.py:27
  195.1 10.9 %collective-permute-start.31 = (bf16[256,1024]{1,0:T(8,128)(2,1)S(1)}, bf16[256,1024]{1,0:T(8,128)(2,1)S(1)}, u32[]{:S(2)}, u32[]{:S(2)}) collective-permute-start(bf16[256,1024]{1,0:T(8,128)(2,1)S(1)} %bitcast.277), channel_id=1, source_target_pairs={{0,1},{1,0},{2,3},{3,2},{4,5},{5,4},{6,7},{7,6},{8,9},{9,8},{10,11... | collective-permute-start | bytes 1572872 | tf_op jit(solution)/shard_map/ppermute | solution.py:27
  207.4 2.9 collective-permute-start.32
  208.9 6.2 %copy-start.9 = (bf16[4,32,1024]{2,1,0:T(8,128)(2,1)S(1)}, bf16[4,32,1024]{2,1,0:T(8,128)(2,1)}, u32[]{:S(2)}) copy-start(bf16[4,32,1024]{2,1,0:T(8,128)(2,1)} %reduce-scatter.2.cloned.1.call-done) | copy-start | bytes 786436
  210.3 1.3 copy-start.1
  212.5 14.6 %collective-permute-start.33 = (bf16[128,2048]{1,0:T(8,128)(2,1)}, bf16[128,2048]{1,0:T(8,128)(2,1)}, u32[]{:S(2)}, u32[]{:S(2)}) collective-permute-start(bf16[128,2048]{1,0:T(8,128)(2,1)} %fusion.61), channel_id=1, source_target_pairs={{0,8},{4,12},{8,0},{12,4},{1,9},{5,13},{9,1},{13,5},{2,10},{6,14},... | collective-permute-start | bytes 1572872 | tf_op jit(solution)/shard_map/ppermute | solution.py:27
  215.8 11.3 %copy-start.2 = (f32[256,2048]{1,0:T(8,128)S(1)}, f32[256,2048]{1,0:T(8,128)}, u32[]{:S(2)}) copy-start(f32[256,2048]{1,0:T(8,128)} %copy-done.1) | copy-start | bytes 6291460
  228.4 3.8 %copy-start.7 = (bf16[128,2048]{1,0:T(8,128)(2,1)}, bf16[128,2048]{1,0:T(8,128)(2,1)S(1)}, u32[]{:S(2)}) copy-start(bf16[128,2048]{1,0:T(8,128)(2,1)S(1)} %add_convert_fusion.1) | copy-start | bytes 1572868
  232.2 13.7 %collective-permute-start.34 = (bf16[4,128,512]{2,1,0:T(8,128)(2,1)}, bf16[4,128,512]{2,1,0:T(8,128)(2,1)S(1)}, u32[]{:S(2)}, u32[]{:S(2)}) collective-permute-start(bf16[4,128,512]{2,1,0:T(8,128)(2,1)} %convolution_convert_fusion.2), channel_id=1, source_target_pairs={{0,16},{16,0},{1,17},{17,1},{2,18},{18,2},{3,19},{19,3},{4,20},{20... | collective-permute-start | bytes 1572872 | tf_op jit(solution)/shard_map/ppermute | solution.py:27
  246.9 20.2 %all-to-all-start.1 = ((bf16[16,32,512]{2,1,0:T(8,128)(2,1)}), bf16[16,32,512]{2,1,0:T(8,128)(2,1)}, u32[]{:S(2)}, u32[]{:S(2)}) async-start(bf16[16,32,512]{2,1,0:T(8,128)(2,1)} %bitcast.105), calls=%async_computation.2 | async-start | bytes 1048576 | tf_op jit(solution)/shard_map/all_to_all | solution.py:217
  267.1 7.6 %copy-start.3 = (bf16[512,1024]{1,0:T(8,128)(2,1)S(1)}, bf16[512,1024]{1,0:T(8,128)(2,1)}, u32[]{:S(2)}) copy-start(bf16[512,1024]{1,0:T(8,128)(2,1)} %param.9) | copy-start | bytes 3145732
  268.3 6.3 %collective-permute-start.35 = (bf16[4,32,512]{2,1,0:T(8,128)(2,1)S(1)}, bf16[4,32,512]{2,1,0:T(8,128)(2,1)S(1)}, u32[]{:S(2)}, u32[]{:S(2)}) collective-permute-start(bf16[4,32,512]{2,1,0:T(8,128)(2,1)S(1)} %pad_maximum_fusion.9), channel_id=1, source_target_pairs={{0,1},{1,0},{2,3},{3,2},{4,5},{5,4},{6,7},{7,6},{8,9},{9,8},{10,11... | collective-permute-start | bytes 393224 | tf_op jit(solution)/shard_map/ppermute | solution.py:27
  270.2 13.0 %collective-permute-start.38 = (bf16[4,32,512]{2,1,0:T(8,128)(2,1)S(1)}, bf16[4,32,512]{2,1,0:T(8,128)(2,1)S(1)}, u32[]{:S(2)}, u32[]{:S(2)}) collective-permute-start(bf16[4,32,512]{2,1,0:T(8,128)(2,1)S(1)} %pad_maximum_fusion.9), channel_id=1, source_target_pairs={{0,2},{1,3},{2,0},{3,1},{4,6},{5,7},{6,4},{7,5},{8,10},{9,11},{10,... | collective-permute-start | bytes 393224 | tf_op jit(solution)/shard_map/ppermute | solution.py:27
  271.6 11.5 %collective-permute-start.39 = (bf16[4,32,512]{2,1,0:T(8,128)(2,1)S(1)}, bf16[4,32,512]{2,1,0:T(8,128)(2,1)S(1)}, u32[]{:S(2)}, u32[]{:S(2)}) collective-permute-start(bf16[4,32,512]{2,1,0:T(8,128)(2,1)S(1)} %pad_maximum_fusion.9), channel_id=1, source_target_pairs={{0,3},{1,2},{2,1},{3,0},{4,7},{5,6},{6,5},{7,4},{8,11},{9,10},{10,... | collective-permute-start | bytes 393224 | tf_op jit(solution)/shard_map/ppermute | solution.py:27
  275.1 8.6 %collective-permute-start.36 = (bf16[128,1024]{1,0:T(8,128)(2,1)S(1)}, bf16[128,1024]{1,0:T(8,128)(2,1)S(1)}, u32[]{:S(2)}, u32[]{:S(2)}) collective-permute-start(bf16[128,1024]{1,0:T(8,128)(2,1)S(1)} %slice.413), channel_id=1, source_target_pairs={{0,4},{4,0},{8,12},{12,8},{1,5},{5,1},{9,13},{13,9},{2,6},{6,2},{1... | collective-permute-start | bytes 786440 | tf_op jit(solution)/shard_map/ppermute | solution.py:27
  283.6 1.6 collective-permute-start.40
  283.8 6.4 %collective-permute-start.37 = (bf16[64,1024]{1,0:T(8,128)(2,1)S(1)}, bf16[64,1024]{1,0:T(8,128)(2,1)S(1)}, u32[]{:S(2)}, u32[]{:S(2)}) collective-permute-start(bf16[64,1024]{1,0:T(8,128)(2,1)S(1)} %fusion.76), channel_id=1, source_target_pairs={{0,8},{4,12},{8,0},{12,4},{1,9},{5,13},{9,1},{13,5},{2,10},{6,14},... | collective-permute-start | bytes 393224 | tf_op jit(solution)/shard_map/ppermute | solution.py:27
  285.3 7.3 %collective-permute-start.41 = (bf16[64,1024]{1,0:T(8,128)(2,1)S(1)}, bf16[64,1024]{1,0:T(8,128)(2,1)S(1)}, u32[]{:S(2)}, u32[]{:S(2)}) collective-permute-start(bf16[64,1024]{1,0:T(8,128)(2,1)S(1)} %fusion.74), channel_id=1, source_target_pairs={{0,8},{4,12},{8,0},{12,4},{1,9},{5,13},{9,1},{13,5},{2,10},{6,14},... | collective-permute-start | bytes 393224 | tf_op jit(solution)/shard_map/ppermute | solution.py:27
  292.6 0.7 copy-start.10
Sparse Core Ops, SparseCore 0:
  68.0 25.9 reduce-scatter.1
  216.0 25.8 all-gather.1
